TPU v7x, 256 devices: a whole 4x4x8 slice. The times are simulated.
256 devices in a mesh: smp: 8 (over x, core), ctx: 32 (over y, z).
Axes of the slice: x: 4, y: 4, z: 8, core: 2. Of those that a mesh axis runs over, the one named last changes fastest.
Arguments:
- query: bfloat16 [8, 4096, 4096], P('smp', 'ctx'), may hold values from -6 to 6
- d_out: bfloat16 [8, 4096, 4096], P('smp', 'ctx'), may hold values from -6 to 6
- branch_kv: bfloat16 [8, 4096, 1024], P('smp', 'ctx'), may hold values from -6 to 6
- prefix_kv: bfloat16 [1024, 1024], P('ctx', 'smp'), may hold values from -6 to 6
- parents: int32 [8, 32], P('smp'), may hold values from -1 to 30, as said below
- lengths: int32 [8, 32], P('smp'), may hold values from 33 to 128, as said below
Outputs:
- attn_out: bfloat16 [8, 4096, 4096], P('smp', 'ctx')
- d_query: bfloat16 [8, 4096, 4096], P('smp', 'ctx')
- d_branch_kv: bfloat16 [8, 4096, 1024], P('smp', 'ctx')
- d_prefix_kv: bfloat16 [1024, 1024], P('ctx', 'smp')
Inputs may be any that keep to these rules, and one draw needn't show every extreme that they name: parents[s, 0] = -1; for i > 0 parents[s, i] lies below i; every path from the prefix to a block has at most 8 blocks, the block included, and block 7 of every sample has exactly 8; parents[s, 31] = 30. lengths[s, 0] = 128 and lengths[s, 1] = 33.
All inputs are finite; a program needn't handle non-finite values.
Results may differ from a plain program's by a relative error of at most 0.03.
Values may be sent and summed in bfloat16 or wider, within the bound.
No kernel may reach another device: no remote copies, remote signals or barrier semaphores. Data moves between devices by JAX's collectives and lax.ppermute only.
A program may use at most 128 MiB of HBM per device.

v0:
```python
import jax
import jax.numpy as jnp
from jax import lax
from jax.sharding import PartitionSpec as P

HK = 4
HD = 128


def build_masks(parent_row, length_row, block_index, depth_slots, block_rows, prefix_rows):
    num_blocks = parent_row.shape[0]
    indices = jnp.arange(num_blocks, dtype=jnp.int32)
    parent_links = (parent_row[:, None] == indices[None, :]).astype(jnp.float32)
    reachable = jnp.eye(num_blocks, dtype=jnp.float32) + parent_links
    for _ in range(num_blocks.bit_length()):
        reachable = jnp.minimum(jnp.dot(reachable, reachable, precision=lax.Precision.HIGHEST), 1.0)
    pick_row = (indices == block_index).astype(jnp.float32)
    ancestry = jnp.dot(pick_row, reachable, precision=lax.Precision.HIGHEST)
    position = jnp.cumsum(ancestry) - 1.0
    slot_ids = jnp.arange(depth_slots, dtype=jnp.float32)
    selector = ancestry[None, :] * (position[None, :] == slot_ids[:, None]).astype(jnp.float32)
    block_float = indices.astype(jnp.float32)
    owner_block = jnp.dot(selector, block_float, precision=lax.Precision.HIGHEST)
    slot_used = jnp.sum(selector, axis=1) > 0.5
    own_slot = slot_used & (jnp.abs(owner_block - jnp.sum(pick_row * block_float)) < 0.5)
    lengths_float = length_row.astype(jnp.float32)
    slot_length = jnp.dot(selector, lengths_float, precision=lax.Precision.HIGHEST)
    own_length = jnp.sum(pick_row * lengths_float)
    place = jnp.arange(block_rows, dtype=jnp.float32)
    row_place = place[:, None, None]
    key_place = place[None, None, :]
    slot_allowed = (
        slot_used[None, :, None]
        & (key_place < slot_length[None, :, None])
        & (jnp.logical_not(own_slot)[None, :, None] | (key_place <= row_place))
    )
    key_allowed = jnp.concatenate(
        [
            jnp.ones((block_rows, prefix_rows), dtype=jnp.bool_),
            slot_allowed.reshape(block_rows, depth_slots * block_rows),
        ],
        axis=1,
    )
    row_valid = place < own_length
    return (selector, key_allowed, row_valid)


def attend(query_block, dout_block, key_values, key_allowed, row_valid, heads_kv, head_dim):
    row_count = query_block.shape[0]
    query_width = query_block.shape[1]
    group_size = query_width // (heads_kv * head_dim)
    key_count = key_values.shape[0]
    softmax_scale = head_dim ** (-0.5)
    grad_live = jnp.where(row_valid[:, None], dout_block, jnp.zeros_like(dout_block))
    query_heads = (
        query_block.reshape(row_count, heads_kv, group_size, head_dim)
        .transpose(1, 0, 2, 3)
        .reshape(heads_kv, row_count * group_size, head_dim)
    )
    grad_heads = (
        grad_live.reshape(row_count, heads_kv, group_size, head_dim)
        .transpose(1, 0, 2, 3)
        .reshape(heads_kv, row_count * group_size, head_dim)
    )
    key_heads = (
        key_values[:, : heads_kv * head_dim]
        .reshape(key_count, heads_kv, head_dim)
        .transpose(1, 0, 2)
    )
    value_heads = (
        key_values[:, heads_kv * head_dim :]
        .reshape(key_count, heads_kv, head_dim)
        .transpose(1, 0, 2)
    )
    mask_rows = jnp.repeat(key_allowed, group_size, axis=0)
    live_rows = jnp.repeat(row_valid, group_size)

    def one_head(inputs):
        query_head, grad_head, key_head, value_head = inputs
        scores = jnp.dot(query_head, key_head.T, preferred_element_type=jnp.float32) * softmax_scale
        scores = jnp.where(mask_rows, scores, -jnp.inf)
        row_max = jnp.max(scores, axis=1, keepdims=True)
        exponent = jnp.exp(scores - row_max)
        probability = exponent / jnp.sum(exponent, axis=1, keepdims=True)
        prob_round = probability.astype(jnp.bfloat16)
        attended = jnp.dot(prob_round, value_head, preferred_element_type=jnp.float32)
        attended_out = jnp.where(live_rows[:, None], attended, 0.0).astype(jnp.bfloat16)
        grad_probs = jnp.dot(grad_head, value_head.T, preferred_element_type=jnp.float32)
        row_delta = jnp.sum(
            grad_head.astype(jnp.float32) * attended_out.astype(jnp.float32), axis=1, keepdims=True
        )
        grad_scores = (probability * (grad_probs - row_delta)).astype(jnp.bfloat16)
        grad_query = (
            jnp.dot(grad_scores, key_head, preferred_element_type=jnp.float32) * softmax_scale
        ).astype(jnp.bfloat16)
        grad_keys = (
            jnp.dot(grad_scores.T, query_head, preferred_element_type=jnp.float32) * softmax_scale
        )
        grad_values = jnp.dot(prob_round.T, grad_head, preferred_element_type=jnp.float32)
        return (attended_out, grad_query, grad_keys, grad_values)

    attended_all, grad_query_all, grad_keys_all, grad_values_all = lax.map(
        one_head, (query_heads, grad_heads, key_heads, value_heads)
    )
    output = (
        attended_all.reshape(heads_kv, row_count, group_size, head_dim)
        .transpose(1, 0, 2, 3)
        .reshape(row_count, query_width)
    )
    grad_query_out = (
        grad_query_all.reshape(heads_kv, row_count, group_size, head_dim)
        .transpose(1, 0, 2, 3)
        .reshape(row_count, query_width)
    )
    grad_pairs = jnp.concatenate(
        [
            grad_keys_all.transpose(1, 0, 2).reshape(key_count, heads_kv * head_dim),
            grad_values_all.transpose(1, 0, 2).reshape(key_count, heads_kv * head_dim),
        ],
        axis=1,
    )
    return (output, grad_query_out, grad_pairs)


def per_device(query, d_out, branch_kv, prefix_kv, parents, lengths):
    num_blocks = parents.shape[1]
    depth_slots = max(4, num_blocks // 4)
    block_rows = query.shape[1]
    block_index = lax.axis_index("ctx")
    with_features = lax.all_gather(prefix_kv, "smp", axis=1, tiled=True)
    prefix_all = lax.all_gather(with_features, "ctx", axis=0, tiled=True)
    prefix_rows = prefix_all.shape[0]
    feature_count = prefix_all.shape[1]
    selector, key_allowed, row_valid = build_masks(
        parents[0], lengths[0], block_index, depth_slots, block_rows, prefix_rows
    )
    selector_low = selector.astype(jnp.bfloat16)
    own_blocks = branch_kv[0]
    all_blocks = lax.all_gather(own_blocks, "ctx", axis=0, tiled=True)
    picked = jnp.einsum(
        "kn,nbf->kbf",
        selector_low,
        all_blocks.reshape(num_blocks, block_rows, feature_count),
        preferred_element_type=jnp.float32,
    ).astype(jnp.bfloat16)
    key_values = jnp.concatenate(
        [prefix_all, picked.reshape(depth_slots * block_rows, feature_count)], axis=0
    )
    output, grad_query, grad_pairs = attend(
        query[0], d_out[0], key_values, key_allowed, row_valid, HK, HD
    )
    grad_prefix = grad_pairs[:prefix_rows]
    slot_grads = grad_pairs[prefix_rows:].reshape(depth_slots, block_rows, feature_count)
    spread = jnp.einsum("km,kbf->mbf", selector, slot_grads, precision=lax.Precision.HIGHEST)
    grad_branch = lax.psum_scatter(
        spread.reshape(block_rows * lax.axis_size("ctx"), feature_count),
        "ctx",
        scatter_dimension=0,
        tiled=True,
    )
    grad_rows = lax.psum_scatter(grad_prefix, "ctx", scatter_dimension=0, tiled=True)
    grad_prefix_out = lax.psum_scatter(grad_rows, "smp", scatter_dimension=1, tiled=True)
    return (
        output[None],
        grad_query[None],
        grad_branch.astype(jnp.bfloat16)[None],
        grad_prefix_out.astype(jnp.bfloat16),
    )


def solution(mesh):
    return jax.shard_map(
        per_device,
        mesh=mesh,
        in_specs=(
            P("smp", "ctx", None),
            P("smp", "ctx", None),
            P("smp", "ctx", None),
            P("ctx", "smp"),
            P("smp", None),
            P("smp", None),
        ),
        out_specs=(
            P("smp", "ctx", None),
            P("smp", "ctx", None),
            P("smp", "ctx", None),
            P("ctx", "smp"),
        ),
        check_vma=False,
    )
```

profile of v0, /device:TPU:1, one launch (start us, length us, event | category | flops | bytes accessed | tf_op | source)
XLA Modules:
  0.0 836.5 jit_solution(6554432926453540240)
XLA Ops:
  8.0 15.3 %all_gather.9 = bf16[32,1024]{1,0:T(8,128)(2,1)} all-gather(bf16[32,128]{1,0:T(8,128)(2,1)} %param.11), channel_id=1, replica_groups=mesh['smp'=8,'ctx'=32] {'smp'}, dimensions={1}, use_global_device_ids=true | all-gather | bytes 73728 | tf_op jit(solution)/shard_map/all_gather | solution.py:130
  25.3 1.5 copy.61
  26.8 1.2 copy.74
  30.0 1.5 copy.41
  33.3 79.1 %all-gather.6.cloned.1.call-done = bf16[1,4096,1024]{2,1,0:T(8,128)(2,1)} async-done(((bf16[1,128,1024]{2,1,0:T(8,128)(2,1)}), bf16[1,4096,1024]{2,1,0:T(8,128)(2,1)}) %all-gather.6.cloned.1.call-update) | async-done | bytes 8388624 | tf_op jit(solution)/shard_map/all_gather | solution.py:139
  112.4 12.3 %fusion.47 = bf16[8,128,1024]{2,0,1:T(8,128)(2,1)S(1)} fusion(bf16[32,128,1024]{2,1,0:T(8,128)(2,1)} %bitcast.210, f32[32]{0:T(128)S(1)} %bitcast.223, f32[32]{0:T(128)S(1)} %add_reduce_fusion), kind=kOutput, calls=%fused_computation.55 | convolution fusion | flops 68157952 | bytes 10486016 | tf_op jit(solution)/shard_map/kn,nbf->kbf/dot_general | solution.py:140
  124.7 1.2 copy.37
  125.9 60.7 %all-gather.4.cloned.1.call-done = bf16[1024,1024]{1,0:T(8,128)(2,1)} async-done(((bf16[32,1024]{1,0:T(8,128)(2,1)}), bf16[1024,1024]{1,0:T(8,128)(2,1)}) %all-gather.4.cloned.1.call-update) | async-done | bytes 2097168 | tf_op jit(solution)/shard_map/all_gather | solution.py:131
  186.5 3.4 pad_maximum_fusion
  190.0 3.1 copy.39
  193.0 4.0 copy.38
  197.0 123.9 %while.17 = (s32[]{:T(128)}, bf16[4,1024,128]{2,1,0:T(8,128)(2,1)}, bf16[4,1024,128]{2,1,0:T(8,128)(2,1)}, f32[4,2048,128]{2,1,0:T(8,128)}, f32[4,2048,128]{2,1,...) while((s32[]{:T(128)}, bf16[4,1024,128]{2,1,0:T(8,128)(2,1)}, ...), condition=%wide.region_8.9_spmd.clone, body=%wide.region_4.8_spmd.clone.sunk | while | flops 3256087552 | bytes 147363152 | solution.py:102
  198.3 3.4 fusion.129
  201.7 2.9 fusion.130
  204.6 3.8 fusion.131
  208.5 1.6 multiply_reduce_fusion.2
  210.0 1.6 copy-done
  212.6 4.9 multiply_convert_fusion.2
  217.4 1.0 copy-done.1
  218.4 3.3 fusion.134
  221.7 3.0 fusion.132
  224.7 3.3 fusion.133
  228.3 1.0 constant_dynamic-slice_fusion.4
  229.4 3.4 fusion.129
  232.8 2.9 fusion.130
  235.7 3.8 fusion.131
  239.5 1.6 multiply_reduce_fusion.2
  241.1 1.6 copy-done
  243.6 4.9 multiply_convert_fusion.2
  248.5 1.0 copy-done.1
  249.5 3.2 fusion.134
  252.7 3.0 fusion.132
  255.7 3.2 fusion.133
  260.3 3.4 fusion.129
  263.7 2.9 fusion.130
  266.6 3.8 fusion.131
  270.4 1.6 multiply_reduce_fusion.2
  272.0 1.6 copy-done
  274.5 4.9 multiply_convert_fusion.2
  279.4 1.0 copy-done.1
  280.4 3.2 fusion.134
  283.6 3.0 fusion.132
  286.6 3.2 fusion.133
  291.2 3.4 fusion.129
  294.5 2.9 fusion.130
  297.5 3.8 fusion.131
  301.3 1.6 multiply_reduce_fusion.2
  302.9 1.6 copy-done
  305.4 4.9 multiply_convert_fusion.2
  310.3 1.0 copy-done.1
  311.2 3.3 fusion.134
  314.5 3.0 fusion.132
  317.5 3.2 fusion.133
  320.9 2.9 bitcast_dynamic-update-slice_fusion.1
  325.0 4.0 fusion.90
  329.1 217.3 %reduce-scatter.6.cloned.1.call-done = f32[32,1024]{1,0:T(8,128)} async-done(((f32[1024,1024]{1,0:T(8,128)}), f32[32,1024]{1,0:T(8,128)}) %reduce-scatter.6.cloned.1.call-update) | async-done | bytes 131088 | tf_op jit(solution)/shard_map/reduce_scatter | solution.py:161
  546.5 16.6 %fusion.44 = f32[32,128,1024]{2,0,1:T(8,128)S(1)} fusion(f32[8,128,1024]{2,1,0:T(8,128)} %bitcast.205, f32[32]{0:T(128)S(1)} %bitcast.224, f32[32]{0:T(128)S(1)} %add_reduce_fusion), kind=kOutput, calls=%fused_computation.51 | convolution fusion | flops 402653696 | bytes 20971776 | tf_op jit(solution)/shard_map/km,kbf->mbf/dot_general | solution.py:154
  563.1 19.0 %copy.52 = f32[32,128,1024]{2,1,0:T(8,128)} copy(f32[32,128,1024]{2,0,1:T(8,128)S(1)} %fusion.44) | data formatting | bytes 33554432 | tf_op jit(solution)/shard_map/km,kbf->mbf/dot_general | solution.py:154
  582.1 1.2 copy-done.5
  584.1 1.3 copy.53
  585.6 1.3 broadcast_in_dim_reshape.8
  586.9 1.3 convert_element_type.57
  588.2 239.6 %reduce-scatter.4.cloned.1.call-done = f32[128,1024]{1,0:T(8,128)} async-done(((f32[4096,1024]{1,0:T(8,128)}), f32[128,1024]{1,0:T(8,128)}) %reduce-scatter.4.cloned.1.call-update) | async-done | bytes 524304 | tf_op jit(solution)/shard_map/reduce_scatter | solution.py:155
  827.8 1.8 convert_bitcast_fusion
  (83 shorter events, 16.5 us)
Async XLA Ops:
  7.2 20.8 %copy-start.3 = (bf16[1,128,4096]{2,1,0:T(8,128)(2,1)S(1)}, bf16[1,128,4096]{2,1,0:T(8,128)(2,1)}, u32[]{:S(2)}) copy-start(bf16[1,128,4096]{2,1,0:T(8,128)(2,1)} %param.9) | copy-start | bytes 3145732
  7.2 21.4 %copy-start.6 = (s32[1,32]{1,0:T(1,128)S(1)}, s32[1,32]{1,0:T(1,128)}, u32[]{:S(2)}) copy-start(s32[1,32]{1,0:T(1,128)} %param.13) | copy-start | bytes 388
  7.2 105.2 %all-gather.6.cloned.1.call-start = ((), (), s32[]{:S(2)}) async-start(), calls=%async_computation.7 | async-start | bytes 8650752 | tf_op jit(solution)/shard_map/all_gather | solution.py:139
  7.9 178.6 %all-gather.4.cloned.1.call-start = ((), (), s32[]{:S(2)}) async-start(), calls=%async_computation.3 | async-start | bytes 2162688 | tf_op jit(solution)/shard_map/all_gather | solution.py:131
  23.3 523.1 %reduce-scatter.6.cloned.1.call-start = ((), (), s32[]{:S(2)}) async-start(), calls=%async_computation.5 | async-start | bytes 4325376 | tf_op jit(solution)/shard_map/reduce_scatter | solution.py:161
  208.4 3.2 copy-start
  212.6 5.8 copy-start.1
  239.5 3.2 copy-start
  243.6 5.8 copy-start.1
  270.4 3.2 copy-start
  274.5 5.8 copy-start.1
  301.3 3.2 copy-start
  305.4 5.8 copy-start.1
  320.9 3.5 copy-start.2
  329.0 257.9 %reduce-scatter.8.cloned.1.call-start = ((), (), s32[]{:S(2)}) async-start(), calls=%async_computation.6 | async-start | bytes 147456 | tf_op jit(solution)/shard_map/reduce_scatter | solution.py:162
  546.4 281.4 %reduce-scatter.4.cloned.1.call-start = ((), (), s32[]{:S(2)}) async-start(), calls=%async_computation.4 | async-start | bytes 17301504 | tf_op jit(solution)/shard_map/reduce_scatter | solution.py:155
  582.1 1.2 copy-start.5
  582.1 3.3 copy-start.4
Sparse Core Ops, SparseCore 0:
  10.6 101.7 all-gather.5
  115.0 71.5 all-gather.3
  329.2 217.1 reduce-scatter.5
  548.9 33.9 reduce-scatter.7
  586.8 240.9 reduce-scatter.3
where the time goes:
time: 850 us; the launch traced here: 836 us
  waiting for transfers between devices  597 us (70%)
  matrix products  109 us (13%)
  local copies, waits for them, and re-layouts  64.4 us (8%)
  other arithmetic  35.4 us (4%)
  blocking collectives  15.3 us (2%)
  between operations  14.4 us (2%)
    reduce_scatter x1, waiting for transfers between devices, per_device(): lax.psum_scatter(spread.reshape(block_rows * lax.axis_size('ctx'), featur...  240 us
    reduce_scatter x1, waiting for transfers between devices, per_device(): lax.psum_scatter(grad_prefix, 'ctx', scatter_dimension=0, tiled=True)  217 us
    all_gather x1, waiting for transfers between devices, per_device(): all_blocks = lax.all_gather(own_blocks, 'ctx', axis=0, tiled=True)  79.1 us
    all_gather x1, waiting for transfers between devices, per_device(): prefix_all = lax.all_gather(with_features, 'ctx', axis=0, tiled=True)  60.7 us
    dot_general x4, matrix products, one_head(): jnp.dot(grad_head, value_head.T, preferred_element_type=jnp.float32)  19.4 us
    dot_general x1, local copies, waits for them, and re-layouts, per_device(): jnp.einsum('km,kbf->mbf', selector, slot_grads, precision=lax.Precision.H...  19 us
  transfers between devices with their start and end apart: 5, of which 4 were waited for; matrix products, arithmetic and copies ran while one was open for 8% of the time, Pallas kernels for 0%

commit v1 on v0

v1 whole, which is shorter than its diff:
```python
import functools

import jax
import jax.numpy as jnp
from jax import lax
from jax.experimental import pallas as pl
from jax.experimental.pallas import tpu as pltpu
from jax.sharding import Mesh, PartitionSpec as P

HK = 4
HD = 128
GROUP = 8
BLOCK = 128
NB = 32
DEPTH = 8
PREFIX = 1024
ROWS = GROUP * BLOCK
CHUNK = 256
SCALE = HD ** -0.5
SCALE_LOG2E = SCALE * 1.4426950408889634
MASKED = -1e30
F32 = jnp.float32
BF16 = jnp.bfloat16


def dot(a, b):
    return lax.dot_general(a, b, (((1,), (0,)), ((), ())), preferred_element_type=F32)


def dot_t(a, b):
    return lax.dot_general(a, b, (((1,), (1,)), ((), ())), preferred_element_type=F32)


def attend_kernel(
    parents, lengths, block_ids, place,
    q_ref, g_ref, bk_ref, bv_ref, pk_ref, pv_ref,
    o_ref, dq_ref, dbk_ref, dbv_ref, dpk_ref, dpv_ref,
    qt, gt, qlt, glt, pkt, pvt, sk, sv, skt, svt, scores, probs, acc, bias,
    abk, abv, apk, apv,
):
    step = pl.program_id(0)
    block = block_ids[step]
    live = lengths[block]

    @pl.when(step == 0)
    def _():
        pkt[...] = pk_ref[...].T
        pvt[...] = pv_ref[...].T
        abk[...] = jnp.zeros_like(abk)
        abv[...] = jnp.zeros_like(abv)
        apk[...] = jnp.zeros_like(apk)
        apv[...] = jnp.zeros_like(apv)

    row_live = lax.broadcasted_iota(jnp.int32, (HD, BLOCK), 1) < live
    for h in range(GROUP):
        cols = slice(h * BLOCK, (h + 1) * BLOCK)
        qt[:, cols] = q_ref[0, :, cols].T
        gt[:, cols] = jnp.where(row_live, g_ref[0, :, cols].astype(F32).T, 0.0).astype(BF16)

    slots, used = [], []
    current = block
    for k in range(DEPTH):
        in_use = current >= 0
        slot = jnp.where(in_use, current, block)
        slots.append(slot)
        used.append(in_use)
        current = jnp.where(in_use, parents[slot], -1)
    key_row = lax.broadcasted_iota(jnp.int32, (BLOCK, BLOCK), 0)
    query_row = lax.broadcasted_iota(jnp.int32, (BLOCK, BLOCK), 1)
    for k in range(DEPTH):
        rows = slice(k * BLOCK, (k + 1) * BLOCK)

        @pl.when(used[k & ~1])
        def _(k=k, rows=rows):
            at = place[slots[k]]
            key = bk_ref[at]
            value = bv_ref[at]
            sk[rows, :] = key
            sv[rows, :] = value
            skt[:, rows] = key.T
            svt[:, rows] = value.T
            seen = key_row < jnp.where(used[k], lengths[slots[k]], 0)
            if k == 0:
                seen = seen & (key_row <= query_row)
            bias[rows, :] = jnp.where(seen, 0.0, MASKED)

    pairs = DEPTH // 2
    top = jnp.full((8, ROWS), MASKED, F32)
    for c in range(PREFIX // CHUNK):
        keys = slice(c * CHUNK, (c + 1) * CHUNK)
        s = dot(pk_ref[keys, :], qt[...])
        scores[keys, :] = s
        top = jnp.maximum(top, jnp.max(s.reshape(CHUNK // 8, 8, ROWS), axis=0))
    acc[0:8, :] = top
    for j in range(pairs):
        @pl.when(used[2 * j])
        def _(j=j):
            rows = slice(j * CHUNK, (j + 1) * CHUNK)
            s = dot(sk[rows, :], qt[...])
            s = s + jnp.concatenate([bias[rows, :]] * GROUP, axis=1)
            scores[PREFIX + j * CHUNK:PREFIX + (j + 1) * CHUNK, :] = s
            acc[0:8, :] = jnp.maximum(acc[0:8, :], jnp.max(s.reshape(CHUNK // 8, 8, ROWS), axis=0))
    peak = jnp.max(acc[0:8, :], axis=0, keepdims=True) * SCALE_LOG2E

    total = jnp.zeros((8, ROWS), F32)
    out_t = jnp.zeros((HD, ROWS), F32)
    for c in range(PREFIX // CHUNK):
        keys = slice(c * CHUNK, (c + 1) * CHUNK)
        e = jnp.exp2(scores[keys, :] * SCALE_LOG2E - peak)
        total = total + jnp.sum(e.reshape(CHUNK // 8, 8, ROWS), axis=0)
        low = e.astype(BF16)
        probs[keys, :] = low
        out_t = out_t + dot(pvt[:, keys], low)
    acc[0:HD, :] = out_t
    acc[HD:HD + 8, :] = total
    for j in range(pairs):
        @pl.when(used[2 * j])
        def _(j=j):
            rows = slice(j * CHUNK, (j + 1) * CHUNK)
            keys = slice(PREFIX + j * CHUNK, PREFIX + (j + 1) * CHUNK)
            e = jnp.exp2(scores[keys, :] * SCALE_LOG2E - peak)
            acc[HD:HD + 8, :] += jnp.sum(e.reshape(CHUNK // 8, 8, ROWS), axis=0)
            low = e.astype(BF16)
            probs[keys, :] = low
            acc[0:HD, :] += dot(svt[:, rows], low)
    inverse = 1.0 / jnp.sum(acc[HD:HD + 8, :], axis=0, keepdims=True)

    out_t = acc[0:HD, :] * inverse
    grad_t = gt[...].astype(F32)
    delta = jnp.sum(grad_t * out_t.astype(BF16).astype(F32), axis=0, keepdims=True)
    glt[...] = (grad_t * inverse).astype(BF16)
    qlt[...] = (qt[...].astype(F32) * (inverse * SCALE)).astype(BF16)
    for h in range(GROUP):
        cols = slice(h * BLOCK, (h + 1) * BLOCK)
        o_ref[0, :, cols] = jnp.where(row_live, out_t[:, cols], 0.0).T.astype(BF16)

    dq_t = jnp.zeros((HD, ROWS), F32)
    for c in range(PREFIX // CHUNK):
        keys = slice(c * CHUNK, (c + 1) * CHUNK)
        low = probs[keys, :]
        ds = (low.astype(F32) * (dot(pv_ref[keys, :], gt[...]) - delta)).astype(BF16)
        apv[keys, :] += dot_t(low, glt[...])
        apk[keys, :] += dot_t(ds, qlt[...])
        dq_t = dq_t + dot(pkt[:, keys], ds)
    acc[0:HD, :] = dq_t
    for j in range(pairs):
        @pl.when(used[2 * j])
        def _(j=j):
            rows = slice(j * CHUNK, (j + 1) * CHUNK)
            keys = slice(PREFIX + j * CHUNK, PREFIX + (j + 1) * CHUNK)
            low = probs[keys, :]
            ds = (low.astype(F32) * (dot(sv[rows, :], gt[...]) - delta)).astype(BF16)
            dv = dot_t(low, glt[...])
            dk = dot_t(ds, qlt[...])
            for k in range(2):
                at = place[slots[2 * j + k]]
                abv[at] += dv[k * BLOCK:(k + 1) * BLOCK]
                abk[at] += dk[k * BLOCK:(k + 1) * BLOCK]
            acc[0:HD, :] += dot(skt[:, rows], ds)
    dq_t = acc[0:HD, :] * (inverse * SCALE)
    for h in range(GROUP):
        cols = slice(h * BLOCK, (h + 1) * BLOCK)
        dq_ref[0, :, cols] = dq_t[:, cols].T.astype(BF16)

    @pl.when(step == pl.num_programs(0) - 1)
    def _():
        dbk_ref[...] = abk[...].astype(BF16)
        dbv_ref[...] = abv[...].astype(BF16)
        dpk_ref[...] = apk[...].astype(BF16)
        dpv_ref[...] = apv[...].astype(BF16)


def attend(parents, lengths, block_ids, place, q, g, bk, bv, pk, pv):
    whole = lambda shape: pl.BlockSpec(shape, lambda i, *_: (0,) * len(shape))
    heads = pl.BlockSpec((1, BLOCK, ROWS), lambda i, *_: (i, 0, 0))
    blocks, prefix = (NB, BLOCK, HD), (PREFIX, HD)
    struct = jax.ShapeDtypeStruct
    wide = lambda rows, dtype: pltpu.VMEM((rows, ROWS), dtype)
    return pl.pallas_call(
        attend_kernel,
        grid_spec=pltpu.PrefetchScalarGridSpec(
            num_scalar_prefetch=4,
            grid=(q.shape[0],),
            in_specs=[heads, heads, whole(blocks), whole(blocks), whole(prefix), whole(prefix)],
            out_specs=[heads, heads, whole(blocks), whole(blocks), whole(prefix), whole(prefix)],
            scratch_shapes=[
                wide(HD, BF16), wide(HD, BF16), wide(HD, BF16), wide(HD, BF16),
                pltpu.VMEM((HD, PREFIX), BF16), pltpu.VMEM((HD, PREFIX), BF16),
                pltpu.VMEM((DEPTH * BLOCK, HD), BF16), pltpu.VMEM((DEPTH * BLOCK, HD), BF16),
                pltpu.VMEM((HD, DEPTH * BLOCK), BF16), pltpu.VMEM((HD, DEPTH * BLOCK), BF16),
                wide(PREFIX + DEPTH * BLOCK, F32), wide(PREFIX + DEPTH * BLOCK, BF16),
                wide(HD + 8, F32), pltpu.VMEM((DEPTH * BLOCK, BLOCK), F32),
                pltpu.VMEM(blocks, F32), pltpu.VMEM(blocks, F32),
                pltpu.VMEM(prefix, F32), pltpu.VMEM(prefix, F32),
            ],
        ),
        out_shape=[
            struct(q.shape, BF16), struct(q.shape, BF16),
            struct(blocks, BF16), struct(blocks, BF16), struct(prefix, BF16), struct(prefix, BF16),
        ],
        compiler_params=pltpu.CompilerParams(vmem_limit_bytes=56 * 1024 * 1024),
        name="attend",
    )(parents, lengths, block_ids, place, q, g, bk, bv, pk, pv)


def per_device(query, d_out, branch_kv, prefix_kv, parents, lengths):
    ny, nz = lax.axis_size("y"), lax.axis_size("z")
    smp = ("x", "core")
    z = lax.axis_index("z")
    exchange = functools.partial(lax.all_to_all, axis_name="y", split_axis=1, concat_axis=0, tiled=True)
    back = functools.partial(lax.all_to_all, axis_name="y", split_axis=0, concat_axis=1, tiled=True)
    half = HK * HD

    prefix_rows = prefix_kv.shape[0]
    with_features = lax.all_gather(prefix_kv, smp, axis=1, tiled=True)
    kv = jnp.concatenate([branch_kv[0], with_features], axis=0)
    k = exchange(kv[:, :half])
    v = exchange(kv[:, half:])
    k = lax.all_gather(k, "z", axis=0, tiled=True).reshape(nz * ny, BLOCK + prefix_rows, HD)
    v = lax.all_gather(v, "z", axis=0, tiled=True).reshape(nz * ny, BLOCK + prefix_rows, HD)
    q = exchange(query[0]).reshape(ny, BLOCK, ROWS)
    g = exchange(d_out[0]).reshape(ny, BLOCK, ROWS)

    block_ids = jnp.arange(ny, dtype=jnp.int32) * nz + z
    ids = jnp.arange(NB, dtype=jnp.int32)
    place = (ids % nz) * ny + ids // nz
    out, dq, dbk, dbv, dpk, dpv = attend(
        parents[0], lengths[0], block_ids, place, q, g,
        k[:, :BLOCK], v[:, :BLOCK],
        k[:, BLOCK:].reshape(PREFIX, HD), v[:, BLOCK:].reshape(PREFIX, HD),
    )

    out = back(out.reshape(ny * BLOCK, ROWS))
    dq = back(dq.reshape(ny * BLOCK, ROWS))
    joined = lambda b, p: jnp.concatenate([b, p.reshape(NB, prefix_rows, HD)], axis=1)
    scatter = functools.partial(lax.psum_scatter, axis_name="z", scatter_dimension=0, tiled=True)
    dk = scatter(joined(dbk, dpk)).reshape(ny * (BLOCK + prefix_rows), HD)
    dv = scatter(joined(dbv, dpv)).reshape(ny * (BLOCK + prefix_rows), HD)
    dkv = jnp.concatenate([back(dk), back(dv)], axis=1)
    terms = lax.all_to_all(dkv[BLOCK:], smp, split_axis=1, concat_axis=0, tiled=True)
    d_prefix = jnp.sum(terms.reshape(-1, prefix_rows, HD).astype(F32), axis=0)
    return out[None], dq[None], dkv[:BLOCK][None], d_prefix.astype(BF16)


def solution(mesh):
    devices = mesh.devices.reshape(4, 2, 4, 8)
    split = Mesh(devices, ("x", "core", "y", "z"))
    smp, ctx = ("x", "core"), ("y", "z")
    return jax.shard_map(
        per_device,
        mesh=split,
        in_specs=(
            P(smp, ctx, None), P(smp, ctx, None), P(smp, ctx, None),
            P(ctx, smp), P(smp, None), P(smp, None),
        ),
        out_specs=(P(smp, ctx, None), P(smp, ctx, None), P(smp, ctx, None), P(ctx, smp)),
        check_vma=False,
    )
```

time: 850 us -> 268 us (0.32); the launches traced: 836 us -> 268 us
  waiting for transfers between devices: 597 us -> 109 us
  matrix products: 109 us -> 0 us
  local copies, waits for them, and re-layouts: 64.4 us -> 20.7 us
  blocking collectives: 15.3 us -> 58.3 us
  Pallas kernels: 0 us -> 34.9 us
  other arithmetic: 35.4 us -> 6.28 us
  starting transfers between devices: 0.2 us -> 25.5 us
    reduce_scatter x3 -> x2, waiting for transfers between devices: 457 us -> 48 us  [the longest x1 32.6 us: per_device(): dv = scatter(joined(dbv, dpv)).reshape(ny * (BLOCK + prefix_rows), HD)]
    dot_general x35 -> x0, matrix products: 109 us -> none  [the longest x4 19.4 us: one_head(): jnp.dot(grad_head, value_head.T, preferred_element_type=jnp.float32)]
    all_gather x2, waiting for transfers between devices: 140 us -> 41.3 us  [the longest x1 35.4 us: per_device(): lax.all_gather(v, 'z', axis=0, tiled=True)]
    all_to_all x0 -> x4, blocking collectives: none -> 43.7 us  [the longest x1 14 us: per_device(): dq = back(dq.reshape(ny * BLOCK, ROWS))]
    pallas_call x0 -> x1, Pallas kernels: none -> 34.9 us  [attend(): pl.pallas_call(attend_kernel, grid_spec=pltpu.PrefetchScalarGridSpec(num_...]
    all_to_all x0 -> x5, starting transfers between devices: none -> 25.3 us  [the longest x1 10.6 us: per_device(): lax.all_to_all(dkv[BLOCK:], smp, split_axis=1, concat_axis=0, tiled=True)]
    all_to_all x0 -> x5, waiting for transfers between devices: none -> 19.2 us  [the longest x1 10.1 us: per_device(): q = exchange(query[0]).reshape(ny, BLOCK, ROWS)]
    dot_general x1 -> x0, local copies, waits for them, and re-layouts: 19 us -> none  [per_device(): jnp.einsum('km,kbf->mbf', selector, slot_grads, precision=lax.Precision.H...]
  transfers between devices with their start and end apart: 5 -> 9, of which waited for: 4 -> 7; matrix products, arithmetic and copies ran while one was open for 8% -> 7% of each run, Pallas kernels for 0% -> 0%
where the time goes in v1:
time: 268 us
  waiting for transfers between devices  109 us (41%)
  blocking collectives  58.3 us (22%)
  Pallas kernels  34.9 us (13%)
  starting transfers between devices  25.5 us (10%)
  local copies, waits for them, and re-layouts  20.7 us (8%)
  between operations  13.9 us (5%)
  other arithmetic  6.28 us (2%)
    all_gather x1, waiting for transfers between devices, per_device(): lax.all_gather(v, 'z', axis=0, tiled=True)  35.4 us
    pallas_call x1, Pallas kernels, attend(): pl.pallas_call(attend_kernel, grid_spec=pltpu.PrefetchScalarGridSpec(num_...  34.9 us
    reduce_scatter x1, waiting for transfers between devices, per_device(): dv = scatter(joined(dbv, dpv)).reshape(ny * (BLOCK + prefix_rows), HD)  32.6 us
    reduce_scatter x1, waiting for transfers between devices, per_device(): dk = scatter(joined(dbk, dpk)).reshape(ny * (BLOCK + prefix_rows), HD)  15.4 us
    all_gather x1, blocking collectives, per_device(): with_features = lax.all_gather(prefix_kv, smp, axis=1, tiled=True)  14.6 us
    all_to_all x1, blocking collectives, per_device(): dq = back(dq.reshape(ny * BLOCK, ROWS))  14 us
    all_to_all x1, blocking collectives, per_device(): out = back(out.reshape(ny * BLOCK, ROWS))  13.5 us
    all_to_all x1, starting transfers between devices, per_device(): lax.all_to_all(dkv[BLOCK:], smp, split_axis=1, concat_axis=0, tiled=True)  10.6 us
  transfers between devices with their start and end apart: 9, of which 7 were waited for; matrix products, arithmetic and copies ran while one was open for 7% of the time, Pallas kernels for 0%

profile of v1, /device:TPU:1, one launch (start us, length us, event | category | flops | bytes accessed | tf_op | source)
XLA Modules:
  0.0 268.2 jit_solution(5121428691194862736)
XLA Ops:
  7.2 0.0 copy-start.2
  7.2 0.0 all-gather.3.cloned.1.call-start
  7.2 14.6 %all_gather.9 = bf16[32,1024]{1,0:T(8,128)(2,1)S(1)} all-gather(bf16[32,128]{1,0:T(8,128)(2,1)} %param.9), channel_id=1, replica_groups=mesh['x'=4,'core'=2,'y'=4,'z'=8] {'x','core'}, dimensions={1}, use_global_device_ids=true | all-gather | bytes 73728 | tf_op jit(solution)/shard_map/all_gather | solution.py:215
  21.8 1.0 fusion.2
  22.9 8.1 %all_to_all.141 = bf16[160,4,128]{2,0,1:T(8,128)(2,1)} all-to-all(bf16[160,4,128]{2,0,1:T(8,128)(2,1)S(1)} %bitcast.68), channel_id=1, replica_groups=mesh['x'=4,'core'=2,'y'=4,'z'=8] {'y'}, dimensions={1} | all-to-all | bytes 327680 | tf_op jit(solution)/shard_map/all_to_all | solution.py:217
  31.0 0.0 all-gather.3.cloned.1.call-update
  31.0 0.0 all-gather.5.cloned.1.call-start
  31.1 8.0 %all_to_all.142 = bf16[160,4,128]{2,0,1:T(8,128)(2,1)} all-to-all(bf16[160,4,128]{2,0,1:T(8,128)(2,1)S(1)} %bitcast.69), channel_id=1, replica_groups=mesh['x'=4,'core'=2,'y'=4,'z'=8] {'y'}, dimensions={1} | all-to-all | bytes 327680 | tf_op jit(solution)/shard_map/all_to_all | solution.py:218
  39.1 0.0 all-gather.5.cloned.1.call-update
  39.1 0.0 copy-done.2
  39.1 0.7 copy.35
  39.8 1.3 copy.36
  41.1 0.0 copy-start.3
  41.1 3.6 %all-to-all-start = ((bf16[128,4,1024]{2,0,1:T(8,128)(2,1)}), bf16[128,4,1024]{2,0,1:T(8,128)(2,1)S(1)}, u32[]{:S(2)}, u32[]{:S(2)}) async-start(bf16[128,4,1024]{2,0,1:T(8,128)(2,1)} %copy.36), calls=%async_computation | async-start | bytes 2097152 | tf_op jit(solution)/shard_map/all_to_all | solution.py:221
  44.8 0.0 copy-done.3
  44.8 0.7 copy.37
  45.5 1.3 copy.38
  46.8 10.1 %all-to-all-done = bf16[128,4,1024]{2,0,1:T(8,128)(2,1)S(1)} async-done(((bf16[128,4,1024]{2,0,1:T(8,128)(2,1)}), bf16[128,4,1024]{2,0,1:T(8,128)(2,1)S(1)}, u32[]{:S(2)}, u32[]{:S(2)}) %all-to-all-start) | async-done | bytes 1048608 | tf_op jit(solution)/shard_map/all_to_all | solution.py:221
  56.9 0.0 copy-start
  56.9 3.5 %all-to-all-start.1 = ((bf16[128,4,1024]{2,0,1:T(8,128)(2,1)}), bf16[128,4,1024]{2,0,1:T(8,128)(2,1)S(1)}, u32[]{:S(2)}, u32[]{:S(2)}) async-start(bf16[128,4,1024]{2,0,1:T(8,128)(2,1)} %copy.38), calls=%async_computation.1 | async-start | bytes 2097152 | tf_op jit(solution)/shard_map/all_to_all | solution.py:222
  60.4 0.0 reduce-scatter.3.cloned.1.call-start
  60.5 0.5 fusion.4.place
  61.0 0.5 multiply_add_fusion.block_ids
  61.5 5.9 %all-gather.3.cloned.1.call-done = bf16[5120,128]{1,0:T(8,128)(2,1)} async-done(((bf16[640,128]{1,0:T(8,128)(2,1)}), bf16[5120,128]{1,0:T(8,128)(2,1)}) %all-gather.3.cloned.1.call-update) | async-done | bytes 1310736 | tf_op jit(solution)/shard_map/all_gather | solution.py:219
  67.4 1.7 slice.36
  69.1 0.0 copy-done
  69.1 2.3 slice.34.bk_ref
  71.4 35.4 %all-gather.5.cloned.1.call-done = bf16[5120,128]{1,0:T(8,128)(2,1)} async-done(((bf16[640,128]{1,0:T(8,128)(2,1)}), bf16[5120,128]{1,0:T(8,128)(2,1)}) %all-gather.5.cloned.1.call-update) | async-done | bytes 1310736 | tf_op jit(solution)/shard_map/all_gather | solution.py:220
  106.9 1.7 slice.37
  108.6 2.3 slice.35.bv_ref
  110.9 0.0 all-to-all-done.1
  110.9 0.0 copy-start.1
  110.9 1.0 copy-done.1
  111.9 34.9 %attend.1 = (bf16[4,128,1024]{2,1,0:T(8,128)(2,1)}, bf16[4,128,1024]{2,1,0:T(8,128)(2,1)}, bf16[32,128,128]{2,1,0:T(8,128)(2,1)}, bf16[32,128,128]{2,1,0:T(8,128...) custom-call(s32[32]{0:T(128)} %bitcast.73, s32[32]{0:T(128)} %bitcast.74, s32[4]{0:T(128)} %multiply_add_fusion.block_ids, ...), custom_call_target="tpu_custom_call" | custom-call | tf_op jit(solution)/shard_map/attend/pallas_call | solution.py:179
  146.8 2.5 pad_maximum_fusion
  149.3 0.0 copy-start.6
  149.3 0.0 copy-start.7
  149.3 0.0 reduce-scatter.3.cloned.1.call-update
  149.3 0.0 reduce-scatter.5.cloned.1.call-start
  149.4 1.1 copy-done.6
  150.5 0.0 copy-done.7
  150.6 1.1 pad_maximum_fusion.1
  151.7 0.0 copy-start.5
  151.7 0.0 reduce-scatter.5.cloned.1.call-update
  151.7 0.0 copy-start.4
  151.8 1.2 copy-done.5
  152.9 13.5 %all_to_all.143 = bf16[4,128,1024]{2,1,0:T(8,128)(2,1)S(1)} all-to-all(bf16[4,128,1024]{2,1,0:T(8,128)(2,1)S(1)} %copy-done.5), channel_id=1, replica_groups=mesh['x'=4,'core'=2,'y'=4,'z'=8] {'y'}, dimensions={0} | all-to-all | bytes 2097152 | tf_op jit(solution)/shard_map/all_to_all | solution.py:233
  166.5 0.0 copy-done.4
  166.5 14.0 %all_to_all.144 = bf16[4,128,1024]{2,1,0:T(8,128)(2,1)S(1)} all-to-all(bf16[4,128,1024]{2,1,0:T(8,128)(2,1)S(1)} %copy-done.4), channel_id=1, replica_groups=mesh['x'=4,'core'=2,'y'=4,'z'=8] {'y'}, dimensions={0} | all-to-all | bytes 2097152 | tf_op jit(solution)/shard_map/all_to_all | solution.py:234
  180.5 15.4 %reduce-scatter.3.cloned.1.call-done = bf16[4,160,128]{2,1,0:T(8,128)(2,1)} async-done(((bf16[32,160,128]{2,1,0:T(8,128)(2,1)}), bf16[4,160,128]{2,1,0:T(8,128)(2,1)}) %reduce-scatter.3.cloned.1.call-update) | async-done | bytes 163856 | tf_op jit(solution)/shard_map/reduce_scatter | solution.py:237
  195.9 3.7 %all-to-all-start.6 = ((bf16[4,160,128]{2,1,0:T(8,128)(2,1)}), bf16[4,160,128]{2,1,0:T(8,128)(2,1)S(1)}, u32[]{:S(2)}, u32[]{:S(2)}) async-start(bf16[4,160,128]{2,1,0:T(8,128)(2,1)} %reduce-scatter.3.cloned.1.call-done), calls=%async_computation.7 | async-start | bytes 327680 | tf_op jit(solution)/shard_map/all_to_all | solution.py:239
  199.6 0.7 copy.41
  200.3 1.3 copy.46
  201.6 0.7 copy.42
  202.3 1.3 copy.47
  203.6 32.6 %reduce-scatter.5.cloned.1.call-done = bf16[4,160,128]{2,1,0:T(8,128)(2,1)} async-done(((bf16[32,160,128]{2,1,0:T(8,128)(2,1)}), bf16[4,160,128]{2,1,0:T(8,128)(2,1)}) %reduce-scatter.5.cloned.1.call-update) | async-done | bytes 163856 | tf_op jit(solution)/shard_map/reduce_scatter | solution.py:238
  236.1 0.0 all-to-all-done.6
  236.1 3.9 %all-to-all-start.7 = ((bf16[4,160,128]{2,1,0:T(8,128)(2,1)}), bf16[4,160,128]{2,1,0:T(8,128)(2,1)S(1)}, u32[]{:S(2)}, u32[]{:S(2)}) async-start(bf16[4,160,128]{2,1,0:T(8,128)(2,1)} %reduce-scatter.5.cloned.1.call-done), calls=%async_computation.9 | async-start | bytes 327680 | tf_op jit(solution)/shard_map/all_to_all | solution.py:239
  240.0 5.0 %all-to-all-done.7 = bf16[4,160,128]{2,1,0:T(8,128)(2,1)S(1)} async-done(((bf16[4,160,128]{2,1,0:T(8,128)(2,1)}), bf16[4,160,128]{2,1,0:T(8,128)(2,1)S(1)}, u32[]{:S(2)}, u32[]{:S(2)}) %all-to-all-start.7) | async-done | bytes 163872 | tf_op jit(solution)/shard_map/all_to_all | solution.py:239
  245.1 0.6 copy_bitcast_fusion.2
  245.7 10.6 %all-to-all-start.8 = ((bf16[32,8,128]{2,0,1:T(8,128)(2,1)}), bf16[32,8,128]{2,0,1:T(8,128)(2,1)S(1)}, u32[]{:S(2)}, u32[]{:S(2)}) async-start(bf16[32,8,128]{2,0,1:T(8,128)(2,1)} %copy_bitcast_fusion.2), calls=%async_computation.10 | async-start | bytes 131072 | tf_op jit(solution)/shard_map/all_to_all | solution.py:240
  256.3 0.7 slice_bitcast_fusion
  257.0 4.1 %all-to-all-done.8 = bf16[32,8,128]{2,0,1:T(8,128)(2,1)S(1)} async-done(((bf16[32,8,128]{2,0,1:T(8,128)(2,1)}), bf16[32,8,128]{2,0,1:T(8,128)(2,1)S(1)}, u32[]{:S(2)}, u32[]{:S(2)}) %all-to-all-start.8) | async-done | bytes 65568 | tf_op jit(solution)/shard_map/all_to_all | solution.py:240
  261.1 0.6 reduce_sum.12
  (4 shorter events, 0.1 us)
Async XLA Ops:
  7.2 32.0 %copy-start.2 = (bf16[1,128,4096]{2,1,0:T(8,128)(2,1)S(1)}, bf16[1,128,4096]{2,1,0:T(8,128)(2,1)}, u32[]{:S(2)}) copy-start(bf16[1,128,4096]{2,1,0:T(8,128)(2,1)} %param.6) | copy-start | bytes 3145732
  7.2 60.2 %all-gather.3.cloned.1.call-start = ((), (), s32[]{:S(2)}) async-start(), calls=%async_computation.11 | async-start | bytes 1474560 | tf_op jit(solution)/shard_map/all_gather | solution.py:219
  31.0 75.9 %all-gather.5.cloned.1.call-start = ((), (), s32[]{:S(2)}) async-start(), calls=%async_computation.12 | async-start | bytes 1474560 | tf_op jit(solution)/shard_map/all_gather | solution.py:220
  41.1 3.7 %copy-start.3 = (bf16[1,128,4096]{2,1,0:T(8,128)(2,1)S(1)}, bf16[1,128,4096]{2,1,0:T(8,128)(2,1)}, u32[]{:S(2)}) copy-start(bf16[1,128,4096]{2,1,0:T(8,128)(2,1)} %param.7) | copy-start | bytes 3145732
  41.1 15.8 %all-to-all-start = ((bf16[128,4,1024]{2,0,1:T(8,128)(2,1)}), bf16[128,4,1024]{2,0,1:T(8,128)(2,1)S(1)}, u32[]{:S(2)}, u32[]{:S(2)}) async-start(bf16[128,4,1024]{2,0,1:T(8,128)(2,1)} %copy.36), calls=%async_computation | async-start | bytes 2097152 | tf_op jit(solution)/shard_map/all_to_all | solution.py:221
  56.9 12.2 %copy-start = (bf16[128,4,1024]{2,0,1:T(8,128)(2,1)}, bf16[128,4,1024]{2,0,1:T(8,128)(2,1)S(1)}, u32[]{:S(2)}) copy-start(bf16[128,4,1024]{2,0,1:T(8,128)(2,1)S(1)} %all-to-all-done) | copy-start | bytes 3145732
  56.9 54.0 %all-to-all-start.1 = ((bf16[128,4,1024]{2,0,1:T(8,128)(2,1)}), bf16[128,4,1024]{2,0,1:T(8,128)(2,1)S(1)}, u32[]{:S(2)}, u32[]{:S(2)}) async-start(bf16[128,4,1024]{2,0,1:T(8,128)(2,1)} %copy.38), calls=%async_computation.1 | async-start | bytes 2097152 | tf_op jit(solution)/shard_map/all_to_all | solution.py:222
  60.4 135.5 %reduce-scatter.3.cloned.1.call-start = ((), (), s32[]{:S(2)}) async-start(), calls=%async_computation.13 | async-start | bytes 1474560 | tf_op jit(solution)/shard_map/reduce_scatter | solution.py:237
  110.9 1.0 copy-start.1
  149.3 1.2 copy-start.6
  149.3 1.3 copy-start.7
  149.3 86.8 %reduce-scatter.5.cloned.1.call-start = ((), (), s32[]{:S(2)}) async-start(), calls=%async_computation.14 | async-start | bytes 1474560 | tf_op jit(solution)/shard_map/reduce_scatter | solution.py:238
  151.7 1.2 copy-start.5
  151.7 14.7 %copy-start.4 = (bf16[4,128,1024]{2,1,0:T(8,128)(2,1)S(1)}, bf16[4,128,1024]{2,1,0:T(8,128)(2,1)}, u32[]{:S(2)}) copy-start(bf16[4,128,1024]{2,1,0:T(8,128)(2,1)} %get-tuple-element.11) | copy-start | bytes 3145732
  195.9 40.2 %all-to-all-start.6 = ((bf16[4,160,128]{2,1,0:T(8,128)(2,1)}), bf16[4,160,128]{2,1,0:T(8,128)(2,1)S(1)}, u32[]{:S(2)}, u32[]{:S(2)}) async-start(bf16[4,160,128]{2,1,0:T(8,128)(2,1)} %reduce-scatter.3.cloned.1.call-done), calls=%async_computation.7 | async-start | bytes 327680 | tf_op jit(solution)/shard_map/all_to_all | solution.py:239
  236.1 8.9 %all-to-all-start.7 = ((bf16[4,160,128]{2,1,0:T(8,128)(2,1)}), bf16[4,160,128]{2,1,0:T(8,128)(2,1)S(1)}, u32[]{:S(2)}, u32[]{:S(2)}) async-start(bf16[4,160,128]{2,1,0:T(8,128)(2,1)} %reduce-scatter.5.cloned.1.call-done), calls=%async_computation.9 | async-start | bytes 327680 | tf_op jit(solution)/shard_map/all_to_all | solution.py:239
  245.7 15.4 %all-to-all-start.8 = ((bf16[32,8,128]{2,0,1:T(8,128)(2,1)}), bf16[32,8,128]{2,0,1:T(8,128)(2,1)S(1)}, u32[]{:S(2)}, u32[]{:S(2)}) async-start(bf16[32,8,128]{2,0,1:T(8,128)(2,1)} %copy_bitcast_fusion.2), calls=%async_computation.10 | async-start | bytes 131072 | tf_op jit(solution)/shard_map/all_to_all | solution.py:240
Sparse Core Ops, SparseCore 0:
  31.1 36.2 all-gather.2
  69.2 37.6 all-gather.4
  149.5 46.3 reduce-scatter.2
  198.3 37.7 reduce-scatter.4

commit v2 on v1

v2 whole, which is shorter than its diff:
```python
import jax
import jax.numpy as jnp
from jax import lax
from jax.experimental import pallas as pl
from jax.experimental.pallas import tpu as pltpu
from jax.sharding import Mesh, PartitionSpec as P

HK = 4
HD = 128
GROUP = 8
BLOCK = 128
NB = 32
DEPTH = 8
PREFIX = 1024
ROWS = GROUP * BLOCK
CHUNK = 256
TILE = 64
SCALE = HD ** -0.5
SCALE_LOG2E = SCALE * 1.4426950408889634
MASKED = -1e30
F32 = jnp.float32
BF16 = jnp.bfloat16


def dot(a, b):
    return lax.dot_general(a, b, (((1,), (0,)), ((), ())), preferred_element_type=F32)


def dot_t(a, b):
    return lax.dot_general(a, b, (((1,), (1,)), ((), ())), preferred_element_type=F32)


def my_blocks(step):
    ny, nz = lax.axis_size("y"), lax.axis_size("z")
    return lax.rem(lax.axis_index("y") - step + ny, ny) * nz + lax.axis_index("z")


def place_of(block):
    ny, nz = lax.axis_size("y"), lax.axis_size("z")
    return lax.rem(block, nz) * ny + lax.rem(lax.axis_index("y") - block // nz + ny, ny)


def half_moves(first):
    moves = []
    for feature in range(2 * HK):
        half = first if feature >= HK else 1 - first
        for holder in range(HK):
            moves.append((feature * HK + holder, (holder * 2 + half) * HK + feature % HK))
    return moves


def fold(a):
    return a.reshape(a.shape[0] // 8, 8, a.shape[1])


def head_cols(h):
    return slice(h * BLOCK, (h + 1) * BLOCK)


def prefix_kernel(
    lengths, qg0, qg1, qg2, qg3, prefix,
    qt, gt, probs, out_t, stats, pkt, pvt, scores,
):
    step = pl.program_id(0)

    @pl.when(step == 0)
    def _():
        pkt[...] = prefix[:, :HD].T
        pvt[...] = prefix[:, HD:].T

    row_live = lax.broadcasted_iota(jnp.int32, (HD, BLOCK), 1) < lengths[my_blocks(step)]
    for d, part in enumerate((qg0, qg1, qg2, qg3)):
        @pl.when(step == d)
        def _(part=part):
            for h in range(GROUP):
                cols = head_cols(h)
                qt[0, :, cols] = part[0, :, cols].T
                gt[0, :, cols] = jnp.where(row_live, part[1, :, cols].astype(F32).T, 0.0).astype(BF16)

    top = jnp.full((8, ROWS), MASKED, F32)
    for c in range(PREFIX // CHUNK):
        keys = slice(c * CHUNK, (c + 1) * CHUNK)
        s = dot(prefix[keys, :HD], qt[0])
        scores[keys, :] = s
        top = jnp.maximum(top, jnp.max(fold(s), axis=0))
    top = jnp.max(top, axis=0, keepdims=True)
    peak = top * SCALE_LOG2E
    total = jnp.zeros((8, ROWS), F32)
    acc = jnp.zeros((HD, ROWS), F32)
    for c in range(PREFIX // CHUNK):
        keys = slice(c * CHUNK, (c + 1) * CHUNK)
        e = jnp.exp2(scores[keys, :] * SCALE_LOG2E - peak)
        total = total + jnp.sum(fold(e), axis=0)
        low = e.astype(BF16)
        probs[0, keys, :] = low
        acc = acc + dot(pvt[:, keys], low)
    out_t[0] = acc
    stats[0, 0:1, :] = top
    stats[0, 1:2, :] = jnp.sum(total, axis=0, keepdims=True)


def branch_kernel(
    parents, lengths, qt, gt, prefix_out, stats, kv,
    out, dq_part, glp, qlp, rows_out, dkv,
    qlt, glt, sk, sv, skt, svt, scores, probs, acc, bias, abk, abv,
):
    step = pl.program_id(0)
    block = my_blocks(step)
    live = lengths[block]

    @pl.when(step == 0)
    def _():
        abk[...] = jnp.zeros_like(abk)
        abv[...] = jnp.zeros_like(abv)

    slots, used = [], []
    current = block
    for k in range(DEPTH):
        in_use = current >= 0
        slot = jnp.where(in_use, current, block)
        slots.append(slot)
        used.append(in_use)
        current = jnp.where(in_use, parents[slot], -1)
    key_row = lax.broadcasted_iota(jnp.int32, (BLOCK, BLOCK), 0)
    query_row = lax.broadcasted_iota(jnp.int32, (BLOCK, BLOCK), 1)
    pairs = DEPTH // 2
    acc[0:8, :] = jnp.broadcast_to(stats[0, 0:1, :], (8, ROWS))
    for j in range(pairs):
        @pl.when(used[2 * j])
        def _(j=j):
            for k in (2 * j, 2 * j + 1):
                rows = head_cols(k)
                at = place_of(slots[k])
                key = kv[at, 0]
                value = kv[at, 1]
                sk[rows, :] = key
                sv[rows, :] = value
                skt[:, rows] = key.T
                svt[:, rows] = value.T
                seen = key_row < jnp.where(used[k], lengths[slots[k]], 0)
                if k == 0:
                    seen = seen & (key_row <= query_row)
                bias[rows, :] = jnp.where(seen, 0.0, MASKED)
            rows = slice(j * CHUNK, (j + 1) * CHUNK)
            s = dot(sk[rows, :], qt[0])
            s = s + jnp.concatenate([bias[rows, :]] * GROUP, axis=1)
            scores[rows, :] = s
            acc[0:8, :] = jnp.maximum(acc[0:8, :], jnp.max(fold(s), axis=0))
    peak = jnp.max(acc[0:8, :], axis=0, keepdims=True) * SCALE_LOG2E

    acc[...] = jnp.zeros_like(acc)
    for j in range(pairs):
        @pl.when(used[2 * j])
        def _(j=j):
            rows = slice(j * CHUNK, (j + 1) * CHUNK)
            e = jnp.exp2(scores[rows, :] * SCALE_LOG2E - peak)
            acc[HD:HD + 8, :] += jnp.sum(fold(e), axis=0)
            low = e.astype(BF16)
            probs[rows, :] = low
            acc[0:HD, :] += dot(svt[:, rows], low)

    alpha = jnp.exp2(stats[0, 0:1, :] * SCALE_LOG2E - peak)
    total = alpha * stats[0, 1:2, :] + jnp.sum(acc[HD:HD + 8, :], axis=0, keepdims=True)
    inverse = 1.0 / total
    prefix_inverse = alpha * inverse
    out_t = acc[0:HD, :] * inverse + prefix_out[0] * prefix_inverse
    grad_t = gt[0].astype(F32)
    query_t = qt[0].astype(F32)
    delta = jnp.sum(grad_t * out_t.astype(BF16).astype(F32), axis=0, keepdims=True)
    glt[...] = (grad_t * inverse).astype(BF16)
    qlt[...] = (query_t * (inverse * SCALE)).astype(BF16)
    glp[0] = (grad_t * prefix_inverse).astype(BF16)
    qlp[0] = (query_t * (prefix_inverse * SCALE)).astype(BF16)
    rows_out[0, 0:1, :] = delta
    rows_out[0, 1:2, :] = prefix_inverse * SCALE
    row_live = lax.broadcasted_iota(jnp.int32, (HD, BLOCK), 1) < live
    for h in range(GROUP):
        cols = head_cols(h)
        out[0, :, cols] = jnp.where(row_live, out_t[:, cols], 0.0).T.astype(BF16)

    acc[0:HD, :] = jnp.zeros((HD, ROWS), F32)
    for j in range(pairs):
        @pl.when(used[2 * j])
        def _(j=j):
            rows = slice(j * CHUNK, (j + 1) * CHUNK)
            low = probs[rows, :]
            ds = (low.astype(F32) * (dot(sv[rows, :], gt[0]) - delta)).astype(BF16)
            dv = dot_t(low, glt[...])
            dk = dot_t(ds, qlt[...])
            for k in range(2):
                at = place_of(slots[2 * j + k])
                abv[at] += dv[k * BLOCK:(k + 1) * BLOCK]
                abk[at] += dk[k * BLOCK:(k + 1) * BLOCK]
            acc[0:HD, :] += dot(skt[:, rows], ds)
    dq_part[0] = acc[0:HD, :] * (inverse * SCALE)

    @pl.when(step == pl.num_programs(0) - 1)
    def _():
        dkv[:, 0] = abk[...].astype(BF16)
        dkv[:, 1] = abv[...].astype(BF16)


def prefix_back_kernel(
    gt, probs, glp, qlp, rows_in, dq_part, out, pkt, prefix, both, dp, apk, apv,
):
    step = pl.program_id(0)

    @pl.when(step == 0)
    def _():
        apk[...] = jnp.zeros_like(apk)
        apv[...] = jnp.zeros_like(apv)

    delta = rows_in[0, 0:1, :]
    acc = jnp.zeros((HD, ROWS), F32)
    for c in range(PREFIX // CHUNK):
        keys = slice(c * CHUNK, (c + 1) * CHUNK)
        low = probs[0, keys, :]
        ds = (low.astype(F32) * (dot(prefix[keys, HD:], gt[0]) - delta)).astype(BF16)
        apv[keys, :] += dot_t(low, glp[0])
        apk[keys, :] += dot_t(ds, qlp[0])
        acc = acc + dot(pkt[:, keys], ds)
    dq_t = acc * rows_in[0, 1:2, :] + dq_part[0]
    for h in range(GROUP):
        cols = head_cols(h)
        both[0, 1, :, cols] = dq_t[:, cols].T.astype(BF16)
    both[0, 0] = out[0]

    @pl.when(step == pl.num_programs(0) - 1)
    def _():
        dp[:, :HD] = apk[...].astype(BF16)
        dp[:, HD:] = apv[...].astype(BF16)


def whole(shape):
    return pl.BlockSpec(shape, lambda i, *_: (0,) * len(shape))


def stepped(shape):
    return pl.BlockSpec((1, *shape[1:]), lambda i, *_: (i,) + (0,) * (len(shape) - 1))


def call(body, name, scalars, steps, args, outs, scratch):
    spec = lambda shape, by_step: stepped(shape) if by_step else whole(shape)
    return pl.pallas_call(
        body,
        grid_spec=pltpu.PrefetchScalarGridSpec(
            num_scalar_prefetch=len(scalars),
            grid=(steps,),
            in_specs=[spec(a.shape, by_step) for a, by_step in args],
            out_specs=[spec(shape, by_step) for shape, _, by_step in outs],
            scratch_shapes=[pltpu.VMEM(shape, dtype) for shape, dtype in scratch],
        ),
        out_shape=[jax.ShapeDtypeStruct(shape, dtype) for shape, dtype, _ in outs],
        compiler_params=pltpu.CompilerParams(vmem_limit_bytes=60 * 1024 * 1024),
        name=name,
    )(*scalars, *[a for a, _ in args])


def prefix_forward(lengths, qg, prefix):
    n = len(qg)
    tall, rows = (n, HD, ROWS), (n, 8, ROWS)
    return call(
        prefix_kernel, "prefix_forward", [lengths], n,
        [(a, False) for a in (*qg, prefix)],
        [(tall, BF16, True), (tall, BF16, True), ((n, PREFIX, ROWS), BF16, True), (tall, F32, True),
         (rows, F32, True), ((HD, PREFIX), BF16, False)],
        [((HD, PREFIX), BF16), ((PREFIX, ROWS), F32)],
    )


def branch(parents, lengths, qt, gt, prefix_out, stats, kv):
    n = qt.shape[0]
    tall, rows, keys = (n, HD, ROWS), (n, 8, ROWS), DEPTH * BLOCK
    return call(
        branch_kernel, "branch", [parents, lengths], n,
        [(qt, True), (gt, True), (prefix_out, True), (stats, True), (kv, False)],
        [((n, BLOCK, ROWS), BF16, True), (tall, F32, True), (tall, BF16, True), (tall, BF16, True),
         (rows, F32, True), (kv.shape, BF16, False)],
        [((HD, ROWS), BF16), ((HD, ROWS), BF16), ((keys, HD), BF16), ((keys, HD), BF16),
         ((HD, keys), BF16), ((HD, keys), BF16), ((keys, ROWS), F32), ((keys, ROWS), BF16),
         ((HD + 8, ROWS), F32), ((keys, BLOCK), F32), ((NB, BLOCK, HD), F32), ((NB, BLOCK, HD), F32)],
    )


def prefix_backward(gt, probs, glp, qlp, rows_in, dq_part, out, pkt, prefix):
    n = gt.shape[0]
    return call(
        prefix_back_kernel, "prefix_backward", [], n,
        [(a, True) for a in (gt, probs, glp, qlp, rows_in, dq_part, out)] + [(pkt, False), (prefix, False)],
        [((n, 2, BLOCK, ROWS), BF16, True), (prefix.shape, BF16, False)],
        [((PREFIX, HD), F32), ((PREFIX, HD), F32)],
    )


def head_at(d):
    return lax.rem(lax.axis_index("y") + d, HK)


def pack_kernel(sources, targets):
    for d, target in enumerate(targets):
        for part in range(2):
            width = target.shape[2]
            source = sources[part % len(sources)]
            first = 0 if len(sources) > 1 else part * HK * width
            cols = pl.ds(pl.multiple_of(first + head_at(d) * width, 128), width)
            target[part] = source[:, cols]


def pack(*sources):
    rows, columns = sources[0].shape
    width = columns // (HK if len(sources) > 1 else 2 * HK)
    tile, n = min(rows, TILE), len(sources)
    return pl.pallas_call(
        lambda *refs: pack_kernel(refs[:n], refs[n:]),
        grid=(rows // tile,),
        in_specs=[pl.BlockSpec((tile, columns), lambda i: (i, 0))] * n,
        out_specs=[pl.BlockSpec((2, tile, width), lambda i: (0, i, 0))] * HK,
        out_shape=[jax.ShapeDtypeStruct((2, rows, width), BF16)] * HK,
        name="pack",
    )(*sources)


def unpack_kernel(sources, targets):
    for d, source in enumerate(sources):
        for part in range(2):
            width = source.shape[2]
            target = targets[part % len(targets)]
            first = 0 if len(targets) > 1 else part * HK * width
            cols = pl.ds(pl.multiple_of(first + head_at(d) * width, 128), width)
            target[:, cols] = source[part]


def unpack(sources, count):
    _, rows, width = sources[0].shape
    tile, n = min(rows, TILE), len(sources)
    columns = 2 * HK * width // count
    return pl.pallas_call(
        lambda *refs: unpack_kernel(refs[:n], refs[n:]),
        grid=(rows // tile,),
        in_specs=[pl.BlockSpec((2, tile, width), lambda i: (0, i, 0))] * n,
        out_specs=[pl.BlockSpec((tile, columns), lambda i: (i, 0))] * count,
        out_shape=[jax.ShapeDtypeStruct((rows, columns), BF16)] * count,
        name="unpack",
    )(*sources)


def shift(x, axis, by):
    n = lax.axis_size(axis)
    return lax.ppermute(x, axis, [(i, (i + by) % n) for i in range(n)])


def spread(x, axes):
    n = lax.axis_size(axes)
    return lax.all_to_all(jnp.broadcast_to(x, (n, *x.shape)), axes, split_axis=0, concat_axis=0, tiled=True)


def gather_terms(x, axes):
    n = lax.axis_size(axes)
    x = x.reshape(n, x.shape[0] // n, x.shape[1])
    return jnp.sum(lax.all_to_all(x, axes, split_axis=0, concat_axis=0, tiled=True).astype(F32), axis=0).astype(BF16)


def per_device(query, d_out, branch_kv, prefix_kv, parents, lengths):
    ny, nz = lax.axis_size("y"), lax.axis_size("z")

    def exchange(parts):
        return [parts[0]] + [shift(parts[d], "y", d) for d in range(1, ny)]

    def back(parts):
        return [parts[0]] + [shift(parts[d], "y", -d) for d in range(1, ny)]

    kv = exchange(pack(branch_kv[0]))
    ring, smp = ("x", "core", "y"), ("x", "core")
    half_rows = prefix_kv.shape[0] // 2
    value_holder = lax.axis_index("x") >= 2
    low, high = prefix_kv[:half_rows], prefix_kv[half_rows:]
    one = lax.ppermute(jnp.where(value_holder, low, high), ring, half_moves(0))
    two = lax.ppermute(jnp.where(value_holder, high, low), ring, half_moves(1))
    odd = lax.axis_index("core") == 1
    mine = jnp.concatenate([jnp.where(odd, one, two), jnp.where(odd, two, one)], axis=1)
    kv = lax.all_gather(jnp.stack(kv), "z", axis=0, tiled=True)
    qg = exchange(pack(query[0], d_out[0]))
    prefix = spread(spread(mine, "z").reshape(-1, 2 * HD), smp).reshape(PREFIX, 2 * HD)

    qt, gt, probs, prefix_out, stats, pkt = prefix_forward(lengths[0], qg, prefix)
    out, dq_part, glp, qlp, rows, dkv = branch(parents[0], lengths[0], qt, gt, prefix_out, stats, kv)
    dkv = lax.psum_scatter(dkv, "z", scatter_dimension=0, tiled=True)
    od, dp = prefix_backward(gt, probs, glp, qlp, rows, dq_part, out, pkt, prefix)

    mine = gather_terms(gather_terms(dp, smp), "z")
    key, value = mine[:, :HD], mine[:, HD:]
    returns = lambda first: [(b, a) for a, b in half_moves(first)]
    one = lax.ppermute(jnp.where(odd, key, value), ring, returns(0))
    two = lax.ppermute(jnp.where(odd, value, key), ring, returns(1))
    d_prefix = jnp.concatenate(
        [jnp.where(value_holder, one, two), jnp.where(value_holder, two, one)], axis=0)
    out, dq = unpack(back([od[d] for d in range(ny)]), 2)
    d_branch, = unpack(back([dkv[d] for d in range(ny)]), 1)
    return out[None], dq[None], d_branch[None], d_prefix


def solution(mesh):
    devices = mesh.devices.reshape(4, 2, 4, 8)
    split = Mesh(devices, ("x", "core", "y", "z"))
    smp, ctx = ("x", "core"), ("y", "z")
    return jax.shard_map(
        per_device,
        mesh=split,
        in_specs=(
            P(smp, ctx, None), P(smp, ctx, None), P(smp, ctx, None),
            P(ctx, smp), P(smp, None), P(smp, None),
        ),
        out_specs=(P(smp, ctx, None), P(smp, ctx, None), P(smp, ctx, None), P(ctx, smp)),
        check_vma=False,
    )
```

time: 268 us -> 179 us (0.67)
  waiting for transfers between devices: 109 us -> 23.7 us
  blocking collectives: 58.3 us -> 16.7 us
  starting transfers between devices: 25.5 us -> 54.1 us
  Pallas kernels: 34.9 us -> 57 us
  local copies, waits for them, and re-layouts: 20.7 us -> 8.73 us
  other arithmetic: 6.28 us -> 3.01 us
    reduce_scatter x2 -> x1, waiting for transfers between devices: 48 us -> 0.02 us  [per_device(): dkv = lax.psum_scatter(dkv, 'z', scatter_dimension=0, tiled=True)]
    all_gather x2 -> x1, waiting for transfers between devices: 41.3 us -> 0.01 us  [per_device(): kv = lax.all_gather(jnp.stack(kv), 'z', axis=0, tiled=True)]
    ppermute x0 -> x16, starting transfers between devices: none -> 34.4 us  [the longest x12 22.2 us: shift(): return lax.ppermute(x, axis, [(i, (i + by) % n) for i in range(n)])]
    all_to_all x4 -> x1, blocking collectives: 43.7 us -> 16.7 us  [gather_terms(): lax.all_to_all(x, axes, split_axis=0, concat_axis=0, tiled=True).astype(F32)]
    pallas_call x1 -> x7, Pallas kernels: 34.9 us -> 57 us  [the longest x3 48.6 us: call(): pl.pallas_call(body, grid_spec=pltpu.PrefetchScalarGridSpec(num_scalar_pr...]
    ppermute x0 -> x16, waiting for transfers between devices: none -> 21.4 us  [the longest x12 18 us: shift(): return lax.ppermute(x, axis, [(i, (i + by) % n) for i in range(n)])]
    all_to_all x5 -> x3, waiting for transfers between devices: 19.2 us -> 2.24 us  [the longest x1 2.24 us: gather_terms(): lax.all_to_all(x, axes, split_axis=0, concat_axis=0, tiled=True).astype(F32)]
    all_gather x1 -> x0, blocking collectives: 14.6 us -> none  [per_device(): with_features = lax.all_gather(prefix_kv, smp, axis=1, tiled=True)]
  transfers between devices with their start and end apart: 9 -> 21, of which waited for: 7 -> 8; matrix products, arithmetic and copies ran while one was open for 7% -> 3% of each run, Pallas kernels for 0% -> 17%
where the time goes in v2:
time: 179 us; the launch traced here: 178 us
  Pallas kernels  57 us (32%)
  starting transfers between devices  54.1 us (30%)
  waiting for transfers between devices  23.7 us (13%)
  blocking collectives  16.7 us (9%)
  between operations  14.2 us (8%)
  local copies, waits for them, and re-layouts  8.73 us (5%)
  other arithmetic  3.01 us (2%)
    pallas_call x3, Pallas kernels, call(): pl.pallas_call(body, grid_spec=pltpu.PrefetchScalarGridSpec(num_scalar_pr...  48.6 us
    ppermute x12, starting transfers between devices, shift(): return lax.ppermute(x, axis, [(i, (i + by) % n) for i in range(n)])  22.2 us
    ppermute x12, waiting for transfers between devices, shift(): return lax.ppermute(x, axis, [(i, (i + by) % n) for i in range(n)])  18 us
    all_to_all x1, blocking collectives, gather_terms(): lax.all_to_all(x, axes, split_axis=0, concat_axis=0, tiled=True).astype(F32)  16.7 us
    all_to_all x2, starting transfers between devices, spread(): lax.all_to_all(jnp.broadcast_to(x, (n, *x.shape)), axes, split_axis=0, co...  16.3 us
    ppermute x1, starting transfers between devices, per_device(): two = lax.ppermute(jnp.where(value_holder, high, low), ring, half_moves(1))  4.95 us
    ppermute x1, starting transfers between devices, per_device(): two = lax.ppermute(jnp.where(odd, value, key), ring, returns(1))  4.5 us
    pallas_call x2, Pallas kernels, pack(): pl.pallas_call(lambda *refs: pack_kernel(refs[:n], refs[n:]), grid=(rows...  4.29 us
  transfers between devices with their start and end apart: 21, of which 8 were waited for; matrix products, arithmetic and copies ran while one was open for 3% of the time, Pallas kernels for 17%

profile of v2, /device:TPU:1, one launch (start us, length us, event | category | flops | bytes accessed | tf_op | source)
XLA Modules:
  0.0 177.5 jit_solution(12455229991768402602)
XLA Ops:
  7.2 0.0 all-gather.2.cloned.1.call-start
  7.2 1.7 pack.3
  8.9 2.1 %collective-permute-start.5 = (bf16[2,128,128]{2,1,0:T(8,128)(2,1)}, bf16[2,128,128]{2,1,0:T(8,128)(2,1)S(1)}, u32[]{:S(2)}, u32[]{:S(2)}) collective-permute-start(bf16[2,128,128]{2,1,0:T(8,128)(2,1)} %get-tuple-element.38), channel_id=1, source_target_pairs={{0,8},{8,16},{16,24},{24,0},{1,9},{9,17},{17,25},{25,1},{2,10},{10... | collective-permute-start | bytes 196616 | tf_op jit(solution)/shard_map/ppermute | solution.py:349
  11.0 2.6 %collective-permute-start.6 = (bf16[2,128,128]{2,1,0:T(8,128)(2,1)}, bf16[2,128,128]{2,1,0:T(8,128)(2,1)S(1)}, u32[]{:S(2)}, u32[]{:S(2)}) collective-permute-start(bf16[2,128,128]{2,1,0:T(8,128)(2,1)} %get-tuple-element.39), channel_id=1, source_target_pairs={{0,16},{8,24},{16,0},{24,8},{1,17},{9,25},{17,1},{25,9},{2,18},{10... | collective-permute-start | bytes 196616 | tf_op jit(solution)/shard_map/ppermute | solution.py:349
  13.7 1.1 collective-permute-start.7
  14.7 0.0 collective-permute-done.5
  14.7 1.7 collective-permute-done.6
  16.5 0.8 collective-permute-done.7
  17.3 1.6 pad_maximum_fusion
  18.9 0.0 all-gather.2.cloned.1.call-update
  18.9 0.7 broadcast_select_fusion.3
  19.6 0.0 collective-permute-start.3
  19.6 4.9 %collective-permute-start.4 = (bf16[16,128]{1,0:T(8,128)(2,1)S(1)}, bf16[16,128]{1,0:T(8,128)(2,1)S(1)}, u32[]{:S(2)}, u32[]{:S(2)}) collective-permute-start(bf16[16,128]{1,0:T(8,128)(2,1)S(1)} %get-tuple-element.67), channel_id=1, source_target_pairs={{0,0},{8,64},{16,128},{24,192},{32,8},{40,72},{48,136},{56,200},{6... | collective-permute-start | bytes 12296 | tf_op jit(solution)/shard_map/ppermute | solution.py:378
  24.6 0.0 collective-permute-done.3
  24.6 3.5 %collective-permute-done.4 = bf16[16,128]{1,0:T(8,128)(2,1)S(1)} collective-permute-done((bf16[16,128]{1,0:T(8,128)(2,1)S(1)}, bf16[16,128]{1,0:T(8,128)(2,1)S(1)}, u32[]{:S(2)}, u32[]{:S(2)}) %collective-permute-start.4) | collective-permute-done | bytes 4128 | tf_op jit(solution)/shard_map/ppermute | solution.py:378
  28.1 0.6 broadcast_in_dim.15
  28.7 8.2 %all-to-all-start = ((bf16[8,16,256]{2,1,0:T(8,128)(2,1)}), bf16[8,16,256]{2,1,0:T(8,128)(2,1)S(1)}, u32[]{:S(2)}, u32[]{:S(2)}) async-start(bf16[8,16,256]{2,1,0:T(8,128)(2,1)} %broadcast_in_dim.15), calls=%async_computation | async-start | bytes 131072 | tf_op jit(solution)/shard_map/all_to_all | solution.py:354
  36.9 2.6 %pack.2 = (bf16[2,128,1024]{2,1,0:T(8,128)(2,1)}, bf16[2,128,1024]{2,1,0:T(8,128)(2,1)}, bf16[2,128,1024]{2,1,0:T(8,128)(2,1)}, bf16[2,128,1024]{2,1,0:T(8,128)(2,1)}) custom-call(bf16[128,4096]{1,0:T(8,128)(2,1)} %bitcast.34, bf16[128,4096]{1,0:T(8,128)(2,1)} %bitcast.35), custom_call_target="tpu_custom_call" | custom-call | tf_op jit(solution)/shard_map/pack/pallas_call | solution.py:313
  39.4 0.4 collective-permute-start
  39.8 4.6 %collective-permute-start.1 = (bf16[2,128,1024]{2,1,0:T(8,128)(2,1)}, bf16[2,128,1024]{2,1,0:T(8,128)(2,1)S(1)}, u32[]{:S(2)}, u32[]{:S(2)}) collective-permute-start(bf16[2,128,1024]{2,1,0:T(8,128)(2,1)} %get-tuple-element.30), channel_id=1, source_target_pairs={{0,16},{8,24},{16,0},{24,8},{1,17},{9,25},{17,1},{25,9},{2,18},{10... | collective-permute-start | bytes 1572872 | tf_op jit(solution)/shard_map/ppermute | solution.py:349
  44.4 1.4 collective-permute-start.2
  45.8 0.0 all-to-all-done
  45.8 0.9 broadcast_in_dim.16
  46.7 8.1 %all-to-all-start.1 = ((bf16[8,128,256]{2,1,0:T(8,128)(2,1)}), bf16[8,128,256]{2,1,0:T(8,128)(2,1)S(1)}, u32[]{:S(2)}, u32[]{:S(2)}) async-start(bf16[8,128,256]{2,1,0:T(8,128)(2,1)} %broadcast_in_dim.16), calls=%async_computation.1 | async-start | bytes 1048576 | tf_op jit(solution)/shard_map/all_to_all | solution.py:354
  54.8 0.0 reduce-scatter.2.cloned.1.call-start
  54.8 0.7 collective-permute-done.qg1
  55.4 12.0 %collective-permute-done.1.qg2 = bf16[2,128,1024]{2,1,0:T(8,128)(2,1)S(1)} collective-permute-done((bf16[2,128,1024]{2,1,0:T(8,128)(2,1)}, bf16[2,128,1024]{2,1,0:T(8,128)(2,1)S(1)}, u32[]{:S(2)}, u32[]{:S(2)}) %collective-permute-start.1) | collective-permute-done | bytes 524320 | tf_op jit(solution)/shard_map/ppermute | solution.py:349
  67.4 0.0 collective-permute-done.2.qg3
  67.4 0.0 all-to-all-done.1
  67.5 0.8 copy-done.4
  68.2 0.2 copy-done.6
  68.4 0.2 copy-done
  68.6 12.4 %prefix_forward.1 = (bf16[4,128,1024]{2,1,0:T(8,128)(2,1)}, bf16[4,128,1024]{2,1,0:T(8,128)(2,1)}, bf16[4,1024,1024]{2,1,0:T(8,128)(2,1)}, f32[4,128,1024]{2,1,0...) custom-call(s32[32]{0:T(128)} %bitcast.45, bf16[2,128,1024]{2,1,0:T(8,128)(2,1)} %get-tuple-element.28.qg0, ...), custom_call_target="tpu_custom_call" | custom-call | tf_op jit(solution)/shard_map/prefix_forward/pallas_call | solution.py:244
  81.0 22.9 %branch.1 = (bf16[4,128,1024]{2,1,0:T(8,128)(2,1)}, f32[4,128,1024]{2,1,0:T(8,128)}, bf16[4,128,1024]{2,1,0:T(8,128)(2,1)}, bf16[4,128,1024]{2,1,0:T(8,128)(2,1)...) custom-call(s32[32]{0:T(128)} %bitcast.47, s32[32]{0:T(128)} %bitcast.46, ...), custom_call_target="tpu_custom_call" | custom-call | tf_op jit(solution)/shard_map/branch/pallas_call | solution.py:244
  103.9 0.0 reduce-scatter.2.cloned.1.call-update
  104.0 13.3 %prefix_backward.1 = (bf16[4,2,128,1024]{3,2,1,0:T(8,128)(2,1)}, bf16[1024,256]{1,0:T(8,128)(2,1)}) custom-call(bf16[4,128,1024]{2,1,0:T(8,128)(2,1)} %get-tuple-element.32.gt, bf16[4,1024,1024]{2,1,0:T(8,128)(2,1)} %get-tuple-element.33.probs, bf16[4,128,1024]{2,1,0:T(8,128)(2,1)} %get-tuple-element.41.glp, bf16[4,128,1024]{2,1,0:T(8,128)(2,1)} %get-tuple-element.42.qlp, ...), custom_call_target="tpu_custom_call" | custom-call | tf_op jit(solution)/shard_map/prefix_backward/pallas_call | solution.py:244
  117.2 3.5 %all-to-all-start.2 = ((bf16[8,128,256]{2,1,0:T(8,128)(2,1)}), bf16[8,128,256]{2,1,0:T(8,128)(2,1)S(1)}, u32[]{:S(2)}, u32[]{:S(2)}) async-start(bf16[8,128,256]{2,1,0:T(8,128)(2,1)} %bitcast.36), calls=%async_computation.3 | async-start | bytes 1048576 | tf_op jit(solution)/shard_map/all_to_all | solution.py:360
  120.7 2.7 %slice_bitcast_fusion = (bf16[2,128,1024]{2,1,0:T(8,128)(2,1)}, bf16[2,128,1024]{2,1,0:T(8,128)(2,1)S(1)}, bf16[2,128,1024]{2,1,0:T(8,128)(2,1)S(1)}, bf16[2,128,1024]{2,1,0:T(8,128)(2,1)}) fusion(bf16[4,2,128,1024]{3,2,1,0:T(8,128)(2,1)} %get-tuple-element.47), kind=kLoop, calls=%fused_computation | loop fusion | bytes 4194304 | tf_op jit(solution)/shard_map/squeeze | solution.py:397
  123.4 0.7 collective-permute-start.10
  124.2 2.9 %collective-permute-start.9 = (bf16[2,128,1024]{2,1,0:T(8,128)(2,1)S(1)}, bf16[2,128,1024]{2,1,0:T(8,128)(2,1)S(1)}, u32[]{:S(2)}, u32[]{:S(2)}) collective-permute-start(bf16[2,128,1024]{2,1,0:T(8,128)(2,1)S(1)} %get-tuple-element.53), channel_id=1, source_target_pairs={{0,16},{8,24},{16,0},{24,8},{1,17},{9,25},{17,1},{25,9},{2,18},{10... | collective-permute-start | bytes 1572872 | tf_op jit(solution)/shard_map/ppermute | solution.py:349
  127.1 0.9 collective-permute-start.8
  127.9 2.2 %all-to-all-done.2 = bf16[8,128,256]{2,1,0:T(8,128)(2,1)S(1)} async-done(((bf16[8,128,256]{2,1,0:T(8,128)(2,1)}), bf16[8,128,256]{2,1,0:T(8,128)(2,1)S(1)}, u32[]{:S(2)}, u32[]{:S(2)}) %all-to-all-start.2) | async-done | bytes 524320 | tf_op jit(solution)/shard_map/all_to_all | solution.py:360
  130.2 0.1 reduce_sum.24
  130.3 16.7 %all_to_all.20 = bf16[8,16,256]{2,1,0:T(8,128)(2,1)S(1)} all-to-all(bf16[8,16,256]{2,1,0:T(8,128)(2,1)S(1)} %bitcast.40), channel_id=1, replica_groups=mesh['x'=4,'core'=2,'y'=4,'z'=8] {'z'}, dimensions={0} | all-to-all | bytes 131072 | tf_op jit(solution)/shard_map/all_to_all | solution.py:360
  147.0 2.7 %collective-permute-start.14 = (bf16[16,128]{1,0:T(8,128)(2,1)S(1)}, bf16[16,128]{1,0:T(8,128)(2,1)S(1)}, u32[]{:S(2)}, u32[]{:S(2)}) collective-permute-start(bf16[16,128]{1,0:T(8,128)(2,1)S(1)} %get-tuple-element.62), channel_id=1, source_target_pairs={{32,0},{96,8},{160,16},{224,24},{40,32},{104,40},{168,48},{232,56}... | collective-permute-start | bytes 12296 | tf_op jit(solution)/shard_map/ppermute | solution.py:393
  149.7 4.5 %collective-permute-start.15 = (bf16[16,128]{1,0:T(8,128)(2,1)S(1)}, bf16[16,128]{1,0:T(8,128)(2,1)S(1)}, u32[]{:S(2)}, u32[]{:S(2)}) collective-permute-start(bf16[16,128]{1,0:T(8,128)(2,1)S(1)} %get-tuple-element.63), channel_id=1, source_target_pairs={{0,0},{64,8},{128,16},{192,24},{8,32},{72,40},{136,48},{200,56},{1... | collective-permute-start | bytes 12296 | tf_op jit(solution)/shard_map/ppermute | solution.py:394
  154.2 0.0 collective-permute-done.10.refs_3_
  154.2 0.0 collective-permute-done.9.refs_2_
  154.2 0.0 collective-permute-done.8.refs_1_
  154.3 0.8 copy-done.1
  155.0 0.2 copy-done.3
  155.2 0.2 copy-done.5
  155.4 2.6 %unpack.2 = (bf16[128,4096]{1,0:T(8,128)(2,1)}, bf16[128,4096]{1,0:T(8,128)(2,1)}) custom-call(bf16[2,128,1024]{2,1,0:T(8,128)(2,1)} %get-tuple-element.55.refs_0_, bf16[2,128,1024]{2,1,0:T(8,128)(2,1)} %copy-done.5, bf16[2,128,1024]{2,1,0:T(8,128)(2,1)} %copy-done.3, bf16[2,128,1024]{2,1,0:T(8,128)(2,1)} %copy-done.1), custom_call_target="tpu_custom_call" | custom-call | tf_op jit(solution)/shard_map/unpack/pallas_call | solution.py:337
  158.0 0.0 collective-permute-done.14
  158.0 0.0 collective-permute-done.15
  158.0 0.0 reduce-scatter.2.cloned.1.call-done
  158.0 1.6 slice_bitcast_fusion.4
  159.6 2.9 %collective-permute-start.13 = (bf16[2,128,128]{2,1,0:T(8,128)(2,1)S(1)}, bf16[2,128,128]{2,1,0:T(8,128)(2,1)S(1)}, u32[]{:S(2)}, u32[]{:S(2)}) collective-permute-start(bf16[2,128,128]{2,1,0:T(8,128)(2,1)S(1)} %get-tuple-element.56), channel_id=1, source_target_pairs={{0,8},{8,16},{16,24},{24,0},{1,9},{9,17},{17,25},{25,1},{2,10},{10... | collective-permute-start | bytes 196616 | tf_op jit(solution)/shard_map/ppermute | solution.py:349
  162.5 2.7 %collective-permute-start.12 = (bf16[2,128,128]{2,1,0:T(8,128)(2,1)S(1)}, bf16[2,128,128]{2,1,0:T(8,128)(2,1)S(1)}, u32[]{:S(2)}, u32[]{:S(2)}) collective-permute-start(bf16[2,128,128]{2,1,0:T(8,128)(2,1)S(1)} %get-tuple-element.57), channel_id=1, source_target_pairs={{0,16},{8,24},{16,0},{24,8},{1,17},{9,25},{17,1},{25,9},{2,18},{10... | collective-permute-start | bytes 196616 | tf_op jit(solution)/shard_map/ppermute | solution.py:349
  165.1 0.6 pad_maximum_fusion.2
  165.7 2.2 %collective-permute-done.12.refs_2_ = bf16[2,128,128]{2,1,0:T(8,128)(2,1)S(1)} collective-permute-done((bf16[2,128,128]{2,1,0:T(8,128)(2,1)S(1)}, bf16[2,128,128]{2,1,0:T(8,128)(2,1)S(1)}, u32[]{:S(2)}, u32[]{:S(2)}) %collective-permute-start.12) | collective-permute-done | bytes 65568 | tf_op jit(solution)/shard_map/ppermute | solution.py:349
  167.9 0.6 collective-permute-done.11.refs_1_
  168.5 0.6 copy-done.9
  169.1 1.6 unpack.3
  (21 shorter events, 0.1 us)
Async XLA Ops:
  7.2 73.8 %all-gather.2.cloned.1.call-start = ((), (), s32[]{:S(2)}) async-start(), calls=%async_computation.5 | async-start | bytes 2359296 | tf_op jit(solution)/shard_map/all_gather | solution.py:381
  8.9 5.8 %collective-permute-start.5 = (bf16[2,128,128]{2,1,0:T(8,128)(2,1)}, bf16[2,128,128]{2,1,0:T(8,128)(2,1)S(1)}, u32[]{:S(2)}, u32[]{:S(2)}) collective-permute-start(bf16[2,128,128]{2,1,0:T(8,128)(2,1)} %get-tuple-element.38), channel_id=1, source_target_pairs={{0,8},{8,16},{16,24},{24,0},{1,9},{9,17},{17,25},{25,1},{2,10},{10... | collective-permute-start | bytes 196616 | tf_op jit(solution)/shard_map/ppermute | solution.py:349
  11.0 5.4 %collective-permute-start.6 = (bf16[2,128,128]{2,1,0:T(8,128)(2,1)}, bf16[2,128,128]{2,1,0:T(8,128)(2,1)S(1)}, u32[]{:S(2)}, u32[]{:S(2)}) collective-permute-start(bf16[2,128,128]{2,1,0:T(8,128)(2,1)} %get-tuple-element.39), channel_id=1, source_target_pairs={{0,16},{8,24},{16,0},{24,8},{1,17},{9,25},{17,1},{25,9},{2,18},{10... | collective-permute-start | bytes 196616 | tf_op jit(solution)/shard_map/ppermute | solution.py:349
  13.7 3.6 %collective-permute-start.7 = (bf16[2,128,128]{2,1,0:T(8,128)(2,1)}, bf16[2,128,128]{2,1,0:T(8,128)(2,1)S(1)}, u32[]{:S(2)}, u32[]{:S(2)}) collective-permute-start(bf16[2,128,128]{2,1,0:T(8,128)(2,1)} %get-tuple-element.40), channel_id=1, source_target_pairs={{0,24},{8,0},{16,8},{24,16},{1,25},{9,1},{17,9},{25,17},{2,26},{10... | collective-permute-start | bytes 196616 | tf_op jit(solution)/shard_map/ppermute | solution.py:349
  19.6 5.0 %collective-permute-start.3 = (bf16[16,128]{1,0:T(8,128)(2,1)S(1)}, bf16[16,128]{1,0:T(8,128)(2,1)S(1)}, u32[]{:S(2)}, u32[]{:S(2)}) collective-permute-start(bf16[16,128]{1,0:T(8,128)(2,1)S(1)} %get-tuple-element.66), channel_id=1, source_target_pairs={{0,32},{8,96},{16,160},{24,224},{32,40},{40,104},{48,168},{56,232}... | collective-permute-start | bytes 12296 | tf_op jit(solution)/shard_map/ppermute | solution.py:377
  19.6 8.4 %collective-permute-start.4 = (bf16[16,128]{1,0:T(8,128)(2,1)S(1)}, bf16[16,128]{1,0:T(8,128)(2,1)S(1)}, u32[]{:S(2)}, u32[]{:S(2)}) collective-permute-start(bf16[16,128]{1,0:T(8,128)(2,1)S(1)} %get-tuple-element.67), channel_id=1, source_target_pairs={{0,0},{8,64},{16,128},{24,192},{32,8},{40,72},{48,136},{56,200},{6... | collective-permute-start | bytes 12296 | tf_op jit(solution)/shard_map/ppermute | solution.py:378
  28.7 17.1 %all-to-all-start = ((bf16[8,16,256]{2,1,0:T(8,128)(2,1)}), bf16[8,16,256]{2,1,0:T(8,128)(2,1)S(1)}, u32[]{:S(2)}, u32[]{:S(2)}) async-start(bf16[8,16,256]{2,1,0:T(8,128)(2,1)} %broadcast_in_dim.15), calls=%async_computation | async-start | bytes 131072 | tf_op jit(solution)/shard_map/all_to_all | solution.py:354
  39.4 16.0 %collective-permute-start = (bf16[2,128,1024]{2,1,0:T(8,128)(2,1)}, bf16[2,128,1024]{2,1,0:T(8,128)(2,1)S(1)}, u32[]{:S(2)}, u32[]{:S(2)}) collective-permute-start(bf16[2,128,1024]{2,1,0:T(8,128)(2,1)} %get-tuple-element.29), channel_id=1, source_target_pairs={{0,8},{8,16},{16,24},{24,0},{1,9},{9,17},{17,25},{25,1},{2,10},{10... | collective-permute-start | bytes 1572872 | tf_op jit(solution)/shard_map/ppermute | solution.py:349
  39.8 27.6 %collective-permute-start.1 = (bf16[2,128,1024]{2,1,0:T(8,128)(2,1)}, bf16[2,128,1024]{2,1,0:T(8,128)(2,1)S(1)}, u32[]{:S(2)}, u32[]{:S(2)}) collective-permute-start(bf16[2,128,1024]{2,1,0:T(8,128)(2,1)} %get-tuple-element.30), channel_id=1, source_target_pairs={{0,16},{8,24},{16,0},{24,8},{1,17},{9,25},{17,1},{25,9},{2,18},{10... | collective-permute-start | bytes 1572872 | tf_op jit(solution)/shard_map/ppermute | solution.py:349
  44.4 23.1 %collective-permute-start.2 = (bf16[2,128,1024]{2,1,0:T(8,128)(2,1)}, bf16[2,128,1024]{2,1,0:T(8,128)(2,1)S(1)}, u32[]{:S(2)}, u32[]{:S(2)}) collective-permute-start(bf16[2,128,1024]{2,1,0:T(8,128)(2,1)} %get-tuple-element.31), channel_id=1, source_target_pairs={{0,24},{8,0},{16,8},{24,16},{1,25},{9,1},{17,9},{25,17},{2,26},{10... | collective-permute-start | bytes 1572872 | tf_op jit(solution)/shard_map/ppermute | solution.py:349
  46.7 20.8 %all-to-all-start.1 = ((bf16[8,128,256]{2,1,0:T(8,128)(2,1)}), bf16[8,128,256]{2,1,0:T(8,128)(2,1)S(1)}, u32[]{:S(2)}, u32[]{:S(2)}) async-start(bf16[8,128,256]{2,1,0:T(8,128)(2,1)} %broadcast_in_dim.16), calls=%async_computation.1 | async-start | bytes 1048576 | tf_op jit(solution)/shard_map/all_to_all | solution.py:354
  54.8 103.2 %reduce-scatter.2.cloned.1.call-start = ((), (), s32[]{:S(2)}) async-start(), calls=%async_computation.6 | async-start | bytes 2359296 | tf_op jit(solution)/shard_map/reduce_scatter | solution.py:387
  55.4 12.0 %copy-start.2 = (bf16[2,128,1024]{2,1,0:T(8,128)(2,1)}, bf16[2,128,1024]{2,1,0:T(8,128)(2,1)S(1)}, u32[]{:S(2)}) copy-start(bf16[2,128,1024]{2,1,0:T(8,128)(2,1)S(1)} %collective-permute-done.qg1) | copy-start | bytes 1572868
  67.4 0.8 copy-start.4
  67.4 1.0 copy-start.6
  67.4 1.2 copy-start
  117.2 12.9 %all-to-all-start.2 = ((bf16[8,128,256]{2,1,0:T(8,128)(2,1)}), bf16[8,128,256]{2,1,0:T(8,128)(2,1)S(1)}, u32[]{:S(2)}, u32[]{:S(2)}) async-start(bf16[8,128,256]{2,1,0:T(8,128)(2,1)} %bitcast.36), calls=%async_computation.3 | async-start | bytes 1048576 | tf_op jit(solution)/shard_map/all_to_all | solution.py:360
  123.4 30.8 %collective-permute-start.10 = (bf16[2,128,1024]{2,1,0:T(8,128)(2,1)}, bf16[2,128,1024]{2,1,0:T(8,128)(2,1)S(1)}, u32[]{:S(2)}, u32[]{:S(2)}) collective-permute-start(bf16[2,128,1024]{2,1,0:T(8,128)(2,1)} %get-tuple-element.52), channel_id=1, source_target_pairs={{0,8},{8,16},{16,24},{24,0},{1,9},{9,17},{17,25},{25,1},{2,10},{10... | collective-permute-start | bytes 1572872 | tf_op jit(solution)/shard_map/ppermute | solution.py:349
  124.2 30.1 %collective-permute-start.9 = (bf16[2,128,1024]{2,1,0:T(8,128)(2,1)S(1)}, bf16[2,128,1024]{2,1,0:T(8,128)(2,1)S(1)}, u32[]{:S(2)}, u32[]{:S(2)}) collective-permute-start(bf16[2,128,1024]{2,1,0:T(8,128)(2,1)S(1)} %get-tuple-element.53), channel_id=1, source_target_pairs={{0,16},{8,24},{16,0},{24,8},{1,17},{9,25},{17,1},{25,9},{2,18},{10... | collective-permute-start | bytes 1572872 | tf_op jit(solution)/shard_map/ppermute | solution.py:349
  127.1 27.2 %collective-permute-start.8 = (bf16[2,128,1024]{2,1,0:T(8,128)(2,1)S(1)}, bf16[2,128,1024]{2,1,0:T(8,128)(2,1)S(1)}, u32[]{:S(2)}, u32[]{:S(2)}) collective-permute-start(bf16[2,128,1024]{2,1,0:T(8,128)(2,1)S(1)} %get-tuple-element.54), channel_id=1, source_target_pairs={{0,24},{8,0},{16,8},{24,16},{1,25},{9,1},{17,9},{25,17},{2,26},{10... | collective-permute-start | bytes 1572872 | tf_op jit(solution)/shard_map/ppermute | solution.py:349
  147.0 11.0 %collective-permute-start.14 = (bf16[16,128]{1,0:T(8,128)(2,1)S(1)}, bf16[16,128]{1,0:T(8,128)(2,1)S(1)}, u32[]{:S(2)}, u32[]{:S(2)}) collective-permute-start(bf16[16,128]{1,0:T(8,128)(2,1)S(1)} %get-tuple-element.62), channel_id=1, source_target_pairs={{32,0},{96,8},{160,16},{224,24},{40,32},{104,40},{168,48},{232,56}... | collective-permute-start | bytes 12296 | tf_op jit(solution)/shard_map/ppermute | solution.py:393
  149.7 8.3 %collective-permute-start.15 = (bf16[16,128]{1,0:T(8,128)(2,1)S(1)}, bf16[16,128]{1,0:T(8,128)(2,1)S(1)}, u32[]{:S(2)}, u32[]{:S(2)}) collective-permute-start(bf16[16,128]{1,0:T(8,128)(2,1)S(1)} %get-tuple-element.63), channel_id=1, source_target_pairs={{0,0},{64,8},{128,16},{192,24},{8,32},{72,40},{136,48},{200,56},{1... | collective-permute-start | bytes 12296 | tf_op jit(solution)/shard_map/ppermute | solution.py:394
  154.2 0.8 copy-start.1
  154.2 1.0 copy-start.3
  154.2 1.1 copy-start.5
  159.6 6.1 %collective-permute-start.13 = (bf16[2,128,128]{2,1,0:T(8,128)(2,1)S(1)}, bf16[2,128,128]{2,1,0:T(8,128)(2,1)S(1)}, u32[]{:S(2)}, u32[]{:S(2)}) collective-permute-start(bf16[2,128,128]{2,1,0:T(8,128)(2,1)S(1)} %get-tuple-element.56), channel_id=1, source_target_pairs={{0,8},{8,16},{16,24},{24,0},{1,9},{9,17},{17,25},{25,1},{2,10},{10... | collective-permute-start | bytes 196616 | tf_op jit(solution)/shard_map/ppermute | solution.py:349
  162.5 5.4 %collective-permute-start.12 = (bf16[2,128,128]{2,1,0:T(8,128)(2,1)S(1)}, bf16[2,128,128]{2,1,0:T(8,128)(2,1)S(1)}, u32[]{:S(2)}, u32[]{:S(2)}) collective-permute-start(bf16[2,128,128]{2,1,0:T(8,128)(2,1)S(1)} %get-tuple-element.57), channel_id=1, source_target_pairs={{0,16},{8,24},{16,0},{24,8},{1,17},{9,25},{17,1},{25,9},{2,18},{10... | collective-permute-start | bytes 196616 | tf_op jit(solution)/shard_map/ppermute | solution.py:349
  165.1 3.4 %collective-permute-start.11 = (bf16[2,128,128]{2,1,0:T(8,128)(2,1)S(1)}, bf16[2,128,128]{2,1,0:T(8,128)(2,1)S(1)}, u32[]{:S(2)}, u32[]{:S(2)}) collective-permute-start(bf16[2,128,128]{2,1,0:T(8,128)(2,1)S(1)} %get-tuple-element.58), channel_id=1, source_target_pairs={{0,24},{8,0},{16,8},{24,16},{1,25},{9,1},{17,9},{25,17},{2,26},{10... | collective-permute-start | bytes 196616 | tf_op jit(solution)/shard_map/ppermute | solution.py:349
  165.7 2.8 %copy-start.7 = (bf16[2,128,128]{2,1,0:T(8,128)(2,1)}, bf16[2,128,128]{2,1,0:T(8,128)(2,1)S(1)}, u32[]{:S(2)}) copy-start(bf16[2,128,128]{2,1,0:T(8,128)(2,1)S(1)} %collective-permute-done.13.refs_3_) | copy-start | bytes 196612
  167.9 0.6 copy-start.8
  168.5 0.6 copy-start.9
Sparse Core Ops, SparseCore 0:
  19.0 42.2 all-gather.1
  104.1 40.4 reduce-scatter.1

commit v3 on v2

v3 whole, which is shorter than its diff:
```python
import jax
import jax.numpy as jnp
from jax import lax
from jax.experimental import pallas as pl
from jax.experimental.pallas import tpu as pltpu
from jax.sharding import Mesh, PartitionSpec as P

HK = 4
HD = 128
GROUP = 8
BLOCK = 128
NB = 32
DEPTH = 8
PREFIX = 1024
NEAR = PREFIX + BLOCK
ROWS = GROUP * BLOCK
CHUNK = 256
TILE = 64
SCALE = HD ** -0.5
SCALE_LOG2E = SCALE * 1.4426950408889634
MASKED = -1e30
F32 = jnp.float32
BF16 = jnp.bfloat16


def dot(a, b):
    return lax.dot_general(a, b, (((1,), (0,)), ((), ())), preferred_element_type=F32)


def dot_t(a, b):
    return lax.dot_general(a, b, (((1,), (1,)), ((), ())), preferred_element_type=F32)


def my_blocks(step):
    ny, nz = lax.axis_size("y"), lax.axis_size("z")
    return lax.rem(lax.axis_index("y") - step + ny, ny) * nz + lax.axis_index("z")


def place_of(block):
    ny, nz = lax.axis_size("y"), lax.axis_size("z")
    return lax.rem(block, nz) * ny + lax.rem(lax.axis_index("y") - block // nz + ny, ny)


def half_moves(first):
    moves = []
    for feature in range(2 * HK):
        half = first if feature >= HK else 1 - first
        for holder in range(HK):
            moves.append((feature * HK + holder, (holder * 2 + half) * HK + feature % HK))
    return moves


def fold(a):
    return a.reshape(a.shape[0] // 8, 8, a.shape[1])


def head_cols(h):
    return slice(h * BLOCK, (h + 1) * BLOCK)


def live_rows(lengths, step):
    return lax.broadcasted_iota(jnp.int32, (HD, BLOCK), 1) < lengths[my_blocks(step)]


NEAR_CHUNKS = [slice(c, min(c + CHUNK, NEAR)) for c in range(0, NEAR, CHUNK)]


def near_kernel(
    lengths, q0, q1, q2, q3, prefix, own,
    qt, probs, out_t, stats, keys, keys_t, values, values_t, scores,
):
    step = pl.program_id(0)

    @pl.when(step == 0)
    def _():
        keys[:PREFIX, :] = prefix[:, :HD]
        values[:PREFIX, :] = prefix[:, HD:]
        keys_t[:, :PREFIX] = prefix[:, :HD].T
        values_t[:, :PREFIX] = prefix[:, HD:].T

    keys[PREFIX:, :] = own[0, 0]
    values[PREFIX:, :] = own[0, 1]
    values_t[:, PREFIX:] = own[0, 1].T

    for d, part in enumerate((q0, q1, q2, q3)):
        @pl.when(step == d)
        def _(part=part):
            for h in range(GROUP):
                cols = head_cols(h)
                qt[0, :, cols] = part[0, :, cols].T

    key_row = lax.broadcasted_iota(jnp.int32, (BLOCK, BLOCK), 0)
    query_row = lax.broadcasted_iota(jnp.int32, (BLOCK, BLOCK), 1)
    seen = (key_row < lengths[my_blocks(step)]) & (key_row <= query_row)
    bias = jnp.where(seen, 0.0, MASKED)
    top = jnp.full((8, ROWS), MASKED, F32)
    for rows in NEAR_CHUNKS:
        s = dot(keys[rows, :], qt[0])
        if rows.start >= PREFIX:
            s = s + jnp.concatenate([bias] * GROUP, axis=1)
        scores[rows, :] = s
        top = jnp.maximum(top, jnp.max(fold(s), axis=0))
    top = jnp.max(top, axis=0, keepdims=True)
    peak = top * SCALE_LOG2E
    total = jnp.zeros((8, ROWS), F32)
    acc = jnp.zeros((HD, ROWS), F32)
    for rows in NEAR_CHUNKS:
        e = jnp.exp2(scores[rows, :] * SCALE_LOG2E - peak)
        total = total + jnp.sum(fold(e), axis=0)
        low = e.astype(BF16)
        probs[0, rows, :] = low
        acc = acc + dot(values_t[:, rows], low)
    out_t[0] = acc
    stats[0, 0:1, :] = top
    stats[0, 1:2, :] = jnp.sum(total, axis=0, keepdims=True)


def branch_kernel(
    parents, lengths, qt, near_out, stats, g0, g1, g2, g3, kv,
    gt, out, dq_part, rows_out, dkv,
    qlt, glt, sk, sv, skt, svt, scores, probs, acc, bias, abk, abv, touched,
):
    step = pl.program_id(0)
    block = my_blocks(step)

    @pl.when(step == 0)
    def _():
        for n in range(NB):
            touched[n] = 0

    row_live = live_rows(lengths, step)
    for d, part in enumerate((g0, g1, g2, g3)):
        @pl.when(step == d)
        def _(part=part):
            for h in range(GROUP):
                cols = head_cols(h)
                gt[0, :, cols] = jnp.where(row_live, part[0, :, cols].astype(F32).T, 0.0).astype(BF16)

    slots, used = [], []
    current = parents[block]
    for k in range(DEPTH):
        in_use = current >= 0
        slot = jnp.where(in_use, current, block)
        slots.append(slot)
        used.append(in_use)
        current = jnp.where(in_use, parents[slot], -1)
    key_row = lax.broadcasted_iota(jnp.int32, (BLOCK, BLOCK), 0)
    pairs = DEPTH // 2
    acc[0:8, :] = jnp.broadcast_to(stats[0, 0:1, :], (8, ROWS))
    for j in range(pairs):
        @pl.when(used[2 * j])
        def _(j=j):
            for k in (2 * j, 2 * j + 1):
                rows = head_cols(k)
                at = place_of(slots[k])
                key = kv[at, 0]
                value = kv[at, 1]
                sk[rows, :] = key
                sv[rows, :] = value
                skt[:, rows] = key.T
                svt[:, rows] = value.T
                seen = key_row < jnp.where(used[k], lengths[slots[k]], 0)
                bias[rows, :] = jnp.where(seen, 0.0, MASKED)
            rows = slice(j * CHUNK, (j + 1) * CHUNK)
            s = dot(sk[rows, :], qt[0])
            s = s + jnp.concatenate([bias[rows, :]] * GROUP, axis=1)
            scores[rows, :] = s
            acc[0:8, :] = jnp.maximum(acc[0:8, :], jnp.max(fold(s), axis=0))
    peak = jnp.max(acc[0:8, :], axis=0, keepdims=True) * SCALE_LOG2E

    acc[...] = jnp.zeros_like(acc)
    for j in range(pairs):
        @pl.when(used[2 * j])
        def _(j=j):
            rows = slice(j * CHUNK, (j + 1) * CHUNK)
            e = jnp.exp2(scores[rows, :] * SCALE_LOG2E - peak)
            acc[HD:HD + 8, :] += jnp.sum(fold(e), axis=0)
            low = e.astype(BF16)
            probs[rows, :] = low
            acc[0:HD, :] += dot(svt[:, rows], low)

    alpha = jnp.exp2(stats[0, 0:1, :] * SCALE_LOG2E - peak)
    total = alpha * stats[0, 1:2, :] + jnp.sum(acc[HD:HD + 8, :], axis=0, keepdims=True)
    inverse = 1.0 / total
    near_inverse = alpha * inverse
    out_t = (acc[0:HD, :] * inverse + near_out[0] * near_inverse).astype(BF16)
    grad_t = gt[0].astype(F32)
    delta = jnp.sum(grad_t * out_t.astype(F32), axis=0, keepdims=True)
    glt[...] = (grad_t * inverse).astype(BF16)
    qlt[...] = (qt[0].astype(F32) * (inverse * SCALE)).astype(BF16)
    rows_out[0, 0:1, :] = delta
    rows_out[0, 1:2, :] = near_inverse
    out[0] = out_t

    acc[0:HD, :] = jnp.zeros((HD, ROWS), F32)
    for j in range(pairs):
        @pl.when(used[2 * j])
        def _(j=j):
            rows = slice(j * CHUNK, (j + 1) * CHUNK)
            low = probs[rows, :]
            ds = (low.astype(F32) * (dot(sv[rows, :], gt[0]) - delta)).astype(BF16)
            dv = dot_t(low, glt[...])
            dk = dot_t(ds, qlt[...])
            for k in range(2):
                at = place_of(slots[2 * j + k])
                had = touched[at] > 0
                abv[at] = jnp.where(had, abv[at], 0.0) + dv[k * BLOCK:(k + 1) * BLOCK]
                abk[at] = jnp.where(had, abk[at], 0.0) + dk[k * BLOCK:(k + 1) * BLOCK]
                touched[at] = 1
            acc[0:HD, :] += dot(skt[:, rows], ds)
    dq_part[0] = acc[0:HD, :] * (inverse * SCALE)

    @pl.when(step == pl.num_programs(0) - 1)
    def _():
        for n in range(NB):
            @pl.when(touched[n] > 0)
            def _(n=n):
                dkv[n, 0] = abk[n].astype(BF16)
                dkv[n, 1] = abv[n].astype(BF16)

            @pl.when(touched[n] == 0)
            def _(n=n):
                dkv[n] = jnp.zeros((2, BLOCK, HD), BF16)


def near_back_kernel(
    lengths, qt, gt, probs, rows_in, dq_part, out, prefix, own,
    both, d_own, dp, keys_t, values, apk, apv, qln, gln,
):
    step = pl.program_id(0)

    @pl.when(step == 0)
    def _():
        keys_t[:, :PREFIX] = prefix[:, :HD].T
        values[:PREFIX, :] = prefix[:, HD:]
        apk[...] = jnp.zeros_like(apk)
        apv[...] = jnp.zeros_like(apv)

    keys_t[:, PREFIX:] = own[0, 0].T
    values[PREFIX:, :] = own[0, 1]
    delta = rows_in[0, 0:1, :]
    inverse = rows_in[0, 1:2, :]
    gln[...] = (gt[0].astype(F32) * inverse).astype(BF16)
    qln[...] = (qt[0].astype(F32) * (inverse * SCALE)).astype(BF16)
    acc = jnp.zeros((HD, ROWS), F32)
    for rows in NEAR_CHUNKS:
        low = probs[0, rows, :]
        ds = (low.astype(F32) * (dot(values[rows, :], gt[0]) - delta)).astype(BF16)
        dv = dot_t(low, gln[...])
        dk = dot_t(ds, qln[...])
        if rows.start >= PREFIX:
            d_own[0, 0] = dk
            d_own[0, 1] = dv
        else:
            apk[rows, :] += dk
            apv[rows, :] += dv
        acc = acc + dot(keys_t[:, rows], ds)
    dq_t = acc * (inverse * SCALE) + dq_part[0]
    row_live = live_rows(lengths, step)
    for h in range(GROUP):
        cols = head_cols(h)
        both[0, 0, :, cols] = jnp.where(row_live, out[0, :, cols].astype(F32), 0.0).T.astype(BF16)
        both[0, 1, :, cols] = dq_t[:, cols].T.astype(BF16)

    @pl.when(step == pl.num_programs(0) - 1)
    def _():
        dp[:, :HD] = apk[...].astype(BF16)
        dp[:, HD:] = apv[...].astype(BF16)


def whole(shape):
    return pl.BlockSpec(shape, lambda i, *_: (0,) * len(shape))


def stepped(shape):
    return pl.BlockSpec((1, *shape[1:]), lambda i, *_: (i,) + (0,) * (len(shape) - 1))


def call(body, name, scalars, steps, args, outs, scratch, more=[]):
    spec = lambda shape, by_step: stepped(shape) if by_step else whole(shape)
    return pl.pallas_call(
        body,
        grid_spec=pltpu.PrefetchScalarGridSpec(
            num_scalar_prefetch=len(scalars),
            grid=(steps,),
            in_specs=[spec(a.shape, by_step) for a, by_step in args],
            out_specs=[spec(shape, by_step) for shape, _, by_step in outs],
            scratch_shapes=[pltpu.VMEM(shape, dtype) for shape, dtype in scratch] + more,
        ),
        out_shape=[jax.ShapeDtypeStruct(shape, dtype) for shape, dtype, _ in outs],
        compiler_params=pltpu.CompilerParams(vmem_limit_bytes=60 * 1024 * 1024),
        name=name,
    )(*scalars, *[a for a, _ in args])


def near_forward(lengths, q, prefix, own):
    n = len(q)
    tall, rows = (n, HD, ROWS), (n, 8, ROWS)
    return call(
        near_kernel, "near_forward", [lengths], n,
        [(a, False) for a in (*q, prefix)] + [(own, True)],
        [(tall, BF16, True), ((n, NEAR, ROWS), BF16, True), (tall, F32, True), (rows, F32, True)],
        [((NEAR, HD), BF16), ((HD, NEAR), BF16), ((NEAR, HD), BF16), ((HD, NEAR), BF16), ((NEAR, ROWS), F32)],
    )


def branch(parents, lengths, qt, near_out, stats, g, kv):
    n = qt.shape[0]
    tall, rows, keys = (n, HD, ROWS), (n, 8, ROWS), DEPTH * BLOCK
    return call(
        branch_kernel, "branch", [parents, lengths], n,
        [(qt, True), (near_out, True), (stats, True)] + [(a, False) for a in (*g, kv)],
        [(tall, BF16, True), (tall, BF16, True), (tall, F32, True), (rows, F32, True), (kv.shape, BF16, False)],
        [((HD, ROWS), BF16), ((HD, ROWS), BF16), ((keys, HD), BF16), ((keys, HD), BF16),
         ((HD, keys), BF16), ((HD, keys), BF16), ((keys, ROWS), F32), ((keys, ROWS), BF16),
         ((HD + 8, ROWS), F32), ((keys, BLOCK), F32), ((NB, BLOCK, HD), F32), ((NB, BLOCK, HD), F32)],
        [pltpu.SMEM((NB,), jnp.int32)],
    )


def near_backward(lengths, qt, gt, probs, rows_in, dq_part, out, prefix, own):
    n = gt.shape[0]
    return call(
        near_back_kernel, "near_backward", [lengths], n,
        [(a, True) for a in (qt, gt, probs, rows_in, dq_part, out)] + [(prefix, False), (own, True)],
        [((n, 2, BLOCK, ROWS), BF16, True), (own.shape, F32, True), (prefix.shape, BF16, False)],
        [((HD, NEAR), BF16), ((NEAR, HD), BF16), ((PREFIX, HD), F32), ((PREFIX, HD), F32),
         ((HD, ROWS), BF16), ((HD, ROWS), BF16)],
    )


def head_at(d):
    return lax.rem(lax.axis_index("y") + d, HK)


def pack_kernel(source, *targets):
    for d, target in enumerate(targets):
        parts, _, width = target.shape
        for part in range(parts):
            cols = pl.ds(pl.multiple_of((part * HK + head_at(d)) * width, 128), width)
            target[part] = source[:, cols]


def pack(source, parts):
    rows, columns = source.shape
    width = columns // (HK * parts)
    return pl.pallas_call(
        pack_kernel,
        grid=(rows // TILE,),
        in_specs=[pl.BlockSpec((TILE, columns), lambda i: (i, 0))],
        out_specs=[pl.BlockSpec((parts, TILE, width), lambda i: (0, i, 0))] * HK,
        out_shape=[jax.ShapeDtypeStruct((parts, rows, width), BF16)] * HK,
        name="pack",
    )(source)


def unpack_kernel(sources, targets):
    for d, source in enumerate(sources):
        for part in range(2):
            width = source.shape[2]
            target = targets[part % len(targets)]
            first = 0 if len(targets) > 1 else part * HK * width
            cols = pl.ds(pl.multiple_of(first + head_at(d) * width, 128), width)
            target[:, cols] = source[part]


def unpack(sources, count):
    _, rows, width = sources[0].shape
    tile, n = min(rows, TILE), len(sources)
    columns = 2 * HK * width // count
    return pl.pallas_call(
        lambda *refs: unpack_kernel(refs[:n], refs[n:]),
        grid=(rows // tile,),
        in_specs=[pl.BlockSpec((2, tile, width), lambda i: (0, i, 0))] * n,
        out_specs=[pl.BlockSpec((tile, columns), lambda i: (i, 0))] * count,
        out_shape=[jax.ShapeDtypeStruct((rows, columns), BF16)] * count,
        name="unpack",
    )(*sources)


def shift(x, axis, by):
    n = lax.axis_size(axis)
    return lax.ppermute(x, axis, [(i, (i + by) % n) for i in range(n)])


def spread(x, axes):
    n = lax.axis_size(axes)
    return lax.all_to_all(jnp.broadcast_to(x, (n, *x.shape)), axes, split_axis=0, concat_axis=0, tiled=True)


def gather_terms(x, axes):
    n = lax.axis_size(axes)
    x = x.reshape(n, x.shape[0] // n, x.shape[1])
    return jnp.sum(lax.all_to_all(x, axes, split_axis=0, concat_axis=0, tiled=True).astype(F32), axis=0).astype(BF16)


def per_device(query, d_out, branch_kv, prefix_kv, parents, lengths):
    ny, nz = lax.axis_size("y"), lax.axis_size("z")

    def exchange(parts):
        return [parts[0]] + [shift(parts[d], "y", d) for d in range(1, ny)]

    def back(parts):
        return [parts[0]] + [shift(parts[d], "y", -d) for d in range(1, ny)]

    kv = exchange(pack(branch_kv[0], 2))
    q = pack(query[0], 1)
    kv, q, d_out = lax.optimization_barrier((kv, q, d_out))
    q = exchange(q)
    ring, smp = ("x", "core", "y"), ("x", "core")
    half_rows = prefix_kv.shape[0] // 2
    value_holder = lax.axis_index("x") >= 2
    low, high = prefix_kv[:half_rows], prefix_kv[half_rows:]
    one = lax.ppermute(jnp.where(value_holder, low, high), ring, half_moves(0))
    two = lax.ppermute(jnp.where(value_holder, high, low), ring, half_moves(1))
    odd = lax.axis_index("core") == 1
    mine = jnp.concatenate([jnp.where(odd, one, two), jnp.where(odd, two, one)], axis=1)
    own = jnp.stack(kv)
    kv = lax.all_gather(own, "z", axis=0, tiled=True)
    g = exchange(pack(d_out[0], 1))
    prefix = spread(mine, "z").reshape(-1, 2 * HD)
    prefix, q = lax.optimization_barrier((prefix, q))
    prefix = spread(prefix, smp).reshape(PREFIX, 2 * HD)

    qt, probs, near_out, stats = near_forward(lengths[0], q, prefix, own)
    gt, out, dq_part, rows, dkv = branch(parents[0], lengths[0], qt, near_out, stats, g, kv)
    dkv = lax.psum_scatter(dkv, "z", scatter_dimension=0, tiled=True)
    od, d_own, dp = near_backward(lengths[0], qt, gt, probs, rows, dq_part, out, prefix, own)

    mine = gather_terms(gather_terms(dp, smp), "z")
    key, value = mine[:, :HD], mine[:, HD:]
    returns = lambda first: [(b, a) for a, b in half_moves(first)]
    one = lax.ppermute(jnp.where(odd, key, value), ring, returns(0))
    two = lax.ppermute(jnp.where(odd, value, key), ring, returns(1))
    d_prefix = jnp.concatenate(
        [jnp.where(value_holder, one, two), jnp.where(value_holder, two, one)], axis=0)
    out, dq = unpack(back([od[d] for d in range(ny)]), 2)
    dkv = (dkv.astype(F32) + d_own).astype(BF16)
    d_branch, = unpack(back([dkv[d] for d in range(ny)]), 1)
    return out[None], dq[None], d_branch[None], d_prefix


def solution(mesh):
    devices = mesh.devices.reshape(4, 2, 4, 8)
    split = Mesh(devices, ("x", "core", "y", "z"))
    smp, ctx = ("x", "core"), ("y", "z")
    return jax.shard_map(
        per_device,
        mesh=split,
        in_specs=(
            P(smp, ctx, None), P(smp, ctx, None), P(smp, ctx, None),
            P(ctx, smp), P(smp, None), P(smp, None),
        ),
        out_specs=(P(smp, ctx, None), P(smp, ctx, None), P(smp, ctx, None), P(ctx, smp)),
        check_vma=False,
    )
```

time: 179 us -> 172 us (0.961)
  blocking collectives: 16.7 us -> 34 us
  waiting for transfers between devices: 23.7 us -> 9.84 us
  starting transfers between devices: 54.1 us -> 50 us
  Pallas kernels: 57 us -> 53.1 us
    all_to_all x0 -> x1, blocking collectives: none -> 15.9 us  [spread(): lax.all_to_all(jnp.broadcast_to(x, (n, *x.shape)), axes, split_axis=0, co...]
    ppermute x12 -> x15, waiting for transfers between devices: 18 us -> 3.89 us  [shift(): return lax.ppermute(x, axis, [(i, (i + by) % n) for i in range(n)])]
    all_to_all x2 -> x1, starting transfers between devices: 16.3 us -> 5.78 us  [spread(): lax.all_to_all(jnp.broadcast_to(x, (n, *x.shape)), axes, split_axis=0, co...]
    pallas_call x3, Pallas kernels: 48.6 us -> 43.1 us  [call(): pl.pallas_call(body, grid_spec=pltpu.PrefetchScalarGridSpec(num_scalar_pr...]
    ppermute x12 -> x15, starting transfers between devices: 22.2 us -> 27.5 us  [shift(): return lax.ppermute(x, axis, [(i, (i + by) % n) for i in range(n)])]
    all_to_all x2 -> x1, waiting for transfers between devices: 0.01 us -> 3.63 us  [spread(): lax.all_to_all(jnp.broadcast_to(x, (n, *x.shape)), axes, split_axis=0, co...]
    ppermute x1, waiting for transfers between devices: 3.46 us -> 0.01 us  [per_device(): two = lax.ppermute(jnp.where(value_holder, high, low), ring, half_moves(1))]
    all_to_all x1, starting transfers between devices: 3.46 us -> 5.56 us  [gather_terms(): lax.all_to_all(x, axes, split_axis=0, concat_axis=0, tiled=True).astype(F32)]
  transfers between devices with their start and end apart: 21 -> 23, of which waited for: 8 -> 5; matrix products, arithmetic and copies ran while one was open for 3% -> 3% of each run, Pallas kernels for 17% -> 21%
where the time goes in v3:
time: 172 us
  Pallas kernels  53.1 us (31%)
  starting transfers between devices  50 us (29%)
  blocking collectives  34 us (20%)
  between operations  14.3 us (8%)
  waiting for transfers between devices  9.84 us (6%)
  local copies, waits for them, and re-layouts  7.58 us (4%)
  other arithmetic  3.31 us (2%)
    pallas_call x3, Pallas kernels, call(): pl.pallas_call(body, grid_spec=pltpu.PrefetchScalarGridSpec(num_scalar_pr...  43.1 us
    ppermute x15, starting transfers between devices, shift(): return lax.ppermute(x, axis, [(i, (i + by) % n) for i in range(n)])  27.5 us
    all_to_all x1, blocking collectives, gather_terms(): lax.all_to_all(x, axes, split_axis=0, concat_axis=0, tiled=True).astype(F32)  18.1 us
    all_to_all x1, blocking collectives, spread(): lax.all_to_all(jnp.broadcast_to(x, (n, *x.shape)), axes, split_axis=0, co...  15.9 us
    pallas_call x3, Pallas kernels, pack(): pl.pallas_call(pack_kernel, grid=(rows // TILE,), in_specs=[pl.BlockSpec(...  5.82 us
    all_to_all x1, starting transfers between devices, spread(): lax.all_to_all(jnp.broadcast_to(x, (n, *x.shape)), axes, split_axis=0, co...  5.78 us
    all_to_all x1, starting transfers between devices, gather_terms(): lax.all_to_all(x, axes, split_axis=0, concat_axis=0, tiled=True).astype(F32)  5.56 us
    ppermute x1, starting transfers between devices, per_device(): two = lax.ppermute(jnp.where(value_holder, high, low), ring, half_moves(1))  4.96 us
  transfers between devices with their start and end apart: 23, of which 5 were waited for; matrix products, arithmetic and copies ran while one was open for 3% of the time, Pallas kernels for 21%

profile of v3, /device:TPU:1, one launch (start us, length us, event | category | flops | bytes accessed | tf_op | source)
XLA Modules:
  0.0 172.1 jit_solution(14445903054582194601)
XLA Ops:
  7.2 0.0 all-gather.2.cloned.1.call-start
  7.2 1.7 pack.3
  8.9 2.1 %collective-permute-start.2 = (bf16[2,128,128]{2,1,0:T(8,128)(2,1)}, bf16[2,128,128]{2,1,0:T(8,128)(2,1)S(1)}, u32[]{:S(2)}, u32[]{:S(2)}) collective-permute-start(bf16[2,128,128]{2,1,0:T(8,128)(2,1)} %get-tuple-element.45), channel_id=1, source_target_pairs={{0,8},{8,16},{16,24},{24,0},{1,9},{9,17},{17,25},{25,1},{2,10},{10... | collective-permute-start | bytes 196616 | tf_op jit(solution)/shard_map/ppermute | solution.py:383
  11.1 2.6 %collective-permute-start.3 = (bf16[2,128,128]{2,1,0:T(8,128)(2,1)}, bf16[2,128,128]{2,1,0:T(8,128)(2,1)S(1)}, u32[]{:S(2)}, u32[]{:S(2)}) collective-permute-start(bf16[2,128,128]{2,1,0:T(8,128)(2,1)} %get-tuple-element.46), channel_id=1, source_target_pairs={{0,16},{8,24},{16,0},{24,8},{1,17},{9,25},{17,1},{25,9},{2,18},{10... | collective-permute-start | bytes 196616 | tf_op jit(solution)/shard_map/ppermute | solution.py:383
  13.7 1.1 collective-permute-start.4
  14.7 2.0 %pack.4 = (bf16[1,128,1024]{2,1,0:T(8,128)(2,1)}, bf16[1,128,1024]{2,1,0:T(8,128)(2,1)}, bf16[1,128,1024]{2,1,0:T(8,128)(2,1)}, bf16[1,128,1024]{2,1,0:T(8,128)(2,1)}) custom-call(bf16[128,4096]{1,0:T(8,128)(2,1)} %bitcast.34), custom_call_target="tpu_custom_call" | custom-call | tf_op jit(solution)/shard_map/pack/pallas_call | solution.py:347
  16.8 0.0 collective-permute-done.2
  16.8 0.0 collective-permute-done.3
  16.8 0.5 collective-permute-done.4
  17.3 1.6 pad_maximum_fusion.own
  18.9 0.0 all-gather.2.cloned.1.call-update
  18.9 0.1 collective-permute-start
  19.0 5.0 %collective-permute-start.1 = (bf16[16,128]{1,0:T(8,128)(2,1)S(1)}, bf16[16,128]{1,0:T(8,128)(2,1)S(1)}, u32[]{:S(2)}, u32[]{:S(2)}) collective-permute-start(bf16[16,128]{1,0:T(8,128)(2,1)S(1)} %get-tuple-element.99), channel_id=1, source_target_pairs={{0,0},{8,64},{16,128},{24,192},{32,8},{40,72},{48,136},{56,200},{6... | collective-permute-start | bytes 12296 | tf_op jit(solution)/shard_map/ppermute | solution.py:415
  24.0 0.3 collective-permute-start.5
  24.3 6.5 %collective-permute-start.6 = (bf16[1,128,1024]{2,1,0:T(8,128)(2,1)}, bf16[1,128,1024]{2,1,0:T(8,128)(2,1)S(1)}, u32[]{:S(2)}, u32[]{:S(2)}) collective-permute-start(bf16[1,128,1024]{2,1,0:T(8,128)(2,1)} %get-tuple-element.54), channel_id=1, source_target_pairs={{0,16},{8,24},{16,0},{24,8},{1,17},{9,25},{17,1},{25,9},{2,18},{10... | collective-permute-start | bytes 786440 | tf_op jit(solution)/shard_map/ppermute | solution.py:383
  30.8 0.2 collective-permute-start.7
  31.0 0.0 collective-permute-done.1
  31.1 15.9 %all_to_all.20 = bf16[8,16,256]{2,1,0:T(8,128)(2,1)S(1)} all-to-all(bf16[8,16,256]{2,1,0:T(8,128)(2,1)S(1)} %broadcast_in_dim.15), channel_id=1, replica_groups=mesh['x'=4,'core'=2,'y'=4,'z'=8] {'z'}, dimensions={0} | all-to-all | bytes 131072 | tf_op jit(solution)/shard_map/all_to_all | solution.py:388
  47.0 0.0 copy-start.6
  47.0 0.0 collective-permute-done.7.q3
  47.0 0.9 broadcast_in_dim.16
  47.9 5.8 %all-to-all-start.1 = ((bf16[8,128,256]{2,1,0:T(8,128)(2,1)}), bf16[8,128,256]{2,1,0:T(8,128)(2,1)S(1)}, u32[]{:S(2)}, u32[]{:S(2)}) async-start(bf16[8,128,256]{2,1,0:T(8,128)(2,1)} %broadcast_in_dim.16), calls=%async_computation.1 | async-start | bytes 1048576 | tf_op jit(solution)/shard_map/all_to_all | solution.py:388
  53.7 2.1 %pack.5 = (bf16[1,128,1024]{2,1,0:T(8,128)(2,1)}, bf16[1,128,1024]{2,1,0:T(8,128)(2,1)}, bf16[1,128,1024]{2,1,0:T(8,128)(2,1)}, bf16[1,128,1024]{2,1,0:T(8,128)(2,1)}) custom-call(bf16[128,4096]{1,0:T(8,128)(2,1)} %bitcast.35), custom_call_target="tpu_custom_call" | custom-call | tf_op jit(solution)/shard_map/pack/pallas_call | solution.py:347
  55.8 1.3 collective-permute-start.8
  57.1 2.5 %collective-permute-start.10 = (bf16[1,128,1024]{2,1,0:T(8,128)(2,1)}, bf16[1,128,1024]{2,1,0:T(8,128)(2,1)S(1)}, u32[]{:S(2)}, u32[]{:S(2)}) collective-permute-start(bf16[1,128,1024]{2,1,0:T(8,128)(2,1)} %get-tuple-element.72), channel_id=1, source_target_pairs={{0,24},{8,0},{16,8},{24,16},{1,25},{9,1},{17,9},{25,17},{2,26},{10... | collective-permute-start | bytes 786440 | tf_op jit(solution)/shard_map/ppermute | solution.py:383
  59.5 3.6 %all-to-all-done.1 = bf16[8,128,256]{2,1,0:T(8,128)(2,1)S(1)} async-done(((bf16[8,128,256]{2,1,0:T(8,128)(2,1)}), bf16[8,128,256]{2,1,0:T(8,128)(2,1)S(1)}, u32[]{:S(2)}, u32[]{:S(2)}) %all-to-all-start.1) | async-done | bytes 524320 | tf_op jit(solution)/shard_map/all_to_all | solution.py:388
  63.2 0.8 copy-done
  64.0 14.4 %near_forward.1 = (bf16[4,128,1024]{2,1,0:T(8,128)(2,1)}, bf16[4,1152,1024]{2,1,0:T(8,128)(2,1)}, f32[4,128,1024]{2,1,0:T(8,128)}, f32[4,8,1024]{2,1,0:T(8,128)}) custom-call(s32[32]{0:T(128)} %bitcast.45, bf16[1,128,1024]{2,1,0:T(8,128)(2,1)} %get-tuple-element.56.q0, bf16[1,128,1024]{2,1,0:T(8,128)(2,1)} %copy-done.5, bf16[1,128,1024]{2,1,0:T(8,128)(2,1)} %copy-done.6, ...), custom_call_target="tpu_custom_call" | custom-call | tf_op jit(solution)/shard_map/near_forward/pallas_call | solution.py:281
  78.4 0.0 collective-permute-done.8.g1
  78.4 0.0 copy-start.8
  78.4 0.0 collective-permute-done.9.g2
  78.5 0.0 all-gather.2.cloned.1.call-done.kv
  78.5 0.6 copy-done.8
  79.1 0.1 copy-done.9
  79.2 0.1 copy-done.10
  79.3 14.2 %branch.1 = (bf16[4,128,1024]{2,1,0:T(8,128)(2,1)}, bf16[4,128,1024]{2,1,0:T(8,128)(2,1)}, f32[4,128,1024]{2,1,0:T(8,128)}, f32[4,8,1024]{2,1,0:T(8,128)}, bf16[32,2,128,128]{3,2,1,0:T(8,128)(2,1)}) custom-call(s32[32]{0:T(128)} %bitcast.48, s32[32]{0:T(128)} %bitcast.46, bf16[4,128,1024]{2,1,0:T(8,128)(2,1)} %get-tuple-element.65.qt, ...), custom_call_target="tpu_custom_call" | custom-call | tf_op jit(solution)/shard_map/branch/pallas_call | solution.py:281
  93.5 0.0 reduce-scatter.2.cloned.1.call-update
  93.5 14.5 %near_backward.1 = (bf16[4,2,128,1024]{3,2,1,0:T(8,128)(2,1)}, f32[4,2,128,128]{3,2,1,0:T(8,128)}, bf16[1024,256]{1,0:T(8,128)(2,1)}) custom-call(s32[32]{0:T(128)} %bitcast.47, bf16[4,128,1024]{2,1,0:T(8,128)(2,1)} %get-tuple-element.65.qt, bf16[4,128,1024]{2,1,0:T(8,128)(2,1)} %get-tuple-element.73.gt, bf16[4,1152,1024]{2,1,0:T(8,128)(2,1)} %get-tuple-element.74.probs, ...), custom_call_target="tpu_custom_call" | custom-call | tf_op jit(solution)/shard_map/near_backward/pallas_call | solution.py:281
  108.0 5.6 %all-to-all-start.2 = ((bf16[8,128,256]{2,1,0:T(8,128)(2,1)}), bf16[8,128,256]{2,1,0:T(8,128)(2,1)S(1)}, u32[]{:S(2)}, u32[]{:S(2)}) async-start(bf16[8,128,256]{2,1,0:T(8,128)(2,1)} %bitcast.36), calls=%async_computation.3 | async-start | bytes 1048576 | tf_op jit(solution)/shard_map/all_to_all | solution.py:394
  113.6 2.7 %slice_bitcast_fusion = (bf16[2,128,1024]{2,1,0:T(8,128)(2,1)}, bf16[2,128,1024]{2,1,0:T(8,128)(2,1)}, bf16[2,128,1024]{2,1,0:T(8,128)(2,1)S(1)}, bf16[2,128,1024]{2,1,0:T(8,128)(2,1)}) fusion(bf16[4,2,128,1024]{3,2,1,0:T(8,128)(2,1)} %get-tuple-element.78), kind=kLoop, calls=%fused_computation.1 | loop fusion | bytes 4194304 | tf_op jit(solution)/shard_map/squeeze | solution.py:437
  116.2 2.1 %collective-permute-start.13 = (bf16[2,128,1024]{2,1,0:T(8,128)(2,1)}, bf16[2,128,1024]{2,1,0:T(8,128)(2,1)S(1)}, u32[]{:S(2)}, u32[]{:S(2)}) collective-permute-start(bf16[2,128,1024]{2,1,0:T(8,128)(2,1)} %get-tuple-element.84), channel_id=1, source_target_pairs={{0,8},{8,16},{16,24},{24,0},{1,9},{9,17},{17,25},{25,1},{2,10},{10... | collective-permute-start | bytes 1572872 | tf_op jit(solution)/shard_map/ppermute | solution.py:383
  118.3 0.0 collective-permute-start.12
  118.3 2.5 %collective-permute-start.11 = (bf16[2,128,1024]{2,1,0:T(8,128)(2,1)S(1)}, bf16[2,128,1024]{2,1,0:T(8,128)(2,1)S(1)}, u32[]{:S(2)}, u32[]{:S(2)}) collective-permute-start(bf16[2,128,1024]{2,1,0:T(8,128)(2,1)S(1)} %get-tuple-element.86), channel_id=1, source_target_pairs={{0,24},{8,0},{16,8},{24,16},{1,25},{9,1},{17,9},{25,17},{2,26},{10... | collective-permute-start | bytes 1572872 | tf_op jit(solution)/shard_map/ppermute | solution.py:383
  120.8 2.2 %all-to-all-done.2 = bf16[8,128,256]{2,1,0:T(8,128)(2,1)S(1)} async-done(((bf16[8,128,256]{2,1,0:T(8,128)(2,1)}), bf16[8,128,256]{2,1,0:T(8,128)(2,1)S(1)}, u32[]{:S(2)}, u32[]{:S(2)}) %all-to-all-start.2) | async-done | bytes 524320 | tf_op jit(solution)/shard_map/all_to_all | solution.py:394
  123.1 0.1 reduce_sum.24
  123.1 18.1 %all_to_all.21 = bf16[8,16,256]{2,1,0:T(8,128)(2,1)S(1)} all-to-all(bf16[8,16,256]{2,1,0:T(8,128)(2,1)S(1)} %bitcast.40), channel_id=1, replica_groups=mesh['x'=4,'core'=2,'y'=4,'z'=8] {'z'}, dimensions={0} | all-to-all | bytes 131072 | tf_op jit(solution)/shard_map/all_to_all | solution.py:394
  141.3 2.6 %collective-permute-start.17 = (bf16[16,128]{1,0:T(8,128)(2,1)S(1)}, bf16[16,128]{1,0:T(8,128)(2,1)S(1)}, u32[]{:S(2)}, u32[]{:S(2)}) collective-permute-start(bf16[16,128]{1,0:T(8,128)(2,1)S(1)} %get-tuple-element.94), channel_id=1, source_target_pairs={{32,0},{96,8},{160,16},{224,24},{40,32},{104,40},{168,48},{232,56}... | collective-permute-start | bytes 12296 | tf_op jit(solution)/shard_map/ppermute | solution.py:433
  143.8 3.5 %collective-permute-start.18 = (bf16[16,128]{1,0:T(8,128)(2,1)S(1)}, bf16[16,128]{1,0:T(8,128)(2,1)S(1)}, u32[]{:S(2)}, u32[]{:S(2)}) collective-permute-start(bf16[16,128]{1,0:T(8,128)(2,1)S(1)} %get-tuple-element.95), channel_id=1, source_target_pairs={{0,0},{64,8},{128,16},{192,24},{8,32},{72,40},{136,48},{200,56},{1... | collective-permute-start | bytes 12296 | tf_op jit(solution)/shard_map/ppermute | solution.py:434
  147.3 0.0 collective-permute-done.13.refs_3_
  147.4 0.8 copy-done.2
  148.1 0.2 copy-done.3
  148.3 0.2 copy-done.4
  148.4 2.6 %unpack.2 = (bf16[128,4096]{1,0:T(8,128)(2,1)}, bf16[128,4096]{1,0:T(8,128)(2,1)}) custom-call(bf16[2,128,1024]{2,1,0:T(8,128)(2,1)} %get-tuple-element.87.refs_0_, bf16[2,128,1024]{2,1,0:T(8,128)(2,1)} %copy-done.4, bf16[2,128,1024]{2,1,0:T(8,128)(2,1)} %copy-done.3, bf16[2,128,1024]{2,1,0:T(8,128)(2,1)} %copy-done.2), custom_call_target="tpu_custom_call" | custom-call | tf_op jit(solution)/shard_map/unpack/pallas_call | solution.py:371
  151.1 0.0 reduce-scatter.2.cloned.1.call-done
  151.1 1.0 add_convert_fusion
  152.1 0.6 slice_bitcast_fusion.4
  152.7 3.0 %collective-permute-start.16 = (bf16[2,128,128]{2,1,0:T(8,128)(2,1)S(1)}, bf16[2,128,128]{2,1,0:T(8,128)(2,1)S(1)}, u32[]{:S(2)}, u32[]{:S(2)}) collective-permute-start(bf16[2,128,128]{2,1,0:T(8,128)(2,1)S(1)} %get-tuple-element.88), channel_id=1, source_target_pairs={{0,8},{8,16},{16,24},{24,0},{1,9},{9,17},{17,25},{25,1},{2,10},{10... | collective-permute-start | bytes 196616 | tf_op jit(solution)/shard_map/ppermute | solution.py:383
  155.7 3.4 %collective-permute-start.15 = (bf16[2,128,128]{2,1,0:T(8,128)(2,1)S(1)}, bf16[2,128,128]{2,1,0:T(8,128)(2,1)S(1)}, u32[]{:S(2)}, u32[]{:S(2)}) collective-permute-start(bf16[2,128,128]{2,1,0:T(8,128)(2,1)S(1)} %get-tuple-element.89), channel_id=1, source_target_pairs={{0,16},{8,24},{16,0},{24,8},{1,17},{9,25},{17,1},{25,9},{2,18},{10... | collective-permute-start | bytes 196616 | tf_op jit(solution)/shard_map/ppermute | solution.py:383
  159.1 0.6 pad_maximum_fusion.2
  159.7 2.7 %collective-permute-done.15.refs_2_ = bf16[2,128,128]{2,1,0:T(8,128)(2,1)S(1)} collective-permute-done((bf16[2,128,128]{2,1,0:T(8,128)(2,1)S(1)}, bf16[2,128,128]{2,1,0:T(8,128)(2,1)S(1)}, u32[]{:S(2)}, u32[]{:S(2)}) %collective-permute-start.15) | collective-permute-done | bytes 65568 | tf_op jit(solution)/shard_map/ppermute | solution.py:383
  162.4 0.6 collective-permute-done.14.refs_1_
  163.1 0.0 copy-done.12
  163.1 0.6 copy-done.13
  163.7 1.6 unpack.3
  (38 shorter events, 0.1 us)
Async XLA Ops:
  7.2 11.7 %copy-start.14 = (bf16[32,128]{1,0:T(8,128)(2,1)S(1)}, bf16[32,128]{1,0:T(8,128)(2,1)}, u32[]{:S(2)}) copy-start(bf16[32,128]{1,0:T(8,128)(2,1)} %param.9) | copy-start | bytes 24580
  7.2 71.3 %all-gather.2.cloned.1.call-start = ((), (), s32[]{:S(2)}) async-start(), calls=%async_computation.5 | async-start | bytes 2359296 | tf_op jit(solution)/shard_map/all_gather | solution.py:419
  8.9 7.8 %collective-permute-start.2 = (bf16[2,128,128]{2,1,0:T(8,128)(2,1)}, bf16[2,128,128]{2,1,0:T(8,128)(2,1)S(1)}, u32[]{:S(2)}, u32[]{:S(2)}) collective-permute-start(bf16[2,128,128]{2,1,0:T(8,128)(2,1)} %get-tuple-element.45), channel_id=1, source_target_pairs={{0,8},{8,16},{16,24},{24,0},{1,9},{9,17},{17,25},{25,1},{2,10},{10... | collective-permute-start | bytes 196616 | tf_op jit(solution)/shard_map/ppermute | solution.py:383
  11.1 5.7 %collective-permute-start.3 = (bf16[2,128,128]{2,1,0:T(8,128)(2,1)}, bf16[2,128,128]{2,1,0:T(8,128)(2,1)S(1)}, u32[]{:S(2)}, u32[]{:S(2)}) collective-permute-start(bf16[2,128,128]{2,1,0:T(8,128)(2,1)} %get-tuple-element.46), channel_id=1, source_target_pairs={{0,16},{8,24},{16,0},{24,8},{1,17},{9,25},{17,1},{25,9},{2,18},{10... | collective-permute-start | bytes 196616 | tf_op jit(solution)/shard_map/ppermute | solution.py:383
  13.7 3.6 %collective-permute-start.4 = (bf16[2,128,128]{2,1,0:T(8,128)(2,1)}, bf16[2,128,128]{2,1,0:T(8,128)(2,1)S(1)}, u32[]{:S(2)}, u32[]{:S(2)}) collective-permute-start(bf16[2,128,128]{2,1,0:T(8,128)(2,1)} %get-tuple-element.47), channel_id=1, source_target_pairs={{0,24},{8,0},{16,8},{24,16},{1,25},{9,1},{17,9},{25,17},{2,26},{10... | collective-permute-start | bytes 196616 | tf_op jit(solution)/shard_map/ppermute | solution.py:383
  18.9 12.1 %collective-permute-start = (bf16[16,128]{1,0:T(8,128)(2,1)S(1)}, bf16[16,128]{1,0:T(8,128)(2,1)S(1)}, u32[]{:S(2)}, u32[]{:S(2)}) collective-permute-start(bf16[16,128]{1,0:T(8,128)(2,1)S(1)} %get-tuple-element.98), channel_id=1, source_target_pairs={{0,32},{8,96},{16,160},{24,224},{32,40},{40,104},{48,168},{56,232}... | collective-permute-start | bytes 12296 | tf_op jit(solution)/shard_map/ppermute | solution.py:414
  19.0 12.0 %collective-permute-start.1 = (bf16[16,128]{1,0:T(8,128)(2,1)S(1)}, bf16[16,128]{1,0:T(8,128)(2,1)S(1)}, u32[]{:S(2)}, u32[]{:S(2)}) collective-permute-start(bf16[16,128]{1,0:T(8,128)(2,1)S(1)} %get-tuple-element.99), channel_id=1, source_target_pairs={{0,0},{8,64},{16,128},{24,192},{32,8},{40,72},{48,136},{56,200},{6... | collective-permute-start | bytes 12296 | tf_op jit(solution)/shard_map/ppermute | solution.py:415
  24.0 23.0 %collective-permute-start.5 = (bf16[1,128,1024]{2,1,0:T(8,128)(2,1)}, bf16[1,128,1024]{2,1,0:T(8,128)(2,1)S(1)}, u32[]{:S(2)}, u32[]{:S(2)}) collective-permute-start(bf16[1,128,1024]{2,1,0:T(8,128)(2,1)} %get-tuple-element.53), channel_id=1, source_target_pairs={{0,8},{8,16},{16,24},{24,0},{1,9},{9,17},{17,25},{25,1},{2,10},{10... | collective-permute-start | bytes 786440 | tf_op jit(solution)/shard_map/ppermute | solution.py:383
  24.3 22.7 %collective-permute-start.6 = (bf16[1,128,1024]{2,1,0:T(8,128)(2,1)}, bf16[1,128,1024]{2,1,0:T(8,128)(2,1)S(1)}, u32[]{:S(2)}, u32[]{:S(2)}) collective-permute-start(bf16[1,128,1024]{2,1,0:T(8,128)(2,1)} %get-tuple-element.54), channel_id=1, source_target_pairs={{0,16},{8,24},{16,0},{24,8},{1,17},{9,25},{17,1},{25,9},{2,18},{10... | collective-permute-start | bytes 786440 | tf_op jit(solution)/shard_map/ppermute | solution.py:383
  30.8 16.2 %collective-permute-start.7 = (bf16[1,128,1024]{2,1,0:T(8,128)(2,1)}, bf16[1,128,1024]{2,1,0:T(8,128)(2,1)S(1)}, u32[]{:S(2)}, u32[]{:S(2)}) collective-permute-start(bf16[1,128,1024]{2,1,0:T(8,128)(2,1)} %get-tuple-element.55), channel_id=1, source_target_pairs={{0,24},{8,0},{16,8},{24,16},{1,25},{9,1},{17,9},{25,17},{2,26},{10... | collective-permute-start | bytes 786440 | tf_op jit(solution)/shard_map/ppermute | solution.py:383
  47.0 16.2 %copy-start.5 = (bf16[1,128,1024]{2,1,0:T(8,128)(2,1)}, bf16[1,128,1024]{2,1,0:T(8,128)(2,1)S(1)}, u32[]{:S(2)}) copy-start(bf16[1,128,1024]{2,1,0:T(8,128)(2,1)S(1)} %collective-permute-done.5.q1) | copy-start | bytes 786436
  47.0 16.2 %copy-start.6 = (bf16[1,128,1024]{2,1,0:T(8,128)(2,1)}, bf16[1,128,1024]{2,1,0:T(8,128)(2,1)S(1)}, u32[]{:S(2)}) copy-start(bf16[1,128,1024]{2,1,0:T(8,128)(2,1)S(1)} %collective-permute-done.6.q2) | copy-start | bytes 786436
  47.0 16.2 %copy-start.7 = (bf16[1,128,1024]{2,1,0:T(8,128)(2,1)}, bf16[1,128,1024]{2,1,0:T(8,128)(2,1)S(1)}, u32[]{:S(2)}) copy-start(bf16[1,128,1024]{2,1,0:T(8,128)(2,1)S(1)} %collective-permute-done.7.q3) | copy-start | bytes 786436
  47.9 15.3 %all-to-all-start.1 = ((bf16[8,128,256]{2,1,0:T(8,128)(2,1)}), bf16[8,128,256]{2,1,0:T(8,128)(2,1)S(1)}, u32[]{:S(2)}, u32[]{:S(2)}) async-start(bf16[8,128,256]{2,1,0:T(8,128)(2,1)} %broadcast_in_dim.16), calls=%async_computation.1 | async-start | bytes 1048576 | tf_op jit(solution)/shard_map/all_to_all | solution.py:388
  53.7 97.4 %reduce-scatter.2.cloned.1.call-start = ((), (), s32[]{:S(2)}) async-start(), calls=%async_computation.6 | async-start | bytes 2359296 | tf_op jit(solution)/shard_map/reduce_scatter | solution.py:427
  55.8 22.6 %collective-permute-start.8 = (bf16[1,128,1024]{2,1,0:T(8,128)(2,1)}, bf16[1,128,1024]{2,1,0:T(8,128)(2,1)S(1)}, u32[]{:S(2)}, u32[]{:S(2)}) collective-permute-start(bf16[1,128,1024]{2,1,0:T(8,128)(2,1)} %get-tuple-element.70), channel_id=1, source_target_pairs={{0,8},{8,16},{16,24},{24,0},{1,9},{9,17},{17,25},{25,1},{2,10},{10... | collective-permute-start | bytes 786440 | tf_op jit(solution)/shard_map/ppermute | solution.py:383
  57.1 21.3 %collective-permute-start.9 = (bf16[1,128,1024]{2,1,0:T(8,128)(2,1)}, bf16[1,128,1024]{2,1,0:T(8,128)(2,1)S(1)}, u32[]{:S(2)}, u32[]{:S(2)}) collective-permute-start(bf16[1,128,1024]{2,1,0:T(8,128)(2,1)} %get-tuple-element.71), channel_id=1, source_target_pairs={{0,16},{8,24},{16,0},{24,8},{1,17},{9,25},{17,1},{25,9},{2,18},{10... | collective-permute-start | bytes 786440 | tf_op jit(solution)/shard_map/ppermute | solution.py:383
  57.1 21.4 %collective-permute-start.10 = (bf16[1,128,1024]{2,1,0:T(8,128)(2,1)}, bf16[1,128,1024]{2,1,0:T(8,128)(2,1)S(1)}, u32[]{:S(2)}, u32[]{:S(2)}) collective-permute-start(bf16[1,128,1024]{2,1,0:T(8,128)(2,1)} %get-tuple-element.72), channel_id=1, source_target_pairs={{0,24},{8,0},{16,8},{24,16},{1,25},{9,1},{17,9},{25,17},{2,26},{10... | collective-permute-start | bytes 786440 | tf_op jit(solution)/shard_map/ppermute | solution.py:383
  63.2 0.8 copy-start
  78.4 0.7 copy-start.8
  78.4 0.8 copy-start.9
  78.5 0.8 copy-start.10
  108.0 15.1 %all-to-all-start.2 = ((bf16[8,128,256]{2,1,0:T(8,128)(2,1)}), bf16[8,128,256]{2,1,0:T(8,128)(2,1)S(1)}, u32[]{:S(2)}, u32[]{:S(2)}) async-start(bf16[8,128,256]{2,1,0:T(8,128)(2,1)} %bitcast.36), calls=%async_computation.3 | async-start | bytes 1048576 | tf_op jit(solution)/shard_map/all_to_all | solution.py:394
  116.2 34.8 %copy-start.1 = (f32[4,2,128,128]{3,2,1,0:T(8,128)S(1)}, f32[4,2,128,128]{3,2,1,0:T(8,128)}, u32[]{:S(2)}) copy-start(f32[4,2,128,128]{3,2,1,0:T(8,128)} %get-tuple-element.82) | copy-start | bytes 1572868
  116.2 31.1 %collective-permute-start.13 = (bf16[2,128,1024]{2,1,0:T(8,128)(2,1)}, bf16[2,128,1024]{2,1,0:T(8,128)(2,1)S(1)}, u32[]{:S(2)}, u32[]{:S(2)}) collective-permute-start(bf16[2,128,1024]{2,1,0:T(8,128)(2,1)} %get-tuple-element.84), channel_id=1, source_target_pairs={{0,8},{8,16},{16,24},{24,0},{1,9},{9,17},{17,25},{25,1},{2,10},{10... | collective-permute-start | bytes 1572872 | tf_op jit(solution)/shard_map/ppermute | solution.py:383
  118.3 29.0 %collective-permute-start.12 = (bf16[2,128,1024]{2,1,0:T(8,128)(2,1)}, bf16[2,128,1024]{2,1,0:T(8,128)(2,1)S(1)}, u32[]{:S(2)}, u32[]{:S(2)}) collective-permute-start(bf16[2,128,1024]{2,1,0:T(8,128)(2,1)} %get-tuple-element.85), channel_id=1, source_target_pairs={{0,16},{8,24},{16,0},{24,8},{1,17},{9,25},{17,1},{25,9},{2,18},{10... | collective-permute-start | bytes 1572872 | tf_op jit(solution)/shard_map/ppermute | solution.py:383
  118.3 29.0 %collective-permute-start.11 = (bf16[2,128,1024]{2,1,0:T(8,128)(2,1)S(1)}, bf16[2,128,1024]{2,1,0:T(8,128)(2,1)S(1)}, u32[]{:S(2)}, u32[]{:S(2)}) collective-permute-start(bf16[2,128,1024]{2,1,0:T(8,128)(2,1)S(1)} %get-tuple-element.86), channel_id=1, source_target_pairs={{0,24},{8,0},{16,8},{24,16},{1,25},{9,1},{17,9},{25,17},{2,26},{10... | collective-permute-start | bytes 1572872 | tf_op jit(solution)/shard_map/ppermute | solution.py:383
  141.3 9.8 %collective-permute-start.17 = (bf16[16,128]{1,0:T(8,128)(2,1)S(1)}, bf16[16,128]{1,0:T(8,128)(2,1)S(1)}, u32[]{:S(2)}, u32[]{:S(2)}) collective-permute-start(bf16[16,128]{1,0:T(8,128)(2,1)S(1)} %get-tuple-element.94), channel_id=1, source_target_pairs={{32,0},{96,8},{160,16},{224,24},{40,32},{104,40},{168,48},{232,56}... | collective-permute-start | bytes 12296 | tf_op jit(solution)/shard_map/ppermute | solution.py:433
  143.8 7.2 %collective-permute-start.18 = (bf16[16,128]{1,0:T(8,128)(2,1)S(1)}, bf16[16,128]{1,0:T(8,128)(2,1)S(1)}, u32[]{:S(2)}, u32[]{:S(2)}) collective-permute-start(bf16[16,128]{1,0:T(8,128)(2,1)S(1)} %get-tuple-element.95), channel_id=1, source_target_pairs={{0,0},{64,8},{128,16},{192,24},{8,32},{72,40},{136,48},{200,56},{1... | collective-permute-start | bytes 12296 | tf_op jit(solution)/shard_map/ppermute | solution.py:434
  147.3 0.8 copy-start.2
  147.3 1.0 copy-start.3
  147.3 1.1 copy-start.4
  152.7 7.0 %collective-permute-start.16 = (bf16[2,128,128]{2,1,0:T(8,128)(2,1)S(1)}, bf16[2,128,128]{2,1,0:T(8,128)(2,1)S(1)}, u32[]{:S(2)}, u32[]{:S(2)}) collective-permute-start(bf16[2,128,128]{2,1,0:T(8,128)(2,1)S(1)} %get-tuple-element.88), channel_id=1, source_target_pairs={{0,8},{8,16},{16,24},{24,0},{1,9},{9,17},{17,25},{25,1},{2,10},{10... | collective-permute-start | bytes 196616 | tf_op jit(solution)/shard_map/ppermute | solution.py:383
  155.7 6.7 %collective-permute-start.15 = (bf16[2,128,128]{2,1,0:T(8,128)(2,1)S(1)}, bf16[2,128,128]{2,1,0:T(8,128)(2,1)S(1)}, u32[]{:S(2)}, u32[]{:S(2)}) collective-permute-start(bf16[2,128,128]{2,1,0:T(8,128)(2,1)S(1)} %get-tuple-element.89), channel_id=1, source_target_pairs={{0,16},{8,24},{16,0},{24,8},{1,17},{9,25},{17,1},{25,9},{2,18},{10... | collective-permute-start | bytes 196616 | tf_op jit(solution)/shard_map/ppermute | solution.py:383
  159.1 4.0 %collective-permute-start.14 = (bf16[2,128,128]{2,1,0:T(8,128)(2,1)S(1)}, bf16[2,128,128]{2,1,0:T(8,128)(2,1)S(1)}, u32[]{:S(2)}, u32[]{:S(2)}) collective-permute-start(bf16[2,128,128]{2,1,0:T(8,128)(2,1)S(1)} %get-tuple-element.90), channel_id=1, source_target_pairs={{0,24},{8,0},{16,8},{24,16},{1,25},{9,1},{17,9},{25,17},{2,26},{10... | collective-permute-start | bytes 196616 | tf_op jit(solution)/shard_map/ppermute | solution.py:383
  159.7 3.4 %copy-start.11 = (bf16[2,128,128]{2,1,0:T(8,128)(2,1)}, bf16[2,128,128]{2,1,0:T(8,128)(2,1)S(1)}, u32[]{:S(2)}) copy-start(bf16[2,128,128]{2,1,0:T(8,128)(2,1)S(1)} %collective-permute-done.16.refs_3_) | copy-start | bytes 196612
  162.4 0.6 copy-start.12
  163.1 0.6 copy-start.13
Sparse Core Ops, SparseCore 0:
  19.0 42.3 all-gather.1
  93.6 43.0 reduce-scatter.1

commit v4 on v3

--- a/solution.py
+++ b/solution.py
@@ -225,7 +225,7 @@
 
 def near_back_kernel(
     lengths, qt, gt, probs, rows_in, dq_part, out, prefix, own,
-    both, d_own, dp, keys_t, values, apk, apv, qln, gln,
+    od0, od1, od2, od3, d_own, dp, keys_t, values, apk, apv, qln, gln,
 ):
     step = pl.program_id(0)
 
@@ -257,10 +257,13 @@
         acc = acc + dot(keys_t[:, rows], ds)
     dq_t = acc * (inverse * SCALE) + dq_part[0]
     row_live = live_rows(lengths, step)
-    for h in range(GROUP):
-        cols = head_cols(h)
-        both[0, 0, :, cols] = jnp.where(row_live, out[0, :, cols].astype(F32), 0.0).T.astype(BF16)
-        both[0, 1, :, cols] = dq_t[:, cols].T.astype(BF16)
+    for d, both in enumerate((od0, od1, od2, od3)):
+        @pl.when(step == d)
+        def _(both=both):
+            for h in range(GROUP):
+                cols = head_cols(h)
+                both[0, :, cols] = jnp.where(row_live, out[0, :, cols].astype(F32), 0.0).T.astype(BF16)
+                both[1, :, cols] = dq_t[:, cols].T.astype(BF16)
 
     @pl.when(step == pl.num_programs(0) - 1)
     def _():
@@ -323,7 +326,7 @@
     return call(
         near_back_kernel, "near_backward", [lengths], n,
         [(a, True) for a in (qt, gt, probs, rows_in, dq_part, out)] + [(prefix, False), (own, True)],
-        [((n, 2, BLOCK, ROWS), BF16, True), (own.shape, F32, True), (prefix.shape, BF16, False)],
+        [((2, BLOCK, ROWS), BF16, False)] * n + [(own.shape, F32, True), (prefix.shape, BF16, False)],
         [((HD, NEAR), BF16), ((NEAR, HD), BF16), ((PREFIX, HD), F32), ((PREFIX, HD), F32),
          ((HD, ROWS), BF16), ((HD, ROWS), BF16)],
     )
@@ -425,7 +428,7 @@
     qt, probs, near_out, stats = near_forward(lengths[0], q, prefix, own)
     gt, out, dq_part, rows, dkv = branch(parents[0], lengths[0], qt, near_out, stats, g, kv)
     dkv = lax.psum_scatter(dkv, "z", scatter_dimension=0, tiled=True)
-    od, d_own, dp = near_backward(lengths[0], qt, gt, probs, rows, dq_part, out, prefix, own)
+    *od, d_own, dp = near_backward(lengths[0], qt, gt, probs, rows, dq_part, out, prefix, own)
 
     mine = gather_terms(gather_terms(dp, smp), "z")
     key, value = mine[:, :HD], mine[:, HD:]
@@ -434,7 +437,7 @@
     two = lax.ppermute(jnp.where(odd, value, key), ring, returns(1))
     d_prefix = jnp.concatenate(
         [jnp.where(value_holder, one, two), jnp.where(value_holder, two, one)], axis=0)
-    out, dq = unpack(back([od[d] for d in range(ny)]), 2)
+    out, dq = unpack(back(od), 2)
     dkv = (dkv.astype(F32) + d_own).astype(BF16)
     d_branch, = unpack(back([dkv[d] for d in range(ny)]), 1)
     return out[None], dq[None], d_branch[None], d_prefix

time: 172 us -> 175 us (1.017)
  Pallas kernels: 53.1 us -> 59.5 us
  blocking collectives: 34 us -> 30.8 us
  waiting for transfers between devices: 9.84 us -> 13 us
  local copies, waits for them, and re-layouts: 7.58 us -> 4.93 us
  starting transfers between devices: 50 us -> 48.2 us
    pallas_call x3, Pallas kernels: 43.1 us -> 49.5 us  [call(): pl.pallas_call(body, grid_spec=pltpu.PrefetchScalarGridSpec(num_scalar_pr...]
    all_to_all x1, waiting for transfers between devices: 2.23 us -> 5.61 us  [gather_terms(): lax.all_to_all(x, axes, split_axis=0, concat_axis=0, tiled=True).astype(F32)]
    all_to_all x1, blocking collectives: 18.1 us -> 14.9 us  [gather_terms(): lax.all_to_all(x, axes, split_axis=0, concat_axis=0, tiled=True).astype(F32)]
    squeeze x1 -> x0, local copies, waits for them, and re-layouts: 2.68 us -> none  [per_device(): out, dq = unpack(back([od[d] for d in range(ny)]), 2)]
  transfers between devices with their start and end apart: 23 -> 23, of which waited for: 5 -> 4; matrix products, arithmetic and copies ran while one was open for 3% -> 1% of each run, Pallas kernels for 21% -> 21%
where the time goes in v4:
time: 175 us; the launch traced here: 174 us
  Pallas kernels  59.5 us (34%)
  starting transfers between devices  48.2 us (28%)
  blocking collectives  30.8 us (18%)
  between operations  14.3 us (8%)
  waiting for transfers between devices  13 us (7%)
  local copies, waits for them, and re-layouts  4.93 us (3%)
  other arithmetic  3.3 us (2%)
    pallas_call x3, Pallas kernels, call(): pl.pallas_call(body, grid_spec=pltpu.PrefetchScalarGridSpec(num_scalar_pr...  49.5 us
    ppermute x15, starting transfers between devices, shift(): return lax.ppermute(x, axis, [(i, (i + by) % n) for i in range(n)])  26.9 us
    all_to_all x1, blocking collectives, spread(): lax.all_to_all(jnp.broadcast_to(x, (n, *x.shape)), axes, split_axis=0, co...  15.9 us
    all_to_all x1, blocking collectives, gather_terms(): lax.all_to_all(x, axes, split_axis=0, concat_axis=0, tiled=True).astype(F32)  14.9 us
    pallas_call x3, Pallas kernels, pack(): pl.pallas_call(pack_kernel, grid=(rows // TILE,), in_specs=[pl.BlockSpec(...  5.83 us
    all_to_all x1, starting transfers between devices, spread(): lax.all_to_all(jnp.broadcast_to(x, (n, *x.shape)), axes, split_axis=0, co...  5.82 us
    all_to_all x1, waiting for transfers between devices, gather_terms(): lax.all_to_all(x, axes, split_axis=0, concat_axis=0, tiled=True).astype(F32)  5.61 us
    ppermute x1, starting transfers between devices, per_device(): two = lax.ppermute(jnp.where(value_holder, high, low), ring, half_moves(1))  4.96 us
  transfers between devices with their start and end apart: 23, of which 4 were waited for; matrix products, arithmetic and copies ran while one was open for 1% of the time, Pallas kernels for 21%

profile of v4, /device:TPU:1, one launch (start us, length us, event | category | flops | bytes accessed | tf_op | source)
XLA Modules:
  0.0 174.0 jit_solution(17813543887522822139)
XLA Ops:
  7.2 0.0 all-gather.2.cloned.1.call-start
  7.2 1.7 pack.3
  8.9 2.1 %collective-permute-start.2 = (bf16[2,128,128]{2,1,0:T(8,128)(2,1)}, bf16[2,128,128]{2,1,0:T(8,128)(2,1)S(1)}, u32[]{:S(2)}, u32[]{:S(2)}) collective-permute-start(bf16[2,128,128]{2,1,0:T(8,128)(2,1)} %get-tuple-element.48), channel_id=1, source_target_pairs={{0,8},{8,16},{16,24},{24,0},{1,9},{9,17},{17,25},{25,1},{2,10},{10... | collective-permute-start | bytes 196616 | tf_op jit(solution)/shard_map/ppermute | solution.py:386
  11.1 2.6 %collective-permute-start.3 = (bf16[2,128,128]{2,1,0:T(8,128)(2,1)}, bf16[2,128,128]{2,1,0:T(8,128)(2,1)S(1)}, u32[]{:S(2)}, u32[]{:S(2)}) collective-permute-start(bf16[2,128,128]{2,1,0:T(8,128)(2,1)} %get-tuple-element.49), channel_id=1, source_target_pairs={{0,16},{8,24},{16,0},{24,8},{1,17},{9,25},{17,1},{25,9},{2,18},{10... | collective-permute-start | bytes 196616 | tf_op jit(solution)/shard_map/ppermute | solution.py:386
  13.7 1.1 collective-permute-start.4
  14.7 2.0 %pack.4 = (bf16[1,128,1024]{2,1,0:T(8,128)(2,1)}, bf16[1,128,1024]{2,1,0:T(8,128)(2,1)}, bf16[1,128,1024]{2,1,0:T(8,128)(2,1)}, bf16[1,128,1024]{2,1,0:T(8,128)(2,1)}) custom-call(bf16[128,4096]{1,0:T(8,128)(2,1)} %bitcast.26), custom_call_target="tpu_custom_call" | custom-call | tf_op jit(solution)/shard_map/pack/pallas_call | solution.py:350
  16.8 0.0 collective-permute-done.2
  16.8 0.0 collective-permute-done.3
  16.8 0.5 collective-permute-done.4
  17.3 1.6 pad_maximum_fusion.own
  18.9 0.0 all-gather.2.cloned.1.call-update
  18.9 0.1 collective-permute-start
  19.0 5.0 %collective-permute-start.1 = (bf16[16,128]{1,0:T(8,128)(2,1)S(1)}, bf16[16,128]{1,0:T(8,128)(2,1)S(1)}, u32[]{:S(2)}, u32[]{:S(2)}) collective-permute-start(bf16[16,128]{1,0:T(8,128)(2,1)S(1)} %get-tuple-element.101), channel_id=1, source_target_pairs={{0,0},{8,64},{16,128},{24,192},{32,8},{40,72},{48,136},{56,200},{6... | collective-permute-start | bytes 12296 | tf_op jit(solution)/shard_map/ppermute | solution.py:418
  24.0 0.3 collective-permute-start.5
  24.2 6.5 %collective-permute-start.6 = (bf16[1,128,1024]{2,1,0:T(8,128)(2,1)}, bf16[1,128,1024]{2,1,0:T(8,128)(2,1)S(1)}, u32[]{:S(2)}, u32[]{:S(2)}) collective-permute-start(bf16[1,128,1024]{2,1,0:T(8,128)(2,1)} %get-tuple-element.57), channel_id=1, source_target_pairs={{0,16},{8,24},{16,0},{24,8},{1,17},{9,25},{17,1},{25,9},{2,18},{10... | collective-permute-start | bytes 786440 | tf_op jit(solution)/shard_map/ppermute | solution.py:386
  30.8 0.2 collective-permute-start.7
  31.0 0.0 collective-permute-done
  31.0 0.0 collective-permute-done.1
  31.1 15.9 %all_to_all.20 = bf16[8,16,256]{2,1,0:T(8,128)(2,1)S(1)} all-to-all(bf16[8,16,256]{2,1,0:T(8,128)(2,1)S(1)} %broadcast_in_dim.15), channel_id=1, replica_groups=mesh['x'=4,'core'=2,'y'=4,'z'=8] {'z'}, dimensions={0} | all-to-all | bytes 131072 | tf_op jit(solution)/shard_map/all_to_all | solution.py:391
  46.9 0.0 copy-start.6
  47.0 0.9 broadcast_in_dim.16
  47.9 5.8 %all-to-all-start.1 = ((bf16[8,128,256]{2,1,0:T(8,128)(2,1)}), bf16[8,128,256]{2,1,0:T(8,128)(2,1)S(1)}, u32[]{:S(2)}, u32[]{:S(2)}) async-start(bf16[8,128,256]{2,1,0:T(8,128)(2,1)} %broadcast_in_dim.16), calls=%async_computation.1 | async-start | bytes 1048576 | tf_op jit(solution)/shard_map/all_to_all | solution.py:391
  53.7 2.1 %pack.5 = (bf16[1,128,1024]{2,1,0:T(8,128)(2,1)}, bf16[1,128,1024]{2,1,0:T(8,128)(2,1)}, bf16[1,128,1024]{2,1,0:T(8,128)(2,1)}, bf16[1,128,1024]{2,1,0:T(8,128)(2,1)}) custom-call(bf16[128,4096]{1,0:T(8,128)(2,1)} %bitcast.27), custom_call_target="tpu_custom_call" | custom-call | tf_op jit(solution)/shard_map/pack/pallas_call | solution.py:350
  55.8 1.3 collective-permute-start.8
  57.1 0.0 collective-permute-start.9
  57.1 2.5 %collective-permute-start.10 = (bf16[1,128,1024]{2,1,0:T(8,128)(2,1)}, bf16[1,128,1024]{2,1,0:T(8,128)(2,1)S(1)}, u32[]{:S(2)}, u32[]{:S(2)}) collective-permute-start(bf16[1,128,1024]{2,1,0:T(8,128)(2,1)} %get-tuple-element.75), channel_id=1, source_target_pairs={{0,24},{8,0},{16,8},{24,16},{1,25},{9,1},{17,9},{25,17},{2,26},{10... | collective-permute-start | bytes 786440 | tf_op jit(solution)/shard_map/ppermute | solution.py:386
  59.6 3.6 %all-to-all-done.1 = bf16[8,128,256]{2,1,0:T(8,128)(2,1)S(1)} async-done(((bf16[8,128,256]{2,1,0:T(8,128)(2,1)}), bf16[8,128,256]{2,1,0:T(8,128)(2,1)S(1)}, u32[]{:S(2)}, u32[]{:S(2)}) %all-to-all-start.1) | async-done | bytes 524320 | tf_op jit(solution)/shard_map/all_to_all | solution.py:391
  63.2 0.8 copy-done
  64.0 14.4 %near_forward.1 = (bf16[4,128,1024]{2,1,0:T(8,128)(2,1)}, bf16[4,1152,1024]{2,1,0:T(8,128)(2,1)}, f32[4,128,1024]{2,1,0:T(8,128)}, f32[4,8,1024]{2,1,0:T(8,128)}) custom-call(s32[32]{0:T(128)} %bitcast.37, bf16[1,128,1024]{2,1,0:T(8,128)(2,1)} %get-tuple-element.59.q0, bf16[1,128,1024]{2,1,0:T(8,128)(2,1)} %copy-done.5, bf16[1,128,1024]{2,1,0:T(8,128)(2,1)} %copy-done.6, ...), custom_call_target="tpu_custom_call" | custom-call | tf_op jit(solution)/shard_map/near_forward/pallas_call | solution.py:284
  78.4 0.0 copy-start.8
  78.4 0.0 collective-permute-done.9.g2
  78.4 0.0 collective-permute-done.10.g3
  78.5 0.0 all-gather.2.cloned.1.call-done.kv
  78.5 0.6 copy-done.8
  79.1 0.1 copy-done.9
  79.2 0.1 copy-done.10
  79.3 19.3 %branch.1 = (bf16[4,128,1024]{2,1,0:T(8,128)(2,1)}, bf16[4,128,1024]{2,1,0:T(8,128)(2,1)}, f32[4,128,1024]{2,1,0:T(8,128)}, f32[4,8,1024]{2,1,0:T(8,128)}, bf16[32,2,128,128]{3,2,1,0:T(8,128)(2,1)}) custom-call(s32[32]{0:T(128)} %bitcast.40, s32[32]{0:T(128)} %bitcast.38, bf16[4,128,1024]{2,1,0:T(8,128)(2,1)} %get-tuple-element.68.qt, ...), custom_call_target="tpu_custom_call" | custom-call | tf_op jit(solution)/shard_map/branch/pallas_call | solution.py:284
  98.6 0.0 reduce-scatter.2.cloned.1.call-update
  98.6 15.8 %near_backward.1 = (bf16[2,128,1024]{2,1,0:T(8,128)(2,1)}, bf16[2,128,1024]{2,1,0:T(8,128)(2,1)}, bf16[2,128,1024]{2,1,0:T(8,128)(2,1)}, bf16[2,128,1024]{2,1,0:...) custom-call(s32[32]{0:T(128)} %bitcast.39, bf16[4,128,1024]{2,1,0:T(8,128)(2,1)} %get-tuple-element.68.qt, ...), custom_call_target="tpu_custom_call" | custom-call | tf_op jit(solution)/shard_map/near_backward/pallas_call | solution.py:284
  114.4 4.7 %all-to-all-start.2 = ((bf16[8,128,256]{2,1,0:T(8,128)(2,1)}), bf16[8,128,256]{2,1,0:T(8,128)(2,1)S(1)}, u32[]{:S(2)}, u32[]{:S(2)}) async-start(bf16[8,128,256]{2,1,0:T(8,128)(2,1)} %bitcast.28), calls=%async_computation.3 | async-start | bytes 1048576 | tf_op jit(solution)/shard_map/all_to_all | solution.py:397
  119.1 0.1 collective-permute-start.11
  119.2 3.8 %collective-permute-start.12 = (bf16[2,128,1024]{2,1,0:T(8,128)(2,1)}, bf16[2,128,1024]{2,1,0:T(8,128)(2,1)S(1)}, u32[]{:S(2)}, u32[]{:S(2)}) collective-permute-start(bf16[2,128,1024]{2,1,0:T(8,128)(2,1)} %get-tuple-element.83), channel_id=1, source_target_pairs={{0,16},{8,24},{16,0},{24,8},{1,17},{9,25},{17,1},{25,9},{2,18},{10... | collective-permute-start | bytes 1572872 | tf_op jit(solution)/shard_map/ppermute | solution.py:386
  123.0 5.6 %all-to-all-done.2 = bf16[8,128,256]{2,1,0:T(8,128)(2,1)S(1)} async-done(((bf16[8,128,256]{2,1,0:T(8,128)(2,1)}), bf16[8,128,256]{2,1,0:T(8,128)(2,1)S(1)}, u32[]{:S(2)}, u32[]{:S(2)}) %all-to-all-start.2) | async-done | bytes 524320 | tf_op jit(solution)/shard_map/all_to_all | solution.py:397
  128.6 0.1 reduce_sum.24
  128.7 14.9 %all_to_all.21 = bf16[8,16,256]{2,1,0:T(8,128)(2,1)S(1)} all-to-all(bf16[8,16,256]{2,1,0:T(8,128)(2,1)S(1)} %bitcast.32), channel_id=1, replica_groups=mesh['x'=4,'core'=2,'y'=4,'z'=8] {'z'}, dimensions={0} | all-to-all | bytes 131072 | tf_op jit(solution)/shard_map/all_to_all | solution.py:397
  143.6 2.3 %collective-permute-start.17 = (bf16[16,128]{1,0:T(8,128)(2,1)S(1)}, bf16[16,128]{1,0:T(8,128)(2,1)S(1)}, u32[]{:S(2)}, u32[]{:S(2)}) collective-permute-start(bf16[16,128]{1,0:T(8,128)(2,1)S(1)} %get-tuple-element.96), channel_id=1, source_target_pairs={{32,0},{96,8},{160,16},{224,24},{40,32},{104,40},{168,48},{232,56}... | collective-permute-start | bytes 12296 | tf_op jit(solution)/shard_map/ppermute | solution.py:436
  145.9 3.4 %collective-permute-start.18 = (bf16[16,128]{1,0:T(8,128)(2,1)S(1)}, bf16[16,128]{1,0:T(8,128)(2,1)S(1)}, u32[]{:S(2)}, u32[]{:S(2)}) collective-permute-start(bf16[16,128]{1,0:T(8,128)(2,1)S(1)} %get-tuple-element.97), channel_id=1, source_target_pairs={{0,0},{64,8},{128,16},{192,24},{8,32},{72,40},{136,48},{200,56},{1... | collective-permute-start | bytes 12296 | tf_op jit(solution)/shard_map/ppermute | solution.py:437
  149.3 0.0 collective-permute-done.11.refs_1_
  149.4 0.7 copy-done.2
  150.1 0.2 copy-done.3
  150.3 0.2 copy-done.4
  150.5 2.6 %unpack.2 = (bf16[128,4096]{1,0:T(8,128)(2,1)}, bf16[128,4096]{1,0:T(8,128)(2,1)}) custom-call(bf16[2,128,1024]{2,1,0:T(8,128)(2,1)} %get-tuple-element.81.refs_0_, bf16[2,128,1024]{2,1,0:T(8,128)(2,1)} %copy-done.2, bf16[2,128,1024]{2,1,0:T(8,128)(2,1)} %copy-done.3, bf16[2,128,1024]{2,1,0:T(8,128)(2,1)} %copy-done.4), custom_call_target="tpu_custom_call" | custom-call | tf_op jit(solution)/shard_map/unpack/pallas_call | solution.py:374
  153.1 0.0 collective-permute-done.17
  153.1 0.0 collective-permute-done.18
  153.1 0.0 reduce-scatter.2.cloned.1.call-done
  153.1 1.0 add_convert_fusion
  154.1 0.6 slice_bitcast_fusion
  154.8 3.6 %collective-permute-start.16 = (bf16[2,128,128]{2,1,0:T(8,128)(2,1)S(1)}, bf16[2,128,128]{2,1,0:T(8,128)(2,1)S(1)}, u32[]{:S(2)}, u32[]{:S(2)}) collective-permute-start(bf16[2,128,128]{2,1,0:T(8,128)(2,1)S(1)} %get-tuple-element.90), channel_id=1, source_target_pairs={{0,8},{8,16},{16,24},{24,0},{1,9},{9,17},{17,25},{25,1},{2,10},{10... | collective-permute-start | bytes 196616 | tf_op jit(solution)/shard_map/ppermute | solution.py:386
  158.4 2.9 %collective-permute-start.15 = (bf16[2,128,128]{2,1,0:T(8,128)(2,1)S(1)}, bf16[2,128,128]{2,1,0:T(8,128)(2,1)S(1)}, u32[]{:S(2)}, u32[]{:S(2)}) collective-permute-start(bf16[2,128,128]{2,1,0:T(8,128)(2,1)S(1)} %get-tuple-element.91), channel_id=1, source_target_pairs={{0,16},{8,24},{16,0},{24,8},{1,17},{9,25},{17,1},{25,9},{2,18},{10... | collective-permute-start | bytes 196616 | tf_op jit(solution)/shard_map/ppermute | solution.py:386
  161.2 0.6 pad_maximum_fusion.2
  161.8 3.2 %collective-permute-done.15.refs_2_ = bf16[2,128,128]{2,1,0:T(8,128)(2,1)S(1)} collective-permute-done((bf16[2,128,128]{2,1,0:T(8,128)(2,1)S(1)}, bf16[2,128,128]{2,1,0:T(8,128)(2,1)S(1)}, u32[]{:S(2)}, u32[]{:S(2)}) %collective-permute-start.15) | collective-permute-done | bytes 65568 | tf_op jit(solution)/shard_map/ppermute | solution.py:386
  165.0 0.6 copy-done.12
  165.6 0.0 copy-done.13
  165.6 1.6 unpack.3
  (37 shorter events, 0.1 us)
Async XLA Ops:
  7.2 11.7 %copy-start.14 = (bf16[32,128]{1,0:T(8,128)(2,1)S(1)}, bf16[32,128]{1,0:T(8,128)(2,1)}, u32[]{:S(2)}) copy-start(bf16[32,128]{1,0:T(8,128)(2,1)} %param.9) | copy-start | bytes 24580
  7.2 71.3 %all-gather.2.cloned.1.call-start = ((), (), s32[]{:S(2)}) async-start(), calls=%async_computation.5 | async-start | bytes 2359296 | tf_op jit(solution)/shard_map/all_gather | solution.py:422
  8.9 7.9 %collective-permute-start.2 = (bf16[2,128,128]{2,1,0:T(8,128)(2,1)}, bf16[2,128,128]{2,1,0:T(8,128)(2,1)S(1)}, u32[]{:S(2)}, u32[]{:S(2)}) collective-permute-start(bf16[2,128,128]{2,1,0:T(8,128)(2,1)} %get-tuple-element.48), channel_id=1, source_target_pairs={{0,8},{8,16},{16,24},{24,0},{1,9},{9,17},{17,25},{25,1},{2,10},{10... | collective-permute-start | bytes 196616 | tf_op jit(solution)/shard_map/ppermute | solution.py:386
  11.1 5.7 %collective-permute-start.3 = (bf16[2,128,128]{2,1,0:T(8,128)(2,1)}, bf16[2,128,128]{2,1,0:T(8,128)(2,1)S(1)}, u32[]{:S(2)}, u32[]{:S(2)}) collective-permute-start(bf16[2,128,128]{2,1,0:T(8,128)(2,1)} %get-tuple-element.49), channel_id=1, source_target_pairs={{0,16},{8,24},{16,0},{24,8},{1,17},{9,25},{17,1},{25,9},{2,18},{10... | collective-permute-start | bytes 196616 | tf_op jit(solution)/shard_map/ppermute | solution.py:386
  13.7 3.6 %collective-permute-start.4 = (bf16[2,128,128]{2,1,0:T(8,128)(2,1)}, bf16[2,128,128]{2,1,0:T(8,128)(2,1)S(1)}, u32[]{:S(2)}, u32[]{:S(2)}) collective-permute-start(bf16[2,128,128]{2,1,0:T(8,128)(2,1)} %get-tuple-element.50), channel_id=1, source_target_pairs={{0,24},{8,0},{16,8},{24,16},{1,25},{9,1},{17,9},{25,17},{2,26},{10... | collective-permute-start | bytes 196616 | tf_op jit(solution)/shard_map/ppermute | solution.py:386
  18.9 12.1 %collective-permute-start = (bf16[16,128]{1,0:T(8,128)(2,1)S(1)}, bf16[16,128]{1,0:T(8,128)(2,1)S(1)}, u32[]{:S(2)}, u32[]{:S(2)}) collective-permute-start(bf16[16,128]{1,0:T(8,128)(2,1)S(1)} %get-tuple-element.100), channel_id=1, source_target_pairs={{0,32},{8,96},{16,160},{24,224},{32,40},{40,104},{48,168},{56,232}... | collective-permute-start | bytes 12296 | tf_op jit(solution)/shard_map/ppermute | solution.py:417
  19.0 12.0 %collective-permute-start.1 = (bf16[16,128]{1,0:T(8,128)(2,1)S(1)}, bf16[16,128]{1,0:T(8,128)(2,1)S(1)}, u32[]{:S(2)}, u32[]{:S(2)}) collective-permute-start(bf16[16,128]{1,0:T(8,128)(2,1)S(1)} %get-tuple-element.101), channel_id=1, source_target_pairs={{0,0},{8,64},{16,128},{24,192},{32,8},{40,72},{48,136},{56,200},{6... | collective-permute-start | bytes 12296 | tf_op jit(solution)/shard_map/ppermute | solution.py:418
  24.0 22.9 %collective-permute-start.5 = (bf16[1,128,1024]{2,1,0:T(8,128)(2,1)}, bf16[1,128,1024]{2,1,0:T(8,128)(2,1)S(1)}, u32[]{:S(2)}, u32[]{:S(2)}) collective-permute-start(bf16[1,128,1024]{2,1,0:T(8,128)(2,1)} %get-tuple-element.56), channel_id=1, source_target_pairs={{0,8},{8,16},{16,24},{24,0},{1,9},{9,17},{17,25},{25,1},{2,10},{10... | collective-permute-start | bytes 786440 | tf_op jit(solution)/shard_map/ppermute | solution.py:386
  24.2 22.7 %collective-permute-start.6 = (bf16[1,128,1024]{2,1,0:T(8,128)(2,1)}, bf16[1,128,1024]{2,1,0:T(8,128)(2,1)S(1)}, u32[]{:S(2)}, u32[]{:S(2)}) collective-permute-start(bf16[1,128,1024]{2,1,0:T(8,128)(2,1)} %get-tuple-element.57), channel_id=1, source_target_pairs={{0,16},{8,24},{16,0},{24,8},{1,17},{9,25},{17,1},{25,9},{2,18},{10... | collective-permute-start | bytes 786440 | tf_op jit(solution)/shard_map/ppermute | solution.py:386
  30.8 16.2 %collective-permute-start.7 = (bf16[1,128,1024]{2,1,0:T(8,128)(2,1)}, bf16[1,128,1024]{2,1,0:T(8,128)(2,1)S(1)}, u32[]{:S(2)}, u32[]{:S(2)}) collective-permute-start(bf16[1,128,1024]{2,1,0:T(8,128)(2,1)} %get-tuple-element.58), channel_id=1, source_target_pairs={{0,24},{8,0},{16,8},{24,16},{1,25},{9,1},{17,9},{25,17},{2,26},{10... | collective-permute-start | bytes 786440 | tf_op jit(solution)/shard_map/ppermute | solution.py:386
  46.9 16.3 %copy-start.5 = (bf16[1,128,1024]{2,1,0:T(8,128)(2,1)}, bf16[1,128,1024]{2,1,0:T(8,128)(2,1)S(1)}, u32[]{:S(2)}) copy-start(bf16[1,128,1024]{2,1,0:T(8,128)(2,1)S(1)} %collective-permute-done.5.q1) | copy-start | bytes 786436
  46.9 16.3 %copy-start.6 = (bf16[1,128,1024]{2,1,0:T(8,128)(2,1)}, bf16[1,128,1024]{2,1,0:T(8,128)(2,1)S(1)}, u32[]{:S(2)}) copy-start(bf16[1,128,1024]{2,1,0:T(8,128)(2,1)S(1)} %collective-permute-done.6.q2) | copy-start | bytes 786436
  46.9 16.2 %copy-start.7 = (bf16[1,128,1024]{2,1,0:T(8,128)(2,1)}, bf16[1,128,1024]{2,1,0:T(8,128)(2,1)S(1)}, u32[]{:S(2)}) copy-start(bf16[1,128,1024]{2,1,0:T(8,128)(2,1)S(1)} %collective-permute-done.7.q3) | copy-start | bytes 786436
  47.9 15.3 %all-to-all-start.1 = ((bf16[8,128,256]{2,1,0:T(8,128)(2,1)}), bf16[8,128,256]{2,1,0:T(8,128)(2,1)S(1)}, u32[]{:S(2)}, u32[]{:S(2)}) async-start(bf16[8,128,256]{2,1,0:T(8,128)(2,1)} %broadcast_in_dim.16), calls=%async_computation.1 | async-start | bytes 1048576 | tf_op jit(solution)/shard_map/all_to_all | solution.py:391
  53.7 99.4 %reduce-scatter.2.cloned.1.call-start = ((), (), s32[]{:S(2)}) async-start(), calls=%async_computation.6 | async-start | bytes 2359296 | tf_op jit(solution)/shard_map/reduce_scatter | solution.py:430
  55.8 22.6 %collective-permute-start.8 = (bf16[1,128,1024]{2,1,0:T(8,128)(2,1)}, bf16[1,128,1024]{2,1,0:T(8,128)(2,1)S(1)}, u32[]{:S(2)}, u32[]{:S(2)}) collective-permute-start(bf16[1,128,1024]{2,1,0:T(8,128)(2,1)} %get-tuple-element.73), channel_id=1, source_target_pairs={{0,8},{8,16},{16,24},{24,0},{1,9},{9,17},{17,25},{25,1},{2,10},{10... | collective-permute-start | bytes 786440 | tf_op jit(solution)/shard_map/ppermute | solution.py:386
  57.1 21.3 %collective-permute-start.9 = (bf16[1,128,1024]{2,1,0:T(8,128)(2,1)}, bf16[1,128,1024]{2,1,0:T(8,128)(2,1)S(1)}, u32[]{:S(2)}, u32[]{:S(2)}) collective-permute-start(bf16[1,128,1024]{2,1,0:T(8,128)(2,1)} %get-tuple-element.74), channel_id=1, source_target_pairs={{0,16},{8,24},{16,0},{24,8},{1,17},{9,25},{17,1},{25,9},{2,18},{10... | collective-permute-start | bytes 786440 | tf_op jit(solution)/shard_map/ppermute | solution.py:386
  57.1 21.3 %collective-permute-start.10 = (bf16[1,128,1024]{2,1,0:T(8,128)(2,1)}, bf16[1,128,1024]{2,1,0:T(8,128)(2,1)S(1)}, u32[]{:S(2)}, u32[]{:S(2)}) collective-permute-start(bf16[1,128,1024]{2,1,0:T(8,128)(2,1)} %get-tuple-element.75), channel_id=1, source_target_pairs={{0,24},{8,0},{16,8},{24,16},{1,25},{9,1},{17,9},{25,17},{2,26},{10... | collective-permute-start | bytes 786440 | tf_op jit(solution)/shard_map/ppermute | solution.py:386
  63.2 0.8 copy-start
  78.4 0.7 copy-start.8
  78.4 0.8 copy-start.9
  78.5 0.8 copy-start.10
  114.4 38.8 %copy-start.1 = (f32[4,2,128,128]{3,2,1,0:T(8,128)S(1)}, f32[4,2,128,128]{3,2,1,0:T(8,128)}, u32[]{:S(2)}) copy-start(f32[4,2,128,128]{3,2,1,0:T(8,128)} %get-tuple-element.88) | copy-start | bytes 1572868
  114.4 14.2 %all-to-all-start.2 = ((bf16[8,128,256]{2,1,0:T(8,128)(2,1)}), bf16[8,128,256]{2,1,0:T(8,128)(2,1)S(1)}, u32[]{:S(2)}, u32[]{:S(2)}) async-start(bf16[8,128,256]{2,1,0:T(8,128)(2,1)} %bitcast.28), calls=%async_computation.3 | async-start | bytes 1048576 | tf_op jit(solution)/shard_map/all_to_all | solution.py:397
  119.1 30.2 %collective-permute-start.11 = (bf16[2,128,1024]{2,1,0:T(8,128)(2,1)}, bf16[2,128,1024]{2,1,0:T(8,128)(2,1)S(1)}, u32[]{:S(2)}, u32[]{:S(2)}) collective-permute-start(bf16[2,128,1024]{2,1,0:T(8,128)(2,1)} %get-tuple-element.82), channel_id=1, source_target_pairs={{0,24},{8,0},{16,8},{24,16},{1,25},{9,1},{17,9},{25,17},{2,26},{10... | collective-permute-start | bytes 1572872 | tf_op jit(solution)/shard_map/ppermute | solution.py:386
  119.2 30.1 %collective-permute-start.12 = (bf16[2,128,1024]{2,1,0:T(8,128)(2,1)}, bf16[2,128,1024]{2,1,0:T(8,128)(2,1)S(1)}, u32[]{:S(2)}, u32[]{:S(2)}) collective-permute-start(bf16[2,128,1024]{2,1,0:T(8,128)(2,1)} %get-tuple-element.83), channel_id=1, source_target_pairs={{0,16},{8,24},{16,0},{24,8},{1,17},{9,25},{17,1},{25,9},{2,18},{10... | collective-permute-start | bytes 1572872 | tf_op jit(solution)/shard_map/ppermute | solution.py:386
  123.0 26.4 %collective-permute-start.13 = (bf16[2,128,1024]{2,1,0:T(8,128)(2,1)}, bf16[2,128,1024]{2,1,0:T(8,128)(2,1)S(1)}, u32[]{:S(2)}, u32[]{:S(2)}) collective-permute-start(bf16[2,128,1024]{2,1,0:T(8,128)(2,1)} %get-tuple-element.84), channel_id=1, source_target_pairs={{0,8},{8,16},{16,24},{24,0},{1,9},{9,17},{17,25},{25,1},{2,10},{10... | collective-permute-start | bytes 1572872 | tf_op jit(solution)/shard_map/ppermute | solution.py:386
  143.6 9.5 %collective-permute-start.17 = (bf16[16,128]{1,0:T(8,128)(2,1)S(1)}, bf16[16,128]{1,0:T(8,128)(2,1)S(1)}, u32[]{:S(2)}, u32[]{:S(2)}) collective-permute-start(bf16[16,128]{1,0:T(8,128)(2,1)S(1)} %get-tuple-element.96), channel_id=1, source_target_pairs={{32,0},{96,8},{160,16},{224,24},{40,32},{104,40},{168,48},{232,56}... | collective-permute-start | bytes 12296 | tf_op jit(solution)/shard_map/ppermute | solution.py:436
  145.9 7.2 %collective-permute-start.18 = (bf16[16,128]{1,0:T(8,128)(2,1)S(1)}, bf16[16,128]{1,0:T(8,128)(2,1)S(1)}, u32[]{:S(2)}, u32[]{:S(2)}) collective-permute-start(bf16[16,128]{1,0:T(8,128)(2,1)S(1)} %get-tuple-element.97), channel_id=1, source_target_pairs={{0,0},{64,8},{128,16},{192,24},{8,32},{72,40},{136,48},{200,56},{1... | collective-permute-start | bytes 12296 | tf_op jit(solution)/shard_map/ppermute | solution.py:437
  149.3 0.8 copy-start.2
  149.3 1.0 copy-start.3
  149.4 1.1 copy-start.4
  154.8 7.0 %collective-permute-start.16 = (bf16[2,128,128]{2,1,0:T(8,128)(2,1)S(1)}, bf16[2,128,128]{2,1,0:T(8,128)(2,1)S(1)}, u32[]{:S(2)}, u32[]{:S(2)}) collective-permute-start(bf16[2,128,128]{2,1,0:T(8,128)(2,1)S(1)} %get-tuple-element.90), channel_id=1, source_target_pairs={{0,8},{8,16},{16,24},{24,0},{1,9},{9,17},{17,25},{25,1},{2,10},{10... | collective-permute-start | bytes 196616 | tf_op jit(solution)/shard_map/ppermute | solution.py:386
  158.4 6.6 %collective-permute-start.15 = (bf16[2,128,128]{2,1,0:T(8,128)(2,1)S(1)}, bf16[2,128,128]{2,1,0:T(8,128)(2,1)S(1)}, u32[]{:S(2)}, u32[]{:S(2)}) collective-permute-start(bf16[2,128,128]{2,1,0:T(8,128)(2,1)S(1)} %get-tuple-element.91), channel_id=1, source_target_pairs={{0,16},{8,24},{16,0},{24,8},{1,17},{9,25},{17,1},{25,9},{2,18},{10... | collective-permute-start | bytes 196616 | tf_op jit(solution)/shard_map/ppermute | solution.py:386
  161.2 3.8 %collective-permute-start.14 = (bf16[2,128,128]{2,1,0:T(8,128)(2,1)S(1)}, bf16[2,128,128]{2,1,0:T(8,128)(2,1)S(1)}, u32[]{:S(2)}, u32[]{:S(2)}) collective-permute-start(bf16[2,128,128]{2,1,0:T(8,128)(2,1)S(1)} %get-tuple-element.92), channel_id=1, source_target_pairs={{0,24},{8,0},{16,8},{24,16},{1,25},{9,1},{17,9},{25,17},{2,26},{10... | collective-permute-start | bytes 196616 | tf_op jit(solution)/shard_map/ppermute | solution.py:386
  161.8 3.2 %copy-start.11 = (bf16[2,128,128]{2,1,0:T(8,128)(2,1)}, bf16[2,128,128]{2,1,0:T(8,128)(2,1)S(1)}, u32[]{:S(2)}) copy-start(bf16[2,128,128]{2,1,0:T(8,128)(2,1)S(1)} %collective-permute-done.16.refs_3_) | copy-start | bytes 196612
  165.0 0.6 copy-start.12
  165.0 0.6 copy-start.13
Sparse Core Ops, SparseCore 0:
  19.0 42.3 all-gather.1
  98.7 38.4 reduce-scatter.1

commit v5 on v3

--- a/solution.py
+++ b/solution.py
@@ -288,7 +288,7 @@
             scratch_shapes=[pltpu.VMEM(shape, dtype) for shape, dtype in scratch] + more,
         ),
         out_shape=[jax.ShapeDtypeStruct(shape, dtype) for shape, dtype, _ in outs],
-        compiler_params=pltpu.CompilerParams(vmem_limit_bytes=60 * 1024 * 1024),
+        compiler_params=pltpu.CompilerParams(vmem_limit_bytes=(60 if name == "branch" else 40) * 1024 * 1024),
         name=name,
     )(*scalars, *[a for a, _ in args])
 

time: 172 us -> 181 us (1.052); the launches traced: 172 us -> 178 us
  local copies, waits for them, and re-layouts: 7.58 us -> 20.8 us
  Pallas kernels: 53.1 us -> 49.9 us
  starting transfers between devices: 50 us -> 48 us
    unnamed x30 -> x50, local copies, waits for them, and re-layouts: 3.33 us -> 16.5 us
    pallas_call x3, Pallas kernels: 43.1 us -> 39.9 us  [call(): pl.pallas_call(body, grid_spec=pltpu.PrefetchScalarGridSpec(num_scalar_pr...]
  transfers between devices with their start and end apart: 23 -> 23, of which waited for: 5 -> 5; matrix products, arithmetic and copies ran while one was open for 3% -> 2% of each run, Pallas kernels for 21% -> 17%
where the time goes in v5:
time: 181 us; the launch traced here: 178 us
  Pallas kernels  49.9 us (28%)
  starting transfers between devices  48 us (27%)
  blocking collectives  32.3 us (18%)
  local copies, waits for them, and re-layouts  20.8 us (11%)
  between operations  14.3 us (8%)
  waiting for transfers between devices  9.83 us (5%)
  other arithmetic  3.33 us (2%)
    pallas_call x3, Pallas kernels, call(): pl.pallas_call(body, grid_spec=pltpu.PrefetchScalarGridSpec(num_scalar_pr...  39.9 us
    ppermute x15, starting transfers between devices, shift(): return lax.ppermute(x, axis, [(i, (i + by) % n) for i in range(n)])  27.5 us
    unnamed x50, local copies, waits for them, and re-layouts  16.5 us
    all_to_all x1, blocking collectives, gather_terms(): lax.all_to_all(x, axes, split_axis=0, concat_axis=0, tiled=True).astype(F32)  16.3 us
    all_to_all x1, blocking collectives, spread(): lax.all_to_all(jnp.broadcast_to(x, (n, *x.shape)), axes, split_axis=0, co...  15.9 us
    pallas_call x3, Pallas kernels, pack(): pl.pallas_call(pack_kernel, grid=(rows // TILE,), in_specs=[pl.BlockSpec(...  5.8 us
    all_to_all x1, starting transfers between devices, spread(): lax.all_to_all(jnp.broadcast_to(x, (n, *x.shape)), axes, split_axis=0, co...  5.78 us
    ppermute x1, starting transfers between devices, per_device(): two = lax.ppermute(jnp.where(value_holder, high, low), ring, half_moves(1))  4.96 us
  transfers between devices with their start and end apart: 23, of which 5 were waited for; matrix products, arithmetic and copies ran while one was open for 2% of the time, Pallas kernels for 17%

profile of v5, /device:TPU:1, one launch (start us, length us, event | category | flops | bytes accessed | tf_op | source)
XLA Modules:
  0.0 178.4 jit_solution(14861783038443576243)
XLA Ops:
  7.2 0.0 all-gather.2.cloned.1.call-start
  7.2 1.7 pack.3
  9.0 2.1 %collective-permute-start.2 = (bf16[2,128,128]{2,1,0:T(8,128)(2,1)}, bf16[2,128,128]{2,1,0:T(8,128)(2,1)S(1)}, u32[]{:S(2)}, u32[]{:S(2)}) collective-permute-start(bf16[2,128,128]{2,1,0:T(8,128)(2,1)} %get-tuple-element.45), channel_id=1, source_target_pairs={{0,8},{8,16},{16,24},{24,0},{1,9},{9,17},{17,25},{25,1},{2,10},{10... | collective-permute-start | bytes 196616 | tf_op jit(solution)/shard_map/ppermute | solution.py:383
  11.1 2.6 %collective-permute-start.3 = (bf16[2,128,128]{2,1,0:T(8,128)(2,1)}, bf16[2,128,128]{2,1,0:T(8,128)(2,1)S(1)}, u32[]{:S(2)}, u32[]{:S(2)}) collective-permute-start(bf16[2,128,128]{2,1,0:T(8,128)(2,1)} %get-tuple-element.46), channel_id=1, source_target_pairs={{0,16},{8,24},{16,0},{24,8},{1,17},{9,25},{17,1},{25,9},{2,18},{10... | collective-permute-start | bytes 196616 | tf_op jit(solution)/shard_map/ppermute | solution.py:383
  13.7 1.1 collective-permute-start.4
  14.8 2.0 %pack.4 = (bf16[1,128,1024]{2,1,0:T(8,128)(2,1)}, bf16[1,128,1024]{2,1,0:T(8,128)(2,1)}, bf16[1,128,1024]{2,1,0:T(8,128)(2,1)}, bf16[1,128,1024]{2,1,0:T(8,128)(2,1)}) custom-call(bf16[128,4096]{1,0:T(8,128)(2,1)} %bitcast.38), custom_call_target="tpu_custom_call" | custom-call | tf_op jit(solution)/shard_map/pack/pallas_call | solution.py:347
  16.8 0.5 collective-permute-done.4
  17.3 1.6 pad_maximum_fusion.own
  18.9 0.0 all-gather.2.cloned.1.call-update
  19.0 0.1 collective-permute-start
  19.1 5.0 %collective-permute-start.1 = (bf16[16,128]{1,0:T(8,128)(2,1)S(1)}, bf16[16,128]{1,0:T(8,128)(2,1)S(1)}, u32[]{:S(2)}, u32[]{:S(2)}) collective-permute-start(bf16[16,128]{1,0:T(8,128)(2,1)S(1)} %get-tuple-element.99), channel_id=1, source_target_pairs={{0,0},{8,64},{16,128},{24,192},{32,8},{40,72},{48,136},{56,200},{6... | collective-permute-start | bytes 12296 | tf_op jit(solution)/shard_map/ppermute | solution.py:415
  24.0 0.3 collective-permute-start.5
  24.3 6.5 %collective-permute-start.6 = (bf16[1,128,1024]{2,1,0:T(8,128)(2,1)}, bf16[1,128,1024]{2,1,0:T(8,128)(2,1)S(1)}, u32[]{:S(2)}, u32[]{:S(2)}) collective-permute-start(bf16[1,128,1024]{2,1,0:T(8,128)(2,1)} %get-tuple-element.54), channel_id=1, source_target_pairs={{0,16},{8,24},{16,0},{24,8},{1,17},{9,25},{17,1},{25,9},{2,18},{10... | collective-permute-start | bytes 786440 | tf_op jit(solution)/shard_map/ppermute | solution.py:383
  30.8 0.2 collective-permute-start.7
  31.1 15.9 %all_to_all.20 = bf16[8,16,256]{2,1,0:T(8,128)(2,1)S(1)} all-to-all(bf16[8,16,256]{2,1,0:T(8,128)(2,1)S(1)} %broadcast_in_dim.15), channel_id=1, replica_groups=mesh['x'=4,'core'=2,'y'=4,'z'=8] {'z'}, dimensions={0} | all-to-all | bytes 131072 | tf_op jit(solution)/shard_map/all_to_all | solution.py:388
  47.0 0.8 broadcast_in_dim.16
  47.9 5.8 %all-to-all-start.1 = ((bf16[8,128,256]{2,1,0:T(8,128)(2,1)}), bf16[8,128,256]{2,1,0:T(8,128)(2,1)S(1)}, u32[]{:S(2)}, u32[]{:S(2)}) async-start(bf16[8,128,256]{2,1,0:T(8,128)(2,1)} %broadcast_in_dim.16), calls=%async_computation.1 | async-start | bytes 1048576 | tf_op jit(solution)/shard_map/all_to_all | solution.py:388
  53.6 2.0 %pack.5 = (bf16[1,128,1024]{2,1,0:T(8,128)(2,1)}, bf16[1,128,1024]{2,1,0:T(8,128)(2,1)}, bf16[1,128,1024]{2,1,0:T(8,128)(2,1)}, bf16[1,128,1024]{2,1,0:T(8,128)(2,1)}) custom-call(bf16[128,4096]{1,0:T(8,128)(2,1)} %bitcast.39), custom_call_target="tpu_custom_call" | custom-call | tf_op jit(solution)/shard_map/pack/pallas_call | solution.py:347
  55.7 1.3 collective-permute-start.8
  57.0 2.5 %collective-permute-start.10 = (bf16[1,128,1024]{2,1,0:T(8,128)(2,1)}, bf16[1,128,1024]{2,1,0:T(8,128)(2,1)S(1)}, u32[]{:S(2)}, u32[]{:S(2)}) collective-permute-start(bf16[1,128,1024]{2,1,0:T(8,128)(2,1)} %get-tuple-element.72), channel_id=1, source_target_pairs={{0,24},{8,0},{16,8},{24,16},{1,25},{9,1},{17,9},{25,17},{2,26},{10... | collective-permute-start | bytes 786440 | tf_op jit(solution)/shard_map/ppermute | solution.py:383
  59.4 3.7 %all-to-all-done.1 = bf16[8,128,256]{2,1,0:T(8,128)(2,1)S(1)} async-done(((bf16[8,128,256]{2,1,0:T(8,128)(2,1)}), bf16[8,128,256]{2,1,0:T(8,128)(2,1)S(1)}, u32[]{:S(2)}, u32[]{:S(2)}) %all-to-all-start.1) | async-done | bytes 524320 | tf_op jit(solution)/shard_map/all_to_all | solution.py:388
  63.1 10.7 %near_forward.1 = (bf16[4,128,1024]{2,1,0:T(8,128)(2,1)S(1)}, bf16[4,1152,1024]{2,1,0:T(8,128)(2,1)S(1)}, f32[4,128,1024]{2,1,0:T(8,128)S(1)}, f32[4,8,1024]{2,1,0:T(8,128)S(1)}) custom-call(s32[32]{0:T(128)S(1)} %bitcast.36, bf16[1,128,1024]{2,1,0:T(8,128)(2,1)S(1)} %copy-done.10, bf16[1,128,1024]{2,1,0:T(8,128)(2,1)S(1)} %collective-permute-done.5.q1, ...), custom_call_target="tpu_custom_call" | custom-call | tf_op jit(solution)/shard_map/near_forward/pallas_call | solution.py:281
  73.8 3.6 %copy-done = bf16[4,1152,1024]{2,1,0:T(8,128)(2,1)} copy-done((bf16[4,1152,1024]{2,1,0:T(8,128)(2,1)}, bf16[4,1152,1024]{2,1,0:T(8,128)(2,1)S(1)}, u32[]{:S(2)}) %copy-start) | copy-done | bytes 9437208
  77.4 1.0 copy-done.2
  78.4 1.3 copy-done.5
  79.8 0.6 copy-done.12
  80.4 0.0 all-gather.2.cloned.1.call-done.kv
  80.5 0.6 copy-done.18
  81.1 0.1 copy-done.19
  81.2 0.1 copy-done.20
  81.3 16.7 %branch.1 = (bf16[4,128,1024]{2,1,0:T(8,128)(2,1)}, bf16[4,128,1024]{2,1,0:T(8,128)(2,1)}, f32[4,128,1024]{2,1,0:T(8,128)}, f32[4,8,1024]{2,1,0:T(8,128)}, bf16[32,2,128,128]{3,2,1,0:T(8,128)(2,1)}) custom-call(s32[32]{0:T(128)} %bitcast.48, s32[32]{0:T(128)} %bitcast.35, bf16[4,128,1024]{2,1,0:T(8,128)(2,1)} %copy-done.2, f32[4,128,1024]{2,1,0:T(8,128)} %copy-done.5, ...), custom_call_target="tpu_custom_call" | custom-call | tf_op jit(solution)/shard_map/branch/pallas_call | solution.py:281
  98.1 0.0 reduce-scatter.2.cloned.1.call-update
  98.1 1.2 copy-done.3
  99.3 0.3 copy-done.7
  99.6 1.6 copy-done.4
  101.2 1.2 copy-done.8
  102.4 0.9 copy-done.11
  103.3 12.5 %near_backward.1 = (bf16[4,2,128,1024]{3,2,1,0:T(8,128)(2,1)S(1)}, f32[4,2,128,128]{3,2,1,0:T(8,128)S(1)}, bf16[1024,256]{1,0:T(8,128)(2,1)S(1)}) custom-call(s32[32]{0:T(128)S(1)} %bitcast.37, bf16[4,128,1024]{2,1,0:T(8,128)(2,1)S(1)} %copy-done.3, bf16[4,128,1024]{2,1,0:T(8,128)(2,1)S(1)} %copy-done.7, bf16[4,1152,1024]{2,1,0:T(8,128)(2,1)} %copy-done, ...), custom_call_target="tpu_custom_call" | custom-call | tf_op jit(solution)/shard_map/near_backward/pallas_call | solution.py:281
  115.8 1.3 copy-done.6
  117.2 0.8 copy-done.9
  118.0 3.8 %all-to-all-start.2 = ((bf16[8,128,256]{2,1,0:T(8,128)(2,1)}), bf16[8,128,256]{2,1,0:T(8,128)(2,1)S(1)}, u32[]{:S(2)}, u32[]{:S(2)}) async-start(bf16[8,128,256]{2,1,0:T(8,128)(2,1)} %bitcast.34), calls=%async_computation.3 | async-start | bytes 1048576 | tf_op jit(solution)/shard_map/all_to_all | solution.py:394
  121.8 2.7 %slice_bitcast_fusion = (bf16[2,128,1024]{2,1,0:T(8,128)(2,1)}, bf16[2,128,1024]{2,1,0:T(8,128)(2,1)}, bf16[2,128,1024]{2,1,0:T(8,128)(2,1)S(1)}, bf16[2,128,1024]{2,1,0:T(8,128)(2,1)}) fusion(bf16[4,2,128,1024]{3,2,1,0:T(8,128)(2,1)} %copy-done.6), kind=kLoop, calls=%fused_computation.1 | loop fusion | bytes 4194304 | tf_op jit(solution)/shard_map/squeeze | solution.py:437
  124.5 2.1 %collective-permute-start.13 = (bf16[2,128,1024]{2,1,0:T(8,128)(2,1)}, bf16[2,128,1024]{2,1,0:T(8,128)(2,1)S(1)}, u32[]{:S(2)}, u32[]{:S(2)}) collective-permute-start(bf16[2,128,1024]{2,1,0:T(8,128)(2,1)} %get-tuple-element.84), channel_id=1, source_target_pairs={{0,8},{8,16},{16,24},{24,0},{1,9},{9,17},{17,25},{25,1},{2,10},{10... | collective-permute-start | bytes 1572872 | tf_op jit(solution)/shard_map/ppermute | solution.py:383
  126.6 2.4 %collective-permute-start.11 = (bf16[2,128,1024]{2,1,0:T(8,128)(2,1)S(1)}, bf16[2,128,1024]{2,1,0:T(8,128)(2,1)S(1)}, u32[]{:S(2)}, u32[]{:S(2)}) collective-permute-start(bf16[2,128,1024]{2,1,0:T(8,128)(2,1)S(1)} %get-tuple-element.86), channel_id=1, source_target_pairs={{0,24},{8,0},{16,8},{24,16},{1,25},{9,1},{17,9},{25,17},{2,26},{10... | collective-permute-start | bytes 1572872 | tf_op jit(solution)/shard_map/ppermute | solution.py:383
  129.0 2.3 %all-to-all-done.2 = bf16[8,128,256]{2,1,0:T(8,128)(2,1)S(1)} async-done(((bf16[8,128,256]{2,1,0:T(8,128)(2,1)}), bf16[8,128,256]{2,1,0:T(8,128)(2,1)S(1)}, u32[]{:S(2)}, u32[]{:S(2)}) %all-to-all-start.2) | async-done | bytes 524320 | tf_op jit(solution)/shard_map/all_to_all | solution.py:394
  131.3 0.1 reduce_sum.24
  131.3 16.3 %all_to_all.21 = bf16[8,16,256]{2,1,0:T(8,128)(2,1)S(1)} all-to-all(bf16[8,16,256]{2,1,0:T(8,128)(2,1)S(1)} %bitcast.43), channel_id=1, replica_groups=mesh['x'=4,'core'=2,'y'=4,'z'=8] {'z'}, dimensions={0} | all-to-all | bytes 131072 | tf_op jit(solution)/shard_map/all_to_all | solution.py:394
  147.7 2.4 %collective-permute-start.17 = (bf16[16,128]{1,0:T(8,128)(2,1)S(1)}, bf16[16,128]{1,0:T(8,128)(2,1)S(1)}, u32[]{:S(2)}, u32[]{:S(2)}) collective-permute-start(bf16[16,128]{1,0:T(8,128)(2,1)S(1)} %get-tuple-element.94), channel_id=1, source_target_pairs={{32,0},{96,8},{160,16},{224,24},{40,32},{104,40},{168,48},{232,56}... | collective-permute-start | bytes 12296 | tf_op jit(solution)/shard_map/ppermute | solution.py:433
  150.1 3.5 %collective-permute-start.18 = (bf16[16,128]{1,0:T(8,128)(2,1)S(1)}, bf16[16,128]{1,0:T(8,128)(2,1)S(1)}, u32[]{:S(2)}, u32[]{:S(2)}) collective-permute-start(bf16[16,128]{1,0:T(8,128)(2,1)S(1)} %get-tuple-element.95), channel_id=1, source_target_pairs={{0,0},{64,8},{128,16},{192,24},{8,32},{72,40},{136,48},{200,56},{1... | collective-permute-start | bytes 12296 | tf_op jit(solution)/shard_map/ppermute | solution.py:434
  153.7 0.7 copy-done.15
  154.4 0.2 copy-done.16
  154.6 0.2 copy-done.17
  154.8 2.6 %unpack.2 = (bf16[128,4096]{1,0:T(8,128)(2,1)}, bf16[128,4096]{1,0:T(8,128)(2,1)}) custom-call(bf16[2,128,1024]{2,1,0:T(8,128)(2,1)} %get-tuple-element.87.refs_0_, bf16[2,128,1024]{2,1,0:T(8,128)(2,1)} %copy-done.17, bf16[2,128,1024]{2,1,0:T(8,128)(2,1)} %copy-done.16, bf16[2,128,1024]{2,1,0:T(8,128)(2,1)} %copy-done.15), custom_call_target="tpu_custom_call" | custom-call | tf_op jit(solution)/shard_map/unpack/pallas_call | solution.py:371
  157.4 0.0 reduce-scatter.2.cloned.1.call-done
  157.4 1.0 add_convert_fusion
  158.4 0.7 slice_bitcast_fusion.4
  159.1 3.3 %collective-permute-start.16 = (bf16[2,128,128]{2,1,0:T(8,128)(2,1)S(1)}, bf16[2,128,128]{2,1,0:T(8,128)(2,1)S(1)}, u32[]{:S(2)}, u32[]{:S(2)}) collective-permute-start(bf16[2,128,128]{2,1,0:T(8,128)(2,1)S(1)} %get-tuple-element.88), channel_id=1, source_target_pairs={{0,8},{8,16},{16,24},{24,0},{1,9},{9,17},{17,25},{25,1},{2,10},{10... | collective-permute-start | bytes 196616 | tf_op jit(solution)/shard_map/ppermute | solution.py:383
  162.3 3.2 %collective-permute-start.15 = (bf16[2,128,128]{2,1,0:T(8,128)(2,1)S(1)}, bf16[2,128,128]{2,1,0:T(8,128)(2,1)S(1)}, u32[]{:S(2)}, u32[]{:S(2)}) collective-permute-start(bf16[2,128,128]{2,1,0:T(8,128)(2,1)S(1)} %get-tuple-element.89), channel_id=1, source_target_pairs={{0,16},{8,24},{16,0},{24,8},{1,17},{9,25},{17,1},{25,9},{2,18},{10... | collective-permute-start | bytes 196616 | tf_op jit(solution)/shard_map/ppermute | solution.py:383
  165.5 0.6 pad_maximum_fusion.2
  166.1 2.8 %collective-permute-done.15.refs_2_ = bf16[2,128,128]{2,1,0:T(8,128)(2,1)S(1)} collective-permute-done((bf16[2,128,128]{2,1,0:T(8,128)(2,1)S(1)}, bf16[2,128,128]{2,1,0:T(8,128)(2,1)S(1)}, u32[]{:S(2)}, u32[]{:S(2)}) %collective-permute-start.15) | collective-permute-done | bytes 65568 | tf_op jit(solution)/shard_map/ppermute | solution.py:383
  169.0 0.4 collective-permute-done.14.refs_1_
  169.4 0.2 copy-done.22
  169.6 0.4 copy-done.23
  170.0 1.6 unpack.3
  (58 shorter events, 0.2 us)
Async XLA Ops:
  7.2 11.8 %copy-start.24 = (bf16[32,128]{1,0:T(8,128)(2,1)S(1)}, bf16[32,128]{1,0:T(8,128)(2,1)}, u32[]{:S(2)}) copy-start(bf16[32,128]{1,0:T(8,128)(2,1)} %param.9) | copy-start | bytes 24580
  7.2 73.3 %all-gather.2.cloned.1.call-start = ((), (), s32[]{:S(2)}) async-start(), calls=%async_computation.5 | async-start | bytes 2359296 | tf_op jit(solution)/shard_map/all_gather | solution.py:419
  9.0 7.9 %collective-permute-start.2 = (bf16[2,128,128]{2,1,0:T(8,128)(2,1)}, bf16[2,128,128]{2,1,0:T(8,128)(2,1)S(1)}, u32[]{:S(2)}, u32[]{:S(2)}) collective-permute-start(bf16[2,128,128]{2,1,0:T(8,128)(2,1)} %get-tuple-element.45), channel_id=1, source_target_pairs={{0,8},{8,16},{16,24},{24,0},{1,9},{9,17},{17,25},{25,1},{2,10},{10... | collective-permute-start | bytes 196616 | tf_op jit(solution)/shard_map/ppermute | solution.py:383
  11.1 5.7 %collective-permute-start.3 = (bf16[2,128,128]{2,1,0:T(8,128)(2,1)}, bf16[2,128,128]{2,1,0:T(8,128)(2,1)S(1)}, u32[]{:S(2)}, u32[]{:S(2)}) collective-permute-start(bf16[2,128,128]{2,1,0:T(8,128)(2,1)} %get-tuple-element.46), channel_id=1, source_target_pairs={{0,16},{8,24},{16,0},{24,8},{1,17},{9,25},{17,1},{25,9},{2,18},{10... | collective-permute-start | bytes 196616 | tf_op jit(solution)/shard_map/ppermute | solution.py:383
  13.7 3.6 %collective-permute-start.4 = (bf16[2,128,128]{2,1,0:T(8,128)(2,1)}, bf16[2,128,128]{2,1,0:T(8,128)(2,1)S(1)}, u32[]{:S(2)}, u32[]{:S(2)}) collective-permute-start(bf16[2,128,128]{2,1,0:T(8,128)(2,1)} %get-tuple-element.47), channel_id=1, source_target_pairs={{0,24},{8,0},{16,8},{24,16},{1,25},{9,1},{17,9},{25,17},{2,26},{10... | collective-permute-start | bytes 196616 | tf_op jit(solution)/shard_map/ppermute | solution.py:383
  16.8 46.3 %copy-start.10 = (bf16[1,128,1024]{2,1,0:T(8,128)(2,1)S(1)}, bf16[1,128,1024]{2,1,0:T(8,128)(2,1)}, u32[]{:S(2)}) copy-start(bf16[1,128,1024]{2,1,0:T(8,128)(2,1)} %get-tuple-element.56.q0) | copy-start | bytes 786436
  16.8 46.3 %copy-start.13 = (s32[1,32]{1,0:T(1,128)S(1)}, s32[1,32]{1,0:T(1,128)}, u32[]{:S(2)}) copy-start(s32[1,32]{1,0:T(1,128)} %param.11) | copy-start | bytes 388
  18.9 44.2 %copy-start.1 = (bf16[4,2,128,128]{3,2,1,0:T(8,128)(2,1)S(1)}, bf16[4,2,128,128]{3,2,1,0:T(8,128)(2,1)}, u32[]{:S(2)}) copy-start(bf16[4,2,128,128]{3,2,1,0:T(8,128)(2,1)} %pad_maximum_fusion.own) | copy-start | bytes 786436
  19.0 12.1 %collective-permute-start = (bf16[16,128]{1,0:T(8,128)(2,1)S(1)}, bf16[16,128]{1,0:T(8,128)(2,1)S(1)}, u32[]{:S(2)}, u32[]{:S(2)}) collective-permute-start(bf16[16,128]{1,0:T(8,128)(2,1)S(1)} %get-tuple-element.98), channel_id=1, source_target_pairs={{0,32},{8,96},{16,160},{24,224},{32,40},{40,104},{48,168},{56,232}... | collective-permute-start | bytes 12296 | tf_op jit(solution)/shard_map/ppermute | solution.py:414
  19.1 12.0 %collective-permute-start.1 = (bf16[16,128]{1,0:T(8,128)(2,1)S(1)}, bf16[16,128]{1,0:T(8,128)(2,1)S(1)}, u32[]{:S(2)}, u32[]{:S(2)}) collective-permute-start(bf16[16,128]{1,0:T(8,128)(2,1)S(1)} %get-tuple-element.99), channel_id=1, source_target_pairs={{0,0},{8,64},{16,128},{24,192},{32,8},{40,72},{48,136},{56,200},{6... | collective-permute-start | bytes 12296 | tf_op jit(solution)/shard_map/ppermute | solution.py:415
  24.0 23.0 %collective-permute-start.5 = (bf16[1,128,1024]{2,1,0:T(8,128)(2,1)}, bf16[1,128,1024]{2,1,0:T(8,128)(2,1)S(1)}, u32[]{:S(2)}, u32[]{:S(2)}) collective-permute-start(bf16[1,128,1024]{2,1,0:T(8,128)(2,1)} %get-tuple-element.53), channel_id=1, source_target_pairs={{0,8},{8,16},{16,24},{24,0},{1,9},{9,17},{17,25},{25,1},{2,10},{10... | collective-permute-start | bytes 786440 | tf_op jit(solution)/shard_map/ppermute | solution.py:383
  24.3 22.7 %collective-permute-start.6 = (bf16[1,128,1024]{2,1,0:T(8,128)(2,1)}, bf16[1,128,1024]{2,1,0:T(8,128)(2,1)S(1)}, u32[]{:S(2)}, u32[]{:S(2)}) collective-permute-start(bf16[1,128,1024]{2,1,0:T(8,128)(2,1)} %get-tuple-element.54), channel_id=1, source_target_pairs={{0,16},{8,24},{16,0},{24,8},{1,17},{9,25},{17,1},{25,9},{2,18},{10... | collective-permute-start | bytes 786440 | tf_op jit(solution)/shard_map/ppermute | solution.py:383
  30.8 16.2 %collective-permute-start.7 = (bf16[1,128,1024]{2,1,0:T(8,128)(2,1)}, bf16[1,128,1024]{2,1,0:T(8,128)(2,1)S(1)}, u32[]{:S(2)}, u32[]{:S(2)}) collective-permute-start(bf16[1,128,1024]{2,1,0:T(8,128)(2,1)} %get-tuple-element.55), channel_id=1, source_target_pairs={{0,24},{8,0},{16,8},{24,16},{1,25},{9,1},{17,9},{25,17},{2,26},{10... | collective-permute-start | bytes 786440 | tf_op jit(solution)/shard_map/ppermute | solution.py:383
  47.9 15.3 %all-to-all-start.1 = ((bf16[8,128,256]{2,1,0:T(8,128)(2,1)}), bf16[8,128,256]{2,1,0:T(8,128)(2,1)S(1)}, u32[]{:S(2)}, u32[]{:S(2)}) async-start(bf16[8,128,256]{2,1,0:T(8,128)(2,1)} %broadcast_in_dim.16), calls=%async_computation.1 | async-start | bytes 1048576 | tf_op jit(solution)/shard_map/all_to_all | solution.py:388
  53.6 103.8 %reduce-scatter.2.cloned.1.call-start = ((), (), s32[]{:S(2)}) async-start(), calls=%async_computation.6 | async-start | bytes 2359296 | tf_op jit(solution)/shard_map/reduce_scatter | solution.py:427
  55.7 24.7 %collective-permute-start.8 = (bf16[1,128,1024]{2,1,0:T(8,128)(2,1)}, bf16[1,128,1024]{2,1,0:T(8,128)(2,1)S(1)}, u32[]{:S(2)}, u32[]{:S(2)}) collective-permute-start(bf16[1,128,1024]{2,1,0:T(8,128)(2,1)} %get-tuple-element.70), channel_id=1, source_target_pairs={{0,8},{8,16},{16,24},{24,0},{1,9},{9,17},{17,25},{25,1},{2,10},{10... | collective-permute-start | bytes 786440 | tf_op jit(solution)/shard_map/ppermute | solution.py:383
  57.0 23.4 %collective-permute-start.9 = (bf16[1,128,1024]{2,1,0:T(8,128)(2,1)}, bf16[1,128,1024]{2,1,0:T(8,128)(2,1)S(1)}, u32[]{:S(2)}, u32[]{:S(2)}) collective-permute-start(bf16[1,128,1024]{2,1,0:T(8,128)(2,1)} %get-tuple-element.71), channel_id=1, source_target_pairs={{0,16},{8,24},{16,0},{24,8},{1,17},{9,25},{17,1},{25,9},{2,18},{10... | collective-permute-start | bytes 786440 | tf_op jit(solution)/shard_map/ppermute | solution.py:383
  57.0 23.5 %collective-permute-start.10 = (bf16[1,128,1024]{2,1,0:T(8,128)(2,1)}, bf16[1,128,1024]{2,1,0:T(8,128)(2,1)S(1)}, u32[]{:S(2)}, u32[]{:S(2)}) collective-permute-start(bf16[1,128,1024]{2,1,0:T(8,128)(2,1)} %get-tuple-element.72), channel_id=1, source_target_pairs={{0,24},{8,0},{16,8},{24,16},{1,25},{9,1},{17,9},{25,17},{2,26},{10... | collective-permute-start | bytes 786440 | tf_op jit(solution)/shard_map/ppermute | solution.py:383
  73.8 3.6 %copy-start = (bf16[4,1152,1024]{2,1,0:T(8,128)(2,1)}, bf16[4,1152,1024]{2,1,0:T(8,128)(2,1)S(1)}, u32[]{:S(2)}) copy-start(bf16[4,1152,1024]{2,1,0:T(8,128)(2,1)S(1)} %get-tuple-element.74.probs) | copy-start | bytes 28311556
  77.4 1.0 copy-start.2
  78.4 1.3 copy-start.5
  79.8 0.7 copy-start.12
  80.4 0.7 copy-start.18
  80.4 0.8 copy-start.19
  80.4 0.9 copy-start.20
  98.0 1.2 copy-start.3
  98.0 1.5 copy-start.7
  98.0 1.5 copy-start.14
  99.6 1.6 copy-start.4
  101.2 1.2 copy-start.8
  102.4 0.9 copy-start.11
  115.8 1.3 copy-start.6
  117.2 0.8 copy-start.9
  118.0 13.3 %all-to-all-start.2 = ((bf16[8,128,256]{2,1,0:T(8,128)(2,1)}), bf16[8,128,256]{2,1,0:T(8,128)(2,1)S(1)}, u32[]{:S(2)}, u32[]{:S(2)}) async-start(bf16[8,128,256]{2,1,0:T(8,128)(2,1)} %bitcast.34), calls=%async_computation.3 | async-start | bytes 1048576 | tf_op jit(solution)/shard_map/all_to_all | solution.py:394
  124.5 29.1 %collective-permute-start.13 = (bf16[2,128,1024]{2,1,0:T(8,128)(2,1)}, bf16[2,128,1024]{2,1,0:T(8,128)(2,1)S(1)}, u32[]{:S(2)}, u32[]{:S(2)}) collective-permute-start(bf16[2,128,1024]{2,1,0:T(8,128)(2,1)} %get-tuple-element.84), channel_id=1, source_target_pairs={{0,8},{8,16},{16,24},{24,0},{1,9},{9,17},{17,25},{25,1},{2,10},{10... | collective-permute-start | bytes 1572872 | tf_op jit(solution)/shard_map/ppermute | solution.py:383
  126.6 27.0 %collective-permute-start.12 = (bf16[2,128,1024]{2,1,0:T(8,128)(2,1)}, bf16[2,128,1024]{2,1,0:T(8,128)(2,1)S(1)}, u32[]{:S(2)}, u32[]{:S(2)}) collective-permute-start(bf16[2,128,1024]{2,1,0:T(8,128)(2,1)} %get-tuple-element.85), channel_id=1, source_target_pairs={{0,16},{8,24},{16,0},{24,8},{1,17},{9,25},{17,1},{25,9},{2,18},{10... | collective-permute-start | bytes 1572872 | tf_op jit(solution)/shard_map/ppermute | solution.py:383
  126.6 27.1 %collective-permute-start.11 = (bf16[2,128,1024]{2,1,0:T(8,128)(2,1)S(1)}, bf16[2,128,1024]{2,1,0:T(8,128)(2,1)S(1)}, u32[]{:S(2)}, u32[]{:S(2)}) collective-permute-start(bf16[2,128,1024]{2,1,0:T(8,128)(2,1)S(1)} %get-tuple-element.86), channel_id=1, source_target_pairs={{0,24},{8,0},{16,8},{24,16},{1,25},{9,1},{17,9},{25,17},{2,26},{10... | collective-permute-start | bytes 1572872 | tf_op jit(solution)/shard_map/ppermute | solution.py:383
  147.7 9.7 %collective-permute-start.17 = (bf16[16,128]{1,0:T(8,128)(2,1)S(1)}, bf16[16,128]{1,0:T(8,128)(2,1)S(1)}, u32[]{:S(2)}, u32[]{:S(2)}) collective-permute-start(bf16[16,128]{1,0:T(8,128)(2,1)S(1)} %get-tuple-element.94), channel_id=1, source_target_pairs={{32,0},{96,8},{160,16},{224,24},{40,32},{104,40},{168,48},{232,56}... | collective-permute-start | bytes 12296 | tf_op jit(solution)/shard_map/ppermute | solution.py:433
  150.1 7.3 %collective-permute-start.18 = (bf16[16,128]{1,0:T(8,128)(2,1)S(1)}, bf16[16,128]{1,0:T(8,128)(2,1)S(1)}, u32[]{:S(2)}, u32[]{:S(2)}) collective-permute-start(bf16[16,128]{1,0:T(8,128)(2,1)S(1)} %get-tuple-element.95), channel_id=1, source_target_pairs={{0,0},{64,8},{128,16},{192,24},{8,32},{72,40},{136,48},{200,56},{1... | collective-permute-start | bytes 12296 | tf_op jit(solution)/shard_map/ppermute | solution.py:434
  153.6 0.8 copy-start.15
  153.6 1.0 copy-start.16
  153.6 1.1 copy-start.17
  159.1 7.0 %collective-permute-start.16 = (bf16[2,128,128]{2,1,0:T(8,128)(2,1)S(1)}, bf16[2,128,128]{2,1,0:T(8,128)(2,1)S(1)}, u32[]{:S(2)}, u32[]{:S(2)}) collective-permute-start(bf16[2,128,128]{2,1,0:T(8,128)(2,1)S(1)} %get-tuple-element.88), channel_id=1, source_target_pairs={{0,8},{8,16},{16,24},{24,0},{1,9},{9,17},{17,25},{25,1},{2,10},{10... | collective-permute-start | bytes 196616 | tf_op jit(solution)/shard_map/ppermute | solution.py:383
  162.3 6.6 %collective-permute-start.15 = (bf16[2,128,128]{2,1,0:T(8,128)(2,1)S(1)}, bf16[2,128,128]{2,1,0:T(8,128)(2,1)S(1)}, u32[]{:S(2)}, u32[]{:S(2)}) collective-permute-start(bf16[2,128,128]{2,1,0:T(8,128)(2,1)S(1)} %get-tuple-element.89), channel_id=1, source_target_pairs={{0,16},{8,24},{16,0},{24,8},{1,17},{9,25},{17,1},{25,9},{2,18},{10... | collective-permute-start | bytes 196616 | tf_op jit(solution)/shard_map/ppermute | solution.py:383
  165.5 3.9 %collective-permute-start.14 = (bf16[2,128,128]{2,1,0:T(8,128)(2,1)S(1)}, bf16[2,128,128]{2,1,0:T(8,128)(2,1)S(1)}, u32[]{:S(2)}, u32[]{:S(2)}) collective-permute-start(bf16[2,128,128]{2,1,0:T(8,128)(2,1)S(1)} %get-tuple-element.90), channel_id=1, source_target_pairs={{0,24},{8,0},{16,8},{24,16},{1,25},{9,1},{17,9},{25,17},{2,26},{10... | collective-permute-start | bytes 196616 | tf_op jit(solution)/shard_map/ppermute | solution.py:383
  166.1 3.2 %copy-start.21 = (bf16[2,128,128]{2,1,0:T(8,128)(2,1)}, bf16[2,128,128]{2,1,0:T(8,128)(2,1)S(1)}, u32[]{:S(2)}) copy-start(bf16[2,128,128]{2,1,0:T(8,128)(2,1)S(1)} %collective-permute-done.16.refs_3_) | copy-start | bytes 196612
  169.0 0.6 copy-start.22
  169.4 0.6 copy-start.23
Sparse Core Ops, SparseCore 0:
  19.1 42.3 all-gather.1
  98.2 40.1 reduce-scatter.1
